TPU v7x, 128 devices: a whole 4x4x4 slice. The times are simulated.
128 devices in a mesh: dp: 4 (over y), section: 4 (over x), mp: 8 (over z, core).
Axes of the slice: x: 4, y: 4, z: 4, core: 2. Of those that a mesh axis runs over, the one named last changes fastest.
Arguments:
- embeds: bfloat16 [8, 32, 8192], P('dp', 'mp'), may hold values from -22 to 22
- targets: int32 [8, 32], replicated, may hold values from 0 to 65535
- lengths: int32 [8], replicated, may hold values from 1 to 32, 192 in all
- source: int32 [8], replicated, may hold values from 0 to 7, each once
- attn_gain: float32 [4, 8192], P('section'), may hold values from 0.25 to 1.75
- w_query: bfloat16 [4, 8192, 4096], P('section', None, 'mp'), may hold values from -1 to 1
- w_key: bfloat16 [4, 8192, 1024], P('section', None, 'mp'), may hold values from -1 to 1
- w_value: bfloat16 [4, 8192, 1024], P('section', None, 'mp'), may hold values from -0.0625 to 0.0625
- w_out: bfloat16 [4, 4096, 8192], P('section', 'mp', 'dp'), may hold values from -0.09375 to 0.09375
- final_gain: float32 [8192], replicated, may hold values from 0.25 to 1.75
- head: bfloat16 [65536, 8192], P(('dp', 'section', 'mp')), may hold values from -3 to 3
Outputs:
- exit_logprobs: float32 [8, 32], P('dp')
- final_logprobs: float32 [8, 32], P('dp')
Inputs may be any that keep to these rules, and one draw needn't show every extreme that they name: `source`: each trainer slot names a different decode slot; decode slot s lies with data group s // 2. `lengths`: positions at or beyond a rollout's length are padding.
All inputs are finite; a program needn't handle non-finite values.
Results may differ from a plain program's by a relative error of at most 0.0038.
Values may be sent and summed in bfloat16 or wider, within the bound.
A program may use at most 128 MiB of HBM per device.

v0:
```python
import jax
import jax.numpy as jnp
from jax import lax
from jax.sharding import PartitionSpec as P

HD = 128


EPS = 1e-05
ROPE_BASE = 500000.0


def shifted_2(value, axis, steps):
    count = lax.axis_size(axis)
    pairs = [(source, (source + steps) % count) for source in range(count)]
    return lax.ppermute(value, axis, pairs)


def joined_2(part, axis, combine):
    gathered = jax.tree.map(lambda a: lax.all_gather(a, axis), part)

    def take(source):
        return jax.tree.map(lambda a: lax.dynamic_index_in_dim(a, source, 0, False), gathered)

    return lax.fori_loop(
        1, lax.axis_size(axis), lambda source, state: combine(state, take(source)), take(0)
    )


def rotate(values, positions, count):
    rows = values.shape[0]
    split = values.reshape(rows, count, HD)
    halfway = HD // 2
    freqs = ROPE_BASE ** (-jnp.arange(halfway).astype(jnp.float32) * 2.0 / HD)
    angles = positions.astype(jnp.float32)[:, None] * freqs[None, :]
    cosine = jnp.cos(angles)[:, None, :]
    sine = jnp.sin(angles)[:, None, :]
    first = split[..., :halfway]
    second = split[..., halfway:]
    joined = jnp.concatenate(
        [first * cosine - second * sine, second * cosine + first * sine], axis=-1
    )
    return joined.reshape(rows, count * HD)


def attend(query, keys, values, length, heads, kv_heads):
    rows = query.shape[0]
    grouped = heads // kv_heads
    query_g = query.reshape(rows, kv_heads, grouped, HD)
    keys_g = keys.reshape(rows, kv_heads, HD)
    values_g = values.reshape(rows, kv_heads, HD)
    scores = jnp.einsum(
        "qkgd,skd->kgqs", query_g, keys_g, preferred_element_type=jnp.float32
    ) * HD ** (-0.5)
    places = jnp.arange(rows)
    allowed = (places[None, :] <= places[:, None]) & (places[None, :] < length)
    scores = jnp.where(allowed, scores, jnp.float32(-1e30))
    highest = jnp.max(scores, axis=-1, keepdims=True)
    weights = jnp.exp(scores - highest)
    probs = (weights / jnp.sum(weights, axis=-1, keepdims=True)).astype(jnp.bfloat16)
    context = jnp.einsum("kgqs,skd->qkgd", probs, values_g, preferred_element_type=jnp.float32)
    return context.astype(jnp.bfloat16).reshape(rows, heads * HD)


def hand_over(states):
    return shifted_2(states, "section", 1)


def combine(first, second):
    highest = jnp.maximum(first[0], second[0])
    summed = first[1] * jnp.exp(first[0] - highest) + second[1] * jnp.exp(second[0] - highest)
    return (highest, summed, first[2] + second[2])


def per_device(
    embeds, targets, lengths, source, attn_gain, w_query, w_key, w_value, w_out, final_gain, head
):
    n_section = lax.axis_size("section")
    n_model = lax.axis_size("mp")
    n_data = lax.axis_size("dp")
    section_index = lax.axis_index("section")
    group_index = lax.axis_index("dp")
    model_index = lax.axis_index("mp")
    rollouts = embeds.shape[0]
    rows_dev = embeds.shape[1]
    width = embeds.shape[2]
    seq_len = rows_dev * n_model
    heads_dev = w_query.shape[2] // HD
    kv_dev = w_key.shape[2] // HD
    out_full, rows_all = (
        lax.all_gather(w_out, "dp", axis=2, tiled=True),
        lax.all_gather(embeds, "dp", axis=0, tiled=True),
    )
    chosen = jnp.take(source, group_index * rollouts + jnp.arange(rollouts), axis=0)
    trainer_rows = jnp.take(rows_all, chosen, axis=0)
    live_mine = jnp.take(lengths, chosen, axis=0)
    norm_gain = attn_gain[0]
    query_w = w_query[0]
    key_w = w_key[0]
    value_w = w_value[0]
    out_w = out_full[0]

    def project(rows):
        positions = jnp.arange(rows.shape[0])
        query = rotate(
            jnp.dot(rows, query_w, preferred_element_type=jnp.float32), positions, heads_dev
        )
        keys = rotate(jnp.dot(rows, key_w, preferred_element_type=jnp.float32), positions, kv_dev)
        values = jnp.dot(rows, value_w, preferred_element_type=jnp.float32)
        return jnp.concatenate([query, keys, values], axis=1).astype(jnp.bfloat16)

    def apply_layer(states, length):
        wide = states.astype(jnp.float32)
        normed = (
            wide * lax.rsqrt(jnp.mean(wide * wide, axis=-1, keepdims=True) + EPS) * norm_gain
        ).astype(jnp.bfloat16)
        projected = project(lax.all_gather(normed, "mp", axis=0, tiled=True))
        query = projected[:, : heads_dev * HD]
        keys = projected[:, heads_dev * HD : (heads_dev + kv_dev) * HD]
        values = projected[:, (heads_dev + kv_dev) * HD :]
        context = attend(query, keys, values, length, heads_dev, kv_dev)
        summed = lax.psum(jnp.dot(context, out_w, preferred_element_type=jnp.float32), "mp")
        delta = lax.dynamic_slice_in_dim(summed, model_index * rows_dev, rows_dev, 0)
        return (wide + delta).astype(jnp.bfloat16)

    def tick_step(tick, carry):
        incoming, outputs = carry
        micro = tick - section_index
        valid = (micro >= 0) & (micro < rollouts)
        clipped = jnp.clip(micro, 0, rollouts - 1)
        fresh = lax.dynamic_index_in_dim(trainer_rows, clipped, 0, keepdims=False)
        states = jnp.where(section_index == 0, fresh, incoming)
        length = lax.dynamic_index_in_dim(live_mine, clipped, 0, keepdims=False)
        result = apply_layer(states, length)
        updated = lax.dynamic_update_index_in_dim(outputs, result, clipped, 0)
        outputs = jnp.where(valid, updated, outputs)
        return (hand_over(result), outputs)

    start_carry = (
        jnp.zeros((rows_dev, width), jnp.bfloat16),
        jnp.zeros((rollouts, rows_dev, width), jnp.bfloat16),
    )
    outputs = lax.fori_loop(0, rollouts + n_section - 1, tick_step, start_carry)[1]
    flat_rows = outputs.reshape(rollouts * rows_dev, width)
    shifted = hand_over(flat_rows)
    half_rows = rollouts * rows_dev // 2
    keep_own = (section_index == 1) | (section_index == 3)
    chosen_rows = jnp.where(keep_own, flat_rows[:half_rows], shifted[half_rows:])
    wide = chosen_rows.astype(jnp.float32)
    scaled = (
        wide * lax.rsqrt(jnp.mean(wide * wide, axis=-1, keepdims=True) + EPS) * final_gain
    ).astype(jnp.bfloat16)
    n_dev = n_data * n_section * n_model
    every = jnp.arange(n_dev * half_rows)
    device_of = every // half_rows
    within = every % half_rows
    group_of = device_of // (n_section * n_model)
    section_of = device_of // n_model % n_section
    model_of = device_of % n_model
    half_of = jnp.where((section_of == 1) | (section_of == 3), 0, 1)
    flat_of = half_of * half_rows + within
    micro_of = flat_of // rows_dev
    position_of = model_of * rows_dev + flat_of % rows_dev
    slot_of = jnp.take(source, group_of * rollouts + micro_of, axis=0)
    order_targets = targets[slot_of, position_of]
    vocab_dev = head.shape[0]
    offset = lax.axis_index(("dp", "section", "mp")) * vocab_dev
    columns = jnp.arange(vocab_dev)
    logits = lax.dot_general(
        lax.all_gather(scaled, ("dp", "section", "mp"), axis=0, tiled=True),
        head,
        (((1,), (1,)), ((), ())),
        preferred_element_type=jnp.float32,
    )
    wanted = order_targets - offset
    highest = jnp.max(logits, axis=-1)
    summed = jnp.sum(jnp.exp(logits - highest[:, None]), axis=-1)
    picked = jnp.sum(
        jnp.where(columns[None, :] == wanted[:, None], logits, jnp.float32(0.0)), axis=-1
    )
    partial_stats = (highest, summed, picked)
    merged = joined_2(partial_stats, ("dp", "section", "mp"), combine)
    logprob = merged[2] - (merged[0] + jnp.log(merged[1]))
    own_group = jnp.take(
        logprob.reshape(n_data, n_section, n_model, half_rows), group_index, axis=0
    )

    def arrange(first, second):
        joined = jnp.concatenate([first, second], axis=-1).reshape(n_model, rollouts, rows_dev)
        return jnp.transpose(joined, (1, 0, 2)).reshape(rollouts, seq_len)

    valid_pos = jnp.arange(seq_len)[None, :] < live_mine[:, None]
    exit_logprobs = jnp.where(valid_pos, arrange(own_group[1], own_group[2]), jnp.float32(0.0))
    final_logprobs = jnp.where(valid_pos, arrange(own_group[3], own_group[0]), jnp.float32(0.0))
    return (exit_logprobs, final_logprobs)


def solution(mesh):
    return jax.shard_map(
        per_device,
        mesh=mesh,
        in_specs=(
            P("dp", "mp", None),
            P(),
            P(),
            P(),
            P("section", None),
            P("section", None, "mp"),
            P("section", None, "mp"),
            P("section", None, "mp"),
            P("section", "mp", "dp"),
            P(),
            P(("dp", "section", "mp"), None),
        ),
        out_specs=(P("dp", None), P("dp", None)),
        check_vma=False,
    )
```

profile of v0, /device:TPU:1, one launch (start us, length us, event | category | flops | bytes accessed | tf_op | source)
XLA Modules:
  0.0 805.9 jit_solution(10834836498741975900)
XLA Ops:
  10.6 12.8 %all_gather.37 = bf16[8,4,8192]{2,1,0:T(4,128)(2,1)S(1)} all-gather(bf16[2,4,8192]{2,1,0:T(4,128)(2,1)} %param.17), channel_id=1, replica_groups=mesh['dp'=4,'section'=4,'mp'=8] {'dp'}, dimensions={0}, use_global_device_ids=true | all-gather | bytes 655360 | tf_op jit(solution)/shard_map/all_gather | solution.py:92
  24.2 71.8 %all-gather.13.cloned.1.call-done = bf16[1,512,8192]{2,1,0:T(8,128)(2,1)} async-done(((bf16[1,512,2048]{2,1,0:T(8,128)(2,1)}), bf16[1,512,8192]{2,1,0:T(8,128)(2,1)}) %all-gather.13.cloned.1.call-update) | async-done | bytes 8388624 | tf_op jit(solution)/shard_map/all_gather | solution.py:91
  96.1 488.8 %while.37 = (s32[]{:T(128)}, bf16[4,8192]{1,0:T(4,128)(2,1)S(1)}, bf16[2,4,8192]{2,1,0:T(4,128)(2,1)S(1)}, pred[]{:T(512)}, s32[]{:T(128)}, /*index=5*/bf16[2,4,...) while((s32[]{:T(128)}, bf16[4,8192]{1,0:T(4,128)(2,1)S(1)}, ...), condition=%wide.region_5.7_spmd, body=%wide.region_0.6_spmd.sunk | while | flops 674064384 | bytes 41654360 | solution.py:143
  97.3 14.1 %all-gather.9 = bf16[8,4,8192]{2,1,0:T(4,128)(2,1)S(1)} all-gather(bf16[1,4,8192]{2,1,0:T(4,128)(2,1)S(1)} %fusion.93), channel_id=1, replica_groups=mesh['dp'=4,'section'=4,'mp'=8] {'mp'}, dimensions={0}, use_global_device_ids=true | all-gather | bytes 589824 | tf_op jit(solution)/shard_map/while/body/eval_jaxpr/all_gather | solution.py:117
  121.3 5.9 fusion.101
  127.3 60.6 %all-reduce.2.cloned.1.call-done = f32[32,8192]{1,0:T(8,128)} async-done(((f32[32,8192]{1,0:T(8,128)}), f32[32,8192]{1,0:T(8,128)}) %all-reduce.2.cloned.1.call-update) | async-done | bytes 1048592 | tf_op jit(solution)/shard_map/while/body/eval_jaxpr/psum | solution.py:122
  194.4 16.8 %all-gather.9 = bf16[8,4,8192]{2,1,0:T(4,128)(2,1)S(1)} all-gather(bf16[1,4,8192]{2,1,0:T(4,128)(2,1)S(1)} %fusion.93), channel_id=1, replica_groups=mesh['dp'=4,'section'=4,'mp'=8] {'mp'}, dimensions={0}, use_global_device_ids=true | all-gather | bytes 589824 | tf_op jit(solution)/shard_map/while/body/eval_jaxpr/all_gather | solution.py:117
  221.1 5.9 fusion.101
  227.1 58.7 %all-reduce.2.cloned.1.call-done = f32[32,8192]{1,0:T(8,128)} async-done(((f32[32,8192]{1,0:T(8,128)}), f32[32,8192]{1,0:T(8,128)}) %all-reduce.2.cloned.1.call-update) | async-done | bytes 1048592 | tf_op jit(solution)/shard_map/while/body/eval_jaxpr/psum | solution.py:122
  292.3 16.8 %all-gather.9 = bf16[8,4,8192]{2,1,0:T(4,128)(2,1)S(1)} all-gather(bf16[1,4,8192]{2,1,0:T(4,128)(2,1)S(1)} %fusion.93), channel_id=1, replica_groups=mesh['dp'=4,'section'=4,'mp'=8] {'mp'}, dimensions={0}, use_global_device_ids=true | all-gather | bytes 589824 | tf_op jit(solution)/shard_map/while/body/eval_jaxpr/all_gather | solution.py:117
  319.0 5.9 fusion.101
  325.0 58.7 %all-reduce.2.cloned.1.call-done = f32[32,8192]{1,0:T(8,128)} async-done(((f32[32,8192]{1,0:T(8,128)}), f32[32,8192]{1,0:T(8,128)}) %all-reduce.2.cloned.1.call-update) | async-done | bytes 1048592 | tf_op jit(solution)/shard_map/while/body/eval_jaxpr/psum | solution.py:122
  390.2 16.8 %all-gather.9 = bf16[8,4,8192]{2,1,0:T(4,128)(2,1)S(1)} all-gather(bf16[1,4,8192]{2,1,0:T(4,128)(2,1)S(1)} %fusion.93), channel_id=1, replica_groups=mesh['dp'=4,'section'=4,'mp'=8] {'mp'}, dimensions={0}, use_global_device_ids=true | all-gather | bytes 589824 | tf_op jit(solution)/shard_map/while/body/eval_jaxpr/all_gather | solution.py:117
  422.9 58.7 %all-reduce.2.cloned.1.call-done = f32[32,8192]{1,0:T(8,128)} async-done(((f32[32,8192]{1,0:T(8,128)}), f32[32,8192]{1,0:T(8,128)}) %all-reduce.2.cloned.1.call-update) | async-done | bytes 1048592 | tf_op jit(solution)/shard_map/while/body/eval_jaxpr/psum | solution.py:122
  488.1 16.8 %all-gather.9 = bf16[8,4,8192]{2,1,0:T(4,128)(2,1)S(1)} all-gather(bf16[1,4,8192]{2,1,0:T(4,128)(2,1)S(1)} %fusion.93), channel_id=1, replica_groups=mesh['dp'=4,'section'=4,'mp'=8] {'mp'}, dimensions={0}, use_global_device_ids=true | all-gather | bytes 589824 | tf_op jit(solution)/shard_map/while/body/eval_jaxpr/all_gather | solution.py:117
  514.8 5.9 fusion.101
  520.8 58.7 %all-reduce.2.cloned.1.call-done = f32[32,8192]{1,0:T(8,128)} async-done(((f32[32,8192]{1,0:T(8,128)}), f32[32,8192]{1,0:T(8,128)}) %all-reduce.2.cloned.1.call-update) | async-done | bytes 1048592 | tf_op jit(solution)/shard_map/while/body/eval_jaxpr/psum | solution.py:122
  599.5 63.8 %all-gather.15.cloned.1.call-done = bf16[128,4,8192]{2,1,0:T(4,128)(2,1)} async-done(((bf16[1,4,8192]{2,1,0:T(4,128)(2,1)}), bf16[128,4,8192]{2,1,0:T(4,128)(2,1)}) %all-gather.15.cloned.1.call-update) | async-done | bytes 8388624 | tf_op jit(solution)/shard_map/all_gather | solution.py:170
  663.3 12.5 %reshape.735 = bf16[512,8192]{1,0:T(8,128)(2,1)} reshape(bf16[128,4,8192]{2,1,0:T(4,128)(2,1)} %all-gather.15.cloned.1.call-done) | data formatting | bytes 16777216
  675.8 9.4 %fusion.52 = (f32[512]{0:T(512)S(1)}, f32[512,512]{0,1:T(8,128)S(1)}) fusion(bf16[512,8192]{1,0:T(8,128)(2,1)} %reshape.735, bf16[512,8192]{1,0:T(8,128)(2,1)} %param.27), kind=kOutput, calls=%fused_computation.141 | convolution fusion | flops 4295228928 | bytes 17827840 | tf_op jit(solution)/shard_map/dot_general | solution.py:169
  685.6 33.5 %all-gather.6 = f32[128,1,512]{2,1,0:T(1,128)S(1)} all-gather(f32[1,1,512]{2,1,0:T(1,128)S(1)} %bitcast.160), channel_id=3, replica_groups=mesh['dp'=4,'section'=4,'mp'=8] {'dp','section','mp'}, dimensions={0}, use_global_device_ids=true | all-gather | bytes 264192 | tf_op jit(solution)/shard_map/all_gather | solution.py:20
  719.1 33.3 %all-gather.7 = f32[128,1,512]{2,1,0:T(1,128)S(1)} all-gather(f32[1,1,512]{2,1,0:T(1,128)S(1)} %bitcast.159), channel_id=4, replica_groups=mesh['dp'=4,'section'=4,'mp'=8] {'dp','section','mp'}, dimensions={0}, use_global_device_ids=true | all-gather | bytes 264192 | tf_op jit(solution)/shard_map/all_gather | solution.py:20
  752.4 33.3 %all-gather.5 = f32[128,1,512]{2,1,0:T(1,128)S(1)} all-gather(f32[1,1,512]{2,1,0:T(1,128)S(1)} %bitcast.158), channel_id=2, replica_groups=mesh['dp'=4,'section'=4,'mp'=8] {'dp','section','mp'}, dimensions={0}, use_global_device_ids=true | all-gather | bytes 264192 | tf_op jit(solution)/shard_map/all_gather | solution.py:20
  785.7 11.8 %while.38 = (s32[]{:T(128)}, f32[512]{0:T(512)S(1)}, f32[512]{0:T(512)S(1)}, f32[512]{0:T(512)S(1)}, f32[128,512]{1,0:T(8,128)S(1)}, /*index=5*/f32[128,512]{1,0...) while((s32[]{:T(128)}, f32[512]{0:T(512)S(1)}, f32[512]{0:T(512)S(1)}, ...), condition=%wide.region_11.13_spmd, body=%wide.region_10.12_spmd.sunk | while | flops 3589 | bytes 30871 | solution.py:25
  (700 shorter events, 115.3 us)
Async XLA Ops:
  7.2 589.7 %copy-start = (s32[8,32]{1,0:T(8,128)S(1)}, s32[8,32]{1,0:T(8,128)}, u32[]{:S(2)}) copy-start(s32[8,32]{1,0:T(8,128)} %param.18) | copy-start | bytes 3076
  7.2 88.9 %all-gather.13.cloned.1.call-start = ((), (), s32[]{:S(2)}) async-start(), calls=%async_computation | async-start | bytes 10485760 | tf_op jit(solution)/shard_map/all_gather | solution.py:91
  96.1 494.1 %copy-start.3 = (f32[8192]{0:T(1024)S(1)}, f32[8192]{0:T(1024)}, u32[]{:S(2)}) copy-start(f32[8192]{0:T(1024)} %param.26) | copy-start | bytes 98308
  96.1 495.0 %copy-start.1 = (s32[8]{0:T(128)S(1)}, s32[8]{0:T(128)}, u32[]{:S(2)}) copy-start(s32[8]{0:T(128)} %param.20) | copy-start | bytes 100
  96.1 91.7 %all-reduce.2.cloned.1.call-start = ((), (), s32[]{:S(2)}) async-start(), calls=%async_computation.2 | async-start | bytes 2097152 | tf_op jit(solution)/shard_map/while/body/eval_jaxpr/psum | solution.py:122
  111.5 5.2 copy-start.2
  188.9 4.4 collective-permute-start
  193.3 92.5 %all-reduce.2.cloned.1.call-start = ((), (), s32[]{:S(2)}) async-start(), calls=%async_computation.2 | async-start | bytes 2097152 | tf_op jit(solution)/shard_map/while/body/eval_jaxpr/psum | solution.py:122
  211.3 5.2 copy-start.2
  286.8 4.4 collective-permute-start
  291.2 92.5 %all-reduce.2.cloned.1.call-start = ((), (), s32[]{:S(2)}) async-start(), calls=%async_computation.2 | async-start | bytes 2097152 | tf_op jit(solution)/shard_map/while/body/eval_jaxpr/psum | solution.py:122
  309.2 5.2 copy-start.2
  384.7 4.4 collective-permute-start
  389.1 92.5 %all-reduce.2.cloned.1.call-start = ((), (), s32[]{:S(2)}) async-start(), calls=%async_computation.2 | async-start | bytes 2097152 | tf_op jit(solution)/shard_map/while/body/eval_jaxpr/psum | solution.py:122
  407.1 5.2 copy-start.2
  482.6 4.4 collective-permute-start
  487.0 92.5 %all-reduce.2.cloned.1.call-start = ((), (), s32[]{:S(2)}) async-start(), calls=%async_computation.2 | async-start | bytes 2097152 | tf_op jit(solution)/shard_map/while/body/eval_jaxpr/psum | solution.py:122
  505.0 5.2 copy-start.2
  580.5 4.4 collective-permute-start
  584.9 78.4 %all-gather.15.cloned.1.call-start = ((), (), s32[]{:S(2)}) async-start(), calls=%async_computation.1 | async-start | bytes 8454144 | tf_op jit(solution)/shard_map/all_gather | solution.py:170
  584.9 5.1 collective-permute-start.1
Sparse Core Ops, SparseCore 0:
  9.7 86.3 all-gather.12
  127.4 60.4 all-reduce.1
  227.2 58.5 all-reduce.1
  325.1 58.5 all-reduce.1
  423.0 58.5 all-reduce.1
  520.9 58.5 all-reduce.1
  591.1 72.1 all-gather.14
where the time goes:
time: 807 us; the launch traced here: 806 us
  waiting for transfers between devices  453 us (56%)
  blocking collectives  194 us (24%)
  matrix products  78.4 us (10%)
  local copies, waits for them, and re-layouts  27.8 us (3%)
  other arithmetic  26.7 us (3%)
  between operations  14.3 us (2%)
    psum x5, waiting for transfers between devices, apply_layer(): lax.psum(jnp.dot(context, out_w, preferred_element_type=jnp.float32), 'mp')  295 us
    all_gather x3, blocking collectives, joined_2(): gathered = jax.tree.map(lambda a: lax.all_gather(a, axis), part)  100 us
    all_gather x5, blocking collectives, apply_layer(): projected = project(lax.all_gather(normed, 'mp', axis=0, tiled=True))  81.3 us
    all_gather x1, waiting for transfers between devices, per_device(): lax.all_gather(w_out, 'dp', axis=2, tiled=True)  71.8 us
    all_gather x1, waiting for transfers between devices, per_device(): lax.all_gather(scaled, ('dp', 'section', 'mp'), axis=0, tiled=True)  63.8 us
    dot_general x5, matrix products, apply_layer(): jnp.dot(context, out_w, preferred_element_type=jnp.float32)  29.5 us
    dot_general x5, matrix products, project(): jnp.dot(rows, query_w, preferred_element_type=jnp.float32)  25.2 us
    ppermute x6, waiting for transfers between devices, shifted_2(): return lax.ppermute(value, axis, pairs)  20.7 us
  transfers between devices with their start and end apart: 13, of which 13 were waited for; matrix products, arithmetic and copies ran while one was open for 1% of the time, Pallas kernels for 0%

commit v1 on v0

v1 whole, which is shorter than its diff:
```python
import jax
import jax.numpy as jnp
import numpy as np
from jax import lax
from jax.experimental import pallas as pl
from jax.experimental.pallas import tpu as pltpu
from jax.sharding import PartitionSpec as P

HD = 128
EPS = 1e-05
ROPE_BASE = 500000.0
NY = 4
NX = 4
NZ = 4
NM = 8
ROWS = 64
D = 8192
QW = 512
MESH = pl.DeviceIdType.MESH
BF = jnp.bfloat16
F32 = jnp.float32


def lane(start, size):
    return pl.ds(pl.multiple_of(start, 128), size)


def kernel(
    emb, live, tgt, gain, fgain, cosine, sine, wq, wk, wv, wo, head, out,
    W, WO, HEAD, EB, X, XN, SS, QA, R, C, PS, PR, PO, ZS, ZR, HP, Y, LT, STO, SA, SB, SC,
    w_sem, eb_s, eb_r, hop_s, hop_r, ag_s, ag_r, res_s, res_r, ctx_s, ctx_r, ps_s, ps_r,
    zz_s, zz_r, y_s, y_r, st_s, st_r,
):
    d = lax.axis_index("dp")
    s = lax.axis_index("section")
    m = lax.axis_index("mp")
    z = m // 2
    c = m % 2
    sib = z * 2 + (1 - c)

    def ypeer(k):
        return (d + k) % NY

    def zpeer(k):
        return ((z + k) % NZ) * 2 + c

    def zother(k):
        return ((z + k) % NZ) * 2 + (1 - c)

    def rcopy(src, dst, ssem, rsem, dev):
        return pltpu.make_async_remote_copy(
            src_ref=src, dst_ref=dst, send_sem=ssem, recv_sem=rsem,
            device_id=dev, device_id_type=MESH,
        )

    here = (d, s, sib)

    loads = []
    for h in range(2):
        loads.append([
            pltpu.make_async_copy(wq.at[:, h], W.at[h, :, :, 0:512], w_sem.at[3 * h]),
            pltpu.make_async_copy(wk.at[:, h], W.at[h, :, :, 512:640], w_sem.at[3 * h + 1]),
            pltpu.make_async_copy(wv.at[:, h], W.at[h, :, :, 640:768], w_sem.at[3 * h + 2]),
        ])
    wo_loads = []
    for h in range(2):
        for mm in range(NM):
            wo_loads.append(pltpu.make_async_copy(
                wo.at[:, mm * 256 + h * 128: mm * 256 + h * 128 + 128],
                WO.at[h, :, mm * 128: mm * 128 + 128], w_sem.at[6 + h * NM + mm]))
    head_load = pltpu.make_async_copy(head, HEAD, w_sem.at[22])
    for group in loads:
        for copy in group:
            copy.start()
    for copy in wo_loads:
        copy.start()
    head_load.start()

    barrier = pltpu.get_barrier_semaphore()
    partners = []
    for k in range(1, 4):
        partners.append((ypeer(k), s, m))
        partners.append((d, (s + k) % NX, m))
        partners.append((d, s, zpeer(k)))
        partners.append((d, s, zother(k)))
        partners.append((ypeer(k), (s + 1) % NX, m))
        partners.append((ypeer(k), (s + 3) % NX, m))
    partners.append(here)
    for dev in partners:
        pl.semaphore_signal(barrier, inc=1, device_id=dev, device_id_type=MESH)
    pl.semaphore_wait(barrier, len(partners))

    def eb_z(k):
        return rcopy(EB.at[m], EB.at[m], eb_s.at[k], eb_r.at[m], (d, s, zpeer(k)))

    def eb_z_in(k):
        mk = zpeer(k)
        return rcopy(EB.at[mk], EB.at[mk], eb_s.at[k], eb_r.at[mk], (d, s, zpeer(k)))

    def eb_fwd(k):
        mk = zpeer(k)
        return rcopy(EB.at[mk], EB.at[mk], eb_s.at[4 + k], eb_r.at[mk], here)

    def eb_sib_in(k):
        mk = zother(k)
        return rcopy(EB.at[mk], EB.at[mk], eb_s.at[4 + k], eb_r.at[mk], here)

    def hop(h, g):
        return rcopy(HP.at[h, g], X.at[h, m, d], hop_s.at[h, g], hop_r.at[h, d],
                     (g, (s + 1) % NX, m))

    def hop_in(h, g):
        return rcopy(HP.at[h, g], X.at[h, m, g], hop_s.at[h, g], hop_r.at[h, g],
                     (g, (s + 1) % NX, m))

    def ag_z(h, k):
        return rcopy(X.at[h, m], X.at[h, m], ag_s.at[h, k], ag_r.at[h, m], (d, s, zpeer(k)))

    def ag_z_in(h, k):
        mk = zpeer(k)
        return rcopy(X.at[h, mk], X.at[h, mk], ag_s.at[h, k], ag_r.at[h, mk], (d, s, zpeer(k)))

    def ag_fwd(h, k):
        mk = zpeer(k)
        return rcopy(X.at[h, mk], X.at[h, mk], ag_s.at[h, 4 + k], ag_r.at[h, mk], here)

    def ag_sib_in(h, k):
        mk = zother(k)
        return rcopy(X.at[h, mk], X.at[h, mk], ag_s.at[h, 4 + k], ag_r.at[h, mk], here)

    def res(h, k):
        g = ypeer(k)
        return rcopy(X.at[h, m, g], R.at[h, d], res_s.at[h, k], res_r.at[h, d], (g, s, m))

    def res_in(h, k):
        g = ypeer(k)
        return rcopy(X.at[h, m, g], R.at[h, g], res_s.at[h, k], res_r.at[h, g], (g, s, m))

    def ctx(k):
        return rcopy(C.at[d], C.at[d], ctx_s.at[k], ctx_r.at[d], (ypeer(k), s, m))

    def ctx_in(k):
        g = ypeer(k)
        return rcopy(C.at[g], C.at[g], ctx_s.at[k], ctx_r.at[g], (g, s, m))

    def part(h, zz):
        return rcopy(PS.at[h, zz], PR.at[h, zz], ps_s.at[h, zz], ps_r.at[h, zz], here)

    def zred(h, k):
        zt = (z + k) % NZ
        return rcopy(ZS.at[h, zt], ZR.at[h, z], zz_s.at[h, k], zz_r.at[h, z], (d, s, zpeer(k)))

    def zred_in(h, k):
        zt = (z + k) % NZ
        return rcopy(ZS.at[h, zt], ZR.at[h, zt], zz_s.at[h, k], zz_r.at[h, zt], (d, s, zpeer(k)))

    def norm_block(h, g, mm, x):
        col = g * 2048 + mm * 256 + h * 128
        scaled = (x * gain[:, lane(col, 128)]).astype(BF)
        XN.at[h, g][:, lane(mm * 128, 128)] = scaled

    def layer():
        SS[...] = jnp.zeros_like(SS)

        @pl.when(s == 0)
        def _():
            EB.at[m][...] = emb[...]
            for k in (2, 1, 3, 0):
                (eb_z(k) if k else eb_fwd(0)).start()
            for k in (1, 3, 2):
                eb_z_in(k).wait_recv()
                eb_fwd(k).start()
            for k in range(4):
                eb_sib_in(k).wait_recv()

            def body(i, _):
                dl = i // 16
                mm = (i // 2) % 8
                h = i % 2
                x = EB[:, :, lane(dl * 2048 + mm * 256 + h * 128, 128)]
                xf = x.astype(F32)
                for half in range(2):
                    xs = xf[:, half * 8: half * 8 + 8, :].reshape(ROWS, 128)
                    g = half * 2 + dl
                    norm_block(h, g, mm, xs)
                    X.at[h, mm, g][...] = xs.astype(BF)
                    SS[...] += xs * xs
                return 0

            lax.fori_loop(0, 32, body, 0)
            for h in range(2):
                for k in (2, 1, 3):
                    res(h, k).start()

        @pl.when(s > 0)
        def _():
            for h in range(2):
                for g in range(NY):
                    hop_in(h, g).wait_recv()
                for k in (2, 1, 3, 0):
                    (ag_z(h, k) if k else ag_fwd(h, 0)).start()
            for h in range(2):
                for k in (2, 1, 3):
                    res(h, k).start()
            for h in range(2):
                for k in (1, 3, 2):
                    ag_z_in(h, k).wait_recv()
                    ag_fwd(h, k).start()

        QA[...] = jnp.zeros_like(QA)
        for h in range(2):
            @pl.when(s > 0)
            def _():
                for k in range(4):
                    ag_sib_in(h, k).wait_recv()

                def body(mm, _):
                    for g in range(NY):
                        xf = X[h, mm, g].astype(F32)
                        norm_block(h, g, mm, xf)
                        SS[...] += xf * xf
                    return 0

                lax.fori_loop(0, NM, body, 0)

            for copy in loads[h]:
                copy.wait()

            def dots(g, _):
                w = W[h, pl.ds(g * 8, 8)].reshape(1024, 768)
                QA[...] += jnp.dot(XN[h, g], w, preferred_element_type=F32)
                return 0

            lax.fori_loop(0, NY, dots, 0)

        r = lax.rsqrt(jnp.sum(SS[...], axis=1, keepdims=True) * (1.0 / D) + EPS)
        cos = cosine[...]
        sin = sine[...]

        def rope(x):
            return (x * cos + pltpu.roll(x, 64, 1) * sin).astype(BF)

        query = jnp.concatenate(
            [rope(QA[:, j * HD:(j + 1) * HD] * r) for j in range(4)], axis=0)
        key = rope(QA[:, 512:640] * r)
        value = (QA[:, 640:768] * r).astype(BF)
        scores = lax.dot_general(query, key, (((1,), (1,)), ((), ())),
                                 preferred_element_type=F32) * (HD ** -0.5)
        shape = (4 * ROWS, ROWS)
        rq = lax.broadcasted_iota(jnp.int32, shape, 0) % ROWS
        rk = lax.broadcasted_iota(jnp.int32, shape, 1)
        slot_q, slot_k = (rq // 4) % 2, (rk // 4) % 2
        pos_q, pos_k = (rq // 8) * 4 + rq % 4, (rk // 8) * 4 + rk % 4
        live_k = jnp.where(slot_k == 0, live[2 * d], live[2 * d + 1])
        allowed = (slot_q == slot_k) & (pos_k <= pos_q) & (pos_k < live_k)
        scores = jnp.where(allowed, scores, F32(-1e30))
        highest = jnp.max(scores, axis=-1, keepdims=True)
        weights = jnp.exp(scores - highest)
        probs = (weights / jnp.sum(weights, axis=-1, keepdims=True)).astype(BF)
        mixed = jnp.dot(probs, value, preferred_element_type=F32).astype(BF)
        for j in range(4):
            C.at[d][:, j * HD:(j + 1) * HD] = mixed[j * ROWS:(j + 1) * ROWS]
        for k in (2, 1, 3):
            ctx(k).start()

        for h in range(2):
            R.at[h, d][...] = X[h, m, d]
        for copy in wo_loads:
            copy.wait()
        for k in (1, 3, 2):
            ctx_in(k).wait_recv()

        context = C[...].reshape(NY * ROWS, QW)
        for h in range(2):
            def project(zz, _):
                p = jnp.dot(context, WO[h, :, lane(zz * 256, 256)], preferred_element_type=F32)
                low, high = p[:, :128], p[:, 128:]
                PO.at[h, zz][...] = jnp.where(c == 0, low, high)
                PS.at[h, zz][...] = jnp.where(c == 0, high, low).astype(BF)
                part(h, zz).start()
                return 0

            lax.fori_loop(0, NZ, project, 0)

        for h in range(2):
            for k in (2, 1, 3):
                zt = (z + k) % NZ
                part(h, zt).wait_recv()
                ZS.at[h, zt][...] = (PO[h, zt] + PR[h, zt].astype(F32)).astype(BF)
                zred(h, k).start()
        for h in range(2):
            part(h, z).wait_recv()
            total = PO[h, z] + PR[h, z].astype(F32)
            for k in (1, 3, 2):
                res_in(h, k).wait_recv()
            total = total + R[h].astype(F32).reshape(NY * ROWS, 128)
            for k in (1, 3, 2):
                zred_in(h, k).wait_recv()
                total = total + ZR[h, (z + k) % NZ].astype(F32)
            hidden = total.astype(BF)
            HP.at[h][...] = hidden.reshape(NY, ROWS, 128)

            @pl.when(s < NX - 1)
            def _():
                for k in (2, 1, 3, 0):
                    hop(h, ypeer(k)).start()

        @pl.when(s % 2 == 1)
        def _():
            b = s // 2
            sums = jnp.zeros((16, NY * ROWS), F32)
            ones = jnp.ones((16, 128), BF)
            nt = (((1,), (1,)), ((), ()))
            for h in range(2):
                wide = HP[h].astype(F32).reshape(NY * ROWS, 128)
                square = wide * wide
                top = square.astype(BF)
                rest = (square - top.astype(F32)).astype(BF)
                sums = sums + lax.dot_general(ones, top, nt, preferred_element_type=F32)
                sums = sums + lax.dot_general(ones, rest, nt, preferred_element_type=F32)
                col = d * 2048 + m * 256 + h * 128
                Y.at[b][0:256, lane(col, 128)] = (wide * fgain[:, lane(col, 128)]).astype(BF)
            top = sums.astype(BF).astype(F32)
            row = lax.broadcasted_iota(jnp.int32, (16, NY * ROWS), 0)
            packed = jnp.where(row == 0, top, jnp.where(row == 1, sums - top, 0.0))
            Y.at[b][256:272, lane(d * 2048 + m * 256, 256)] = packed.astype(BF)

    def piece(b, g, mm):
        return Y.at[b, :, lane(g * 2048 + mm * 256, 256)]

    def ycopy(b, g, mm, index, dev):
        ref = piece(b, g, mm)
        return rcopy(ref, ref, y_s.at[b, index], y_r.at[b, g * NM + mm], dev)

    def first_piece(k):
        return (jnp.where(c == 0, ypeer(k), d), jnp.where(c == 0, m, zpeer(k)))

    def second_piece(i, k):
        g0, m0 = first_piece(i)
        return (jnp.where(c == 0, g0, ypeer(k)), jnp.where(c == 0, zpeer(k), m0))

    def first_dev(k):
        g, mm = first_piece(k)
        return (g, s, mm)

    def second_dev(k):
        g, mm = second_piece(0, k)
        return (g, s, mm)

    def y_x(b, k):
        return ycopy(b, d, m, k, (d, (s + k) % NX, m))

    def y_first(b, k):
        return ycopy(b, d, m, 3 + k, first_dev(k))

    def y_second(b, i, k):
        g, mm = first_piece(i)
        return ycopy(b, g, mm, 7 + i * 3 + k - 1, second_dev(k))

    def y_fwd(b, i, k):
        g, mm = second_piece(i, k) if k else first_piece(i)
        return ycopy(b, g, mm, 19 + i * 4 + k, here)

    def y_in(b, g, mm):
        return ycopy(b, g, mm, 0, here)

    def score(b):
        source = 2 * b + 1

        @pl.when(s == source)
        def _():
            for k in (2, 1, 3):
                y_x(b, k).start()

        @pl.when(s != source)
        def _():
            y_in(b, d, m).wait_recv()

        for k in (2, 1, 3):
            y_first(b, k).start()
        for k in (2, 1, 3):
            y_second(b, 0, k).start()
        y_fwd(b, 0, 0).start()
        for i in (1, 3, 2):
            g, mm = first_piece(i)
            y_in(b, g, mm).wait_recv()
            for k in (2, 1, 3):
                y_second(b, i, k).start()
            y_fwd(b, i, 0).start()
        for i in (0, 1, 3, 2):
            for k in (1, 3, 2):
                g, mm = second_piece(i, k)
                y_in(b, g, mm).wait_recv()
                y_fwd(b, i, k).start()
        for g in range(NY):
            for zz in range(NZ):
                y_in(b, g, zz * 2 + (1 - c)).wait_recv()

        LT[...] = jnp.zeros_like(LT)

        def dots(g, _):
            cols = pl.ds(pl.multiple_of(g * 2048, 2048), 2048)
            LT[...] += lax.dot_general(HEAD[:, cols], Y[b, 0:256, cols],
                                       (((1,), (1,)), ((), ())), preferred_element_type=F32)
            return 0

        lax.fori_loop(0, NY, dots, 0)
        wide = jnp.sum(Y[b, 256:272, :].astype(F32), axis=0, keepdims=True)
        sums = wide[:, 0:256]
        for i in range(1, NY * NM):
            sums = sums + wide[:, i * 256:(i + 1) * 256]
        r = lax.rsqrt(sums * (1.0 / D) + EPS)
        logits = LT[...] * r
        highest = jnp.max(logits, axis=0, keepdims=True)
        summed = jnp.sum(jnp.exp(logits - highest), axis=0, keepdims=True)
        vocab = HEAD.shape[0]
        wanted = tgt[...] - ((d * NX + s) * NM + m) * vocab
        index = lax.broadcasted_iota(jnp.int32, logits.shape, 0)
        picked = jnp.sum(jnp.where(index == wanted, logits, 0.0), axis=0, keepdims=True)
        lanes = pl.ds(pl.multiple_of(b * 256, 256), 256)
        rows = lax.broadcasted_iota(jnp.int32, (8, 256), 0)
        STO[:, lanes] = jnp.where(rows == 0, highest,
                                  jnp.where(rows == 1, summed,
                                            jnp.where(rows == 2, picked, 0.0)))

    def step(t, _):
        place = jnp.where(s == NX - 1, 1, 0)

        @pl.when(t == place)
        def _():
            layer()

        @pl.when(t != place)
        def _():
            @pl.when((t == 0) | ((t == 1) & (s != NX - 1)))
            def _():
                head_load.wait()
            score(jnp.where(t == 2, 1, 0))
        return 0

    lax.fori_loop(0, 3, step, 0)

    def merge(ref, count):
        parts = [ref[j] for j in range(count)]
        highest = parts[0][0:1]
        for p in parts[1:]:
            highest = jnp.maximum(highest, p[0:1])
        summed = jnp.zeros_like(highest)
        picked = jnp.zeros_like(highest)
        for p in parts:
            summed = summed + p[1:2] * jnp.exp(p[0:1] - highest)
            picked = picked + p[2:3]
        return highest, summed, picked

    def stacked(highest, summed, picked):
        rows = lax.broadcasted_iota(jnp.int32, (8, 512), 0)
        return jnp.where(rows == 0, highest,
                         jnp.where(rows == 1, summed, jnp.where(rows == 2, picked, 0.0)))

    def st_y(k):
        return rcopy(SA.at[d], SA.at[d], st_s.at[0, k], st_r.at[0, d], (ypeer(k), s, m))

    def st_y_in(k):
        g = ypeer(k)
        return rcopy(SA.at[g], SA.at[g], st_s.at[0, k], st_r.at[0, g], (g, s, m))

    def m_of(k):
        return (m + k) % NM

    def st_m(k):
        return rcopy(SB.at[m], SB.at[m], st_s.at[1, k], st_r.at[1, m], (d, s, m_of(k)))

    def st_m_in(k):
        mm = m_of(k)
        return rcopy(SB.at[mm], SB.at[mm], st_s.at[1, k], st_r.at[1, mm], (d, s, mm))

    def st_x(k):
        return rcopy(SC.at[s], SC.at[s], st_s.at[2, k], st_r.at[2, s], (d, (s + k) % NX, m))

    def st_x_in(k):
        ss = (s + k) % NX
        return rcopy(SC.at[ss], SC.at[ss], st_s.at[2, k], st_r.at[2, ss], (d, ss, m))

    SA.at[d][...] = STO[...]
    for k in (2, 1, 3):
        st_y(k).start()
    for k in (1, 3, 2):
        st_y_in(k).wait_recv()
    SB.at[m][...] = stacked(*merge(SA, NY))
    for k in (4, 3, 5, 2, 6, 1, 7):
        st_m(k).start()
    for k in (1, 7, 2, 6, 3, 5, 4):
        st_m_in(k).wait_recv()
    SC.at[s][...] = stacked(*merge(SB, NM))
    for k in (2, 1, 3):
        st_x(k).start()
    for k in (1, 3, 2):
        st_x_in(k).wait_recv()
    highest, summed, picked = merge(SC, NX)
    out[...] = jnp.broadcast_to(picked - (highest + jnp.log(summed)), out.shape)

    @pl.when(s == 0)
    def _():
        for k in range(4):
            (eb_z(k) if k else eb_fwd(0)).wait_send()
        for k in range(1, 4):
            eb_fwd(k).wait_send()

    @pl.when(s > 0)
    def _():
        for h in range(2):
            for k in range(1, 4):
                ag_z(h, k).wait_send()
            for k in range(4):
                ag_fwd(h, k).wait_send()

    @pl.when(s < NX - 1)
    def _():
        for h in range(2):
            for k in range(4):
                hop(h, ypeer(k)).wait_send()

    for h in range(2):
        for k in range(1, 4):
            res(h, k).wait_send()
            zred(h, k).wait_send()
        for zz in range(NZ):
            part(h, zz).wait_send()
    for k in range(1, 4):
        ctx(k).wait_send()
        st_y(k).wait_send()
        st_x(k).wait_send()
    for k in range(1, 8):
        st_m(k).wait_send()
    for b in range(2):
        @pl.when(s == 2 * b + 1)
        def _():
            for k in range(1, 4):
                y_x(b, k).wait_send()
        for k in range(1, 4):
            y_first(b, k).wait_send()
        for i in range(4):
            for k in range(1, 4):
                y_second(b, i, k).wait_send()
            for k in range(4):
                y_fwd(b, i, k).wait_send()


def tables():
    row = np.arange(ROWS)
    position = (row // 8) * 4 + row % 4
    half = HD // 2
    freqs = (ROPE_BASE ** (-np.arange(half) * 2.0 / HD)).astype(np.float32)
    angles = (position.astype(np.float32)[:, None] * freqs[None, :]).astype(np.float64)
    cos, sin = np.cos(angles), np.sin(angles)
    return (np.concatenate([cos, cos], 1).astype(np.float32),
            np.concatenate([-sin, sin], 1).astype(np.float32))


def per_device(
    embeds, targets, lengths, source, attn_gain, w_query, w_key, w_value, w_out, final_gain, head
):
    d = lax.axis_index("dp")
    vocab = head.shape[0]
    emb = embeds.reshape(8, 2, 4096).transpose(1, 0, 2).reshape(16, 4096)
    tgt = targets.reshape(NY, 2, NM, 4).transpose(0, 2, 1, 3).reshape(1, NY * ROWS)
    cos, sin = tables()
    vmem = pl.BlockSpec(memory_space=pltpu.VMEM)
    hbm = pl.BlockSpec(memory_space=pl.ANY)
    smem = pl.BlockSpec(memory_space=pltpu.SMEM)
    dma = pltpu.SemaphoreType.DMA
    stats = pl.pallas_call(
        kernel,
        out_shape=jax.ShapeDtypeStruct((8, 512), F32),
        in_specs=[vmem, smem, vmem, vmem, vmem, vmem, vmem, hbm, hbm, hbm, hbm, hbm],
        out_specs=vmem,
        scratch_shapes=[
            pltpu.VMEM((2, 32, 128, 768), BF),
            pltpu.VMEM((2, QW, 1024), BF),
            pltpu.VMEM((vocab, D), BF),
            pltpu.VMEM((NM, 16, 4096), BF),
            pltpu.VMEM((2, NM, NY, ROWS, 128), BF),
            pltpu.VMEM((2, NY, ROWS, 1024), BF),
            pltpu.VMEM((ROWS, 128), F32),
            pltpu.VMEM((ROWS, 768), F32),
            pltpu.VMEM((2, NY, ROWS, 128), BF),
            pltpu.VMEM((NY, ROWS, QW), BF),
            pltpu.VMEM((2, NZ, NY * ROWS, 128), BF),
            pltpu.VMEM((2, NZ, NY * ROWS, 128), BF),
            pltpu.VMEM((2, NZ, NY * ROWS, 128), F32),
            pltpu.VMEM((2, NZ, NY * ROWS, 128), BF),
            pltpu.VMEM((2, NZ, NY * ROWS, 128), BF),
            pltpu.VMEM((2, NY, ROWS, 128), BF),
            pltpu.VMEM((2, 272, D), BF),
            pltpu.VMEM((vocab, 256), F32),
            pltpu.VMEM((8, 512), F32),
            pltpu.VMEM((NY, 8, 512), F32),
            pltpu.VMEM((NM, 8, 512), F32),
            pltpu.VMEM((NX, 8, 512), F32),
            dma((23,)),
            dma((8,)), dma((8,)),
            dma((2, 4)), dma((2, 4)),
            dma((2, 8)), dma((2, 8)),
            dma((2, 4)), dma((2, 4)),
            dma((4,)), dma((4,)),
            dma((2, 4)), dma((2, 4)),
            dma((2, 4)), dma((2, 4)),
            dma((2, 36)), dma((2, 32)),
            dma((3, 8)), dma((3, 8)),
        ],
        compiler_params=pltpu.CompilerParams(
            collective_id=0, has_side_effects=True, vmem_limit_bytes=60 * 1024 * 1024),
        cost_estimate=pl.CostEstimate(flops=8_000_000_000, bytes_accessed=24_000_000,
                                      transcendentals=300_000),
    )(
        emb, lengths, tgt, attn_gain, final_gain.reshape(1, D), jnp.asarray(cos), jnp.asarray(sin),
        w_query.reshape(32, 2, 128, 512), w_key.reshape(32, 2, 128, 128),
        w_value.reshape(32, 2, 128, 128), w_out.reshape(512, 2048), head,
    )
    slots = stats[0].reshape(2, NY, NM, 2, 4).transpose(0, 1, 3, 2, 4).reshape(2, 8, 32)
    chosen = lax.dynamic_slice_in_dim(source, d * 2, 2, 0)
    live = jnp.take(lengths, chosen, axis=0)
    picked = jnp.take(slots, chosen, axis=1)
    valid = jnp.arange(32)[None, :] < live[:, None]
    result = jnp.where(valid[None], picked, F32(0.0))
    return (result[0], result[1])


def solution(mesh):
    return jax.shard_map(
        per_device,
        mesh=mesh,
        in_specs=(
            P("dp", "mp", None),
            P(),
            P(),
            P(),
            P("section", None),
            P("section", None, "mp"),
            P("section", None, "mp"),
            P("section", None, "mp"),
            P("section", "mp", "dp"),
            P(),
            P(("dp", "section", "mp"), None),
        ),
        out_specs=(P("dp", None), P("dp", None)),
        check_vma=False,
    )
```

time: 807 us -> 178 us (0.22)
  waiting for transfers between devices: 453 us -> 0 us
  blocking collectives: 194 us -> 0 us
  Pallas kernels: 0 us -> 171 us
  matrix products: 78.4 us -> 0 us
  other arithmetic: 26.7 us -> 0.25 us
  local copies, waits for them, and re-layouts: 27.8 us -> 5.99 us
  between operations: 14.3 us -> 0.69 us
    psum x5 -> x0, waiting for transfers between devices: 295 us -> none  [apply_layer(): lax.psum(jnp.dot(context, out_w, preferred_element_type=jnp.float32), 'mp')]
    all_gather x9 -> x0, blocking collectives: 194 us -> none  [the longest x3 100 us: joined_2(): gathered = jax.tree.map(lambda a: lax.all_gather(a, axis), part)]
    pallas_call x0 -> x1, Pallas kernels: none -> 171 us  [per_device(): pl.pallas_call(kernel, out_shape=jax.ShapeDtypeStruct((8, 512), F32), in_...]
    all_gather x2 -> x0, waiting for transfers between devices: 136 us -> none  [the longest x1 71.8 us: per_device(): lax.all_gather(w_out, 'dp', axis=2, tiled=True)]
    dot_general x26 -> x0, matrix products: 78.4 us -> none  [the longest x5 29.5 us: apply_layer(): jnp.dot(context, out_w, preferred_element_type=jnp.float32)]
    ppermute x6 -> x0, waiting for transfers between devices: 20.7 us -> none  [shifted_2(): return lax.ppermute(value, axis, pairs)]
    unnamed x10 -> x4, local copies, waits for them, and re-layouts: 12.6 us -> 0.01 us
  transfers between devices with their start and end apart: 13 -> 0, of which waited for: 13 -> 0; matrix products, arithmetic and copies ran while one was open for 1% -> 0% of each run, Pallas kernels for 0% -> 0%
where the time goes in v1:
time: 178 us; the launch traced here: 177 us
  Pallas kernels  171 us (96%)
  local copies, waits for them, and re-layouts  5.99 us (3%)
    pallas_call x1, Pallas kernels, per_device(): pl.pallas_call(kernel, out_shape=jax.ShapeDtypeStruct((8, 512), F32), in_...  171 us

profile of v1, /device:TPU:1, one launch (start us, length us, event | category | flops | bytes accessed | tf_op | source)
XLA Modules:
  0.0 177.4 jit_solution(5811962210032588920)
XLA Ops:
  0.6 1.1 reshape.62
  1.7 0.7 copy.24
  2.4 0.8 reshape.64
  3.2 0.7 reshape.65.tgt
  3.9 0.0 copy-start.1
  3.9 0.0 copy-start
  3.9 170.5 %shard_map.140 = f32[8,512]{1,0:T(8,128)} custom-call(bf16[16,4096]{1,0:T(8,128)(2,1)} %bitcast.21, s32[8]{0:T(128)} %live.1, s32[1,256]{1,0:T(1,128)} %reshape.65.tgt, f32[1,8192]{1,0:T(1,128)} %gain.1, f32[1,8192]{1,0:T(1,128)} %bitcast.29, f32[64,128]{1,0:T(8,128)} %constant.45.clone.cosine, f32[64,128]{1,0:T(8,128)} %constant.46.clone.sine, ...), custom_call_target="tpu_custom_call" | custom-call | flops 8000000000 | bytes 24000000 | tf_op jit(solution)/shard_map/pallas_call | solution.py:572
  174.4 0.7 slice_reduce_fusion
  175.1 0.1 reshape_squeeze.3
  175.3 0.1 reshape.90
  175.4 0.0 copy-done.1
  175.4 0.1 compare_and_fusion
  175.5 0.6 gather_fusion.1
  176.1 0.0 copy-done
  176.1 0.6 gather_fusion
  176.7 0.1 iota_compare_fusion
  176.8 0.1 select_bitcast_fusion
  176.9 0.6 fusion
  (4 shorter events, 0.0 us)
Async XLA Ops:
  3.9 171.5 %copy-start.1 = (s32[8]{0:T(128)S(1)}, s32[8]{0:T(128)}, u32[]{:S(2)}) copy-start(s32[8]{0:T(128)} %param.16) | copy-start | bytes 100
  3.9 172.2 %copy-start = (s32[8]{0:T(128)S(1)}, s32[8]{0:T(128)}, u32[]{:S(2)}) copy-start(s32[8]{0:T(128)} %live.1) | copy-start | bytes 100

commit v2 on v1

--- a/solution.py
+++ b/solution.py
@@ -90,20 +90,29 @@
         pl.semaphore_signal(barrier, inc=1, device_id=dev, device_id_type=MESH)
     pl.semaphore_wait(barrier, len(partners))
 
+    ahead = jnp.where(c == 0, 1, 3)
+    behind = jnp.where(c == 0, 3, 1)
+    steps = {"behind": behind, "ahead": ahead, "far": 2, "own": 0}
+    sends = {"own": 4, "behind": 5, "ahead": 6, "far": 7}
+
     def eb_z(k):
         return rcopy(EB.at[m], EB.at[m], eb_s.at[k], eb_r.at[m], (d, s, zpeer(k)))
 
-    def eb_z_in(k):
-        mk = zpeer(k)
-        return rcopy(EB.at[mk], EB.at[mk], eb_s.at[k], eb_r.at[mk], (d, s, zpeer(k)))
-
-    def eb_fwd(k):
-        mk = zpeer(k)
-        return rcopy(EB.at[mk], EB.at[mk], eb_s.at[4 + k], eb_r.at[mk], here)
+    def eb_in(who):
+        mk = zpeer(steps[who])
+        return rcopy(EB.at[mk], EB.at[mk], eb_s.at[0], eb_r.at[mk], here)
+
+    def eb_relay():
+        mk = zpeer(behind)
+        return rcopy(EB.at[mk], EB.at[mk], eb_s.at[2], eb_r.at[mk], (d, s, zpeer(ahead)))
+
+    def eb_fwd(who):
+        mk = zpeer(steps[who])
+        return rcopy(EB.at[mk], EB.at[mk], eb_s.at[sends[who]], eb_r.at[mk], here)
 
     def eb_sib_in(k):
         mk = zother(k)
-        return rcopy(EB.at[mk], EB.at[mk], eb_s.at[4 + k], eb_r.at[mk], here)
+        return rcopy(EB.at[mk], EB.at[mk], eb_s.at[0], eb_r.at[mk], here)
 
     def hop(h, g):
         return rcopy(HP.at[h, g], X.at[h, m, d], hop_s.at[h, g], hop_r.at[h, d],
@@ -116,17 +125,22 @@
     def ag_z(h, k):
         return rcopy(X.at[h, m], X.at[h, m], ag_s.at[h, k], ag_r.at[h, m], (d, s, zpeer(k)))
 
-    def ag_z_in(h, k):
-        mk = zpeer(k)
-        return rcopy(X.at[h, mk], X.at[h, mk], ag_s.at[h, k], ag_r.at[h, mk], (d, s, zpeer(k)))
-
-    def ag_fwd(h, k):
-        mk = zpeer(k)
-        return rcopy(X.at[h, mk], X.at[h, mk], ag_s.at[h, 4 + k], ag_r.at[h, mk], here)
+    def ag_in(h, who):
+        mk = zpeer(steps[who])
+        return rcopy(X.at[h, mk], X.at[h, mk], ag_s.at[h, 0], ag_r.at[h, mk], here)
+
+    def ag_relay(h):
+        mk = zpeer(behind)
+        return rcopy(X.at[h, mk], X.at[h, mk], ag_s.at[h, 2], ag_r.at[h, mk],
+                     (d, s, zpeer(ahead)))
+
+    def ag_fwd(h, who):
+        mk = zpeer(steps[who])
+        return rcopy(X.at[h, mk], X.at[h, mk], ag_s.at[h, sends[who]], ag_r.at[h, mk], here)
 
     def ag_sib_in(h, k):
         mk = zother(k)
-        return rcopy(X.at[h, mk], X.at[h, mk], ag_s.at[h, 4 + k], ag_r.at[h, mk], here)
+        return rcopy(X.at[h, mk], X.at[h, mk], ag_s.at[h, 0], ag_r.at[h, mk], here)
 
     def res(h, k):
         g = ypeer(k)
@@ -141,18 +155,18 @@
 
     def ctx_in(k):
         g = ypeer(k)
-        return rcopy(C.at[g], C.at[g], ctx_s.at[k], ctx_r.at[g], (g, s, m))
+        return rcopy(C.at[g], C.at[g], ctx_s.at[0], ctx_r.at[g], here)
+
+    def ctx_relay():
+        g = ypeer(behind)
+        return rcopy(C.at[g], C.at[g], ctx_s.at[2], ctx_r.at[g], (ypeer(ahead), s, m))
 
     def part(h, zz):
         return rcopy(PS.at[h, zz], PR.at[h, zz], ps_s.at[h, zz], ps_r.at[h, zz], here)
 
-    def zred(h, k):
-        zt = (z + k) % NZ
-        return rcopy(ZS.at[h, zt], ZR.at[h, z], zz_s.at[h, k], zz_r.at[h, z], (d, s, zpeer(k)))
-
-    def zred_in(h, k):
-        zt = (z + k) % NZ
-        return rcopy(ZS.at[h, zt], ZR.at[h, zt], zz_s.at[h, k], zz_r.at[h, zt], (d, s, zpeer(k)))
+    def zred(h, i):
+        return rcopy(ZS.at[h, i], ZR.at[h, i], zz_s.at[h, i], zz_r.at[h, i],
+                     (d, s, zpeer(behind if i == 1 else ahead)))
 
     def norm_block(h, g, mm, x):
         col = g * 2048 + mm * 256 + h * 128
@@ -165,11 +179,16 @@
         @pl.when(s == 0)
         def _():
             EB.at[m][...] = emb[...]
-            for k in (2, 1, 3, 0):
-                (eb_z(k) if k else eb_fwd(0)).start()
-            for k in (1, 3, 2):
-                eb_z_in(k).wait_recv()
-                eb_fwd(k).start()
+            eb_z(1).start()
+            eb_z(3).start()
+            eb_fwd("own").start()
+            eb_in("behind").wait_recv()
+            eb_relay().start()
+            eb_fwd("behind").start()
+            eb_in("ahead").wait_recv()
+            eb_fwd("ahead").start()
+            eb_in("far").wait_recv()
+            eb_fwd("far").start()
             for k in range(4):
                 eb_sib_in(k).wait_recv()
 
@@ -197,15 +216,21 @@
             for h in range(2):
                 for g in range(NY):
                     hop_in(h, g).wait_recv()
-                for k in (2, 1, 3, 0):
-                    (ag_z(h, k) if k else ag_fwd(h, 0)).start()
-            for h in range(2):
+                ag_z(h, 1).start()
+                ag_z(h, 3).start()
+                ag_fwd(h, "own").start()
+            for h in range(2):
+                ag_in(h, "behind").wait_recv()
+                ag_relay(h).start()
+                ag_fwd(h, "behind").start()
+            for h in range(2):
+                ag_in(h, "ahead").wait_recv()
+                ag_fwd(h, "ahead").start()
                 for k in (2, 1, 3):
                     res(h, k).start()
             for h in range(2):
-                for k in (1, 3, 2):
-                    ag_z_in(h, k).wait_recv()
-                    ag_fwd(h, k).start()
+                ag_in(h, "far").wait_recv()
+                ag_fwd(h, "far").start()
 
         QA[...] = jnp.zeros_like(QA)
         for h in range(2):
@@ -260,19 +285,22 @@
         mixed = jnp.dot(probs, value, preferred_element_type=F32).astype(BF)
         for j in range(4):
             C.at[d][:, j * HD:(j + 1) * HD] = mixed[j * ROWS:(j + 1) * ROWS]
-        for k in (2, 1, 3):
-            ctx(k).start()
-
+        ctx(1).start()
+        ctx(3).start()
         for h in range(2):
             R.at[h, d][...] = X[h, m, d]
         for copy in wo_loads:
             copy.wait()
-        for k in (1, 3, 2):
-            ctx_in(k).wait_recv()
+        ctx_in(behind).wait_recv()
+        ctx_relay().start()
+        ctx_in(ahead).wait_recv()
+        ctx_in(2).wait_recv()
 
         context = C[...].reshape(NY * ROWS, QW)
         for h in range(2):
-            def project(zz, _):
+            def project(i, _):
+                step = jnp.where(i == 0, 2, jnp.where(i == 1, behind, jnp.where(i == 2, ahead, 0)))
+                zz = (z + step) % NZ
                 p = jnp.dot(context, WO[h, :, lane(zz * 256, 256)], preferred_element_type=F32)
                 low, high = p[:, :128], p[:, 128:]
                 PO.at[h, zz][...] = jnp.where(c == 0, low, high)
@@ -282,55 +310,69 @@
 
             lax.fori_loop(0, NZ, project, 0)
 
-        for h in range(2):
-            for k in (2, 1, 3):
-                zt = (z + k) % NZ
-                part(h, zt).wait_recv()
-                ZS.at[h, zt][...] = (PO[h, zt] + PR[h, zt].astype(F32)).astype(BF)
-                zred(h, k).start()
-        for h in range(2):
-            part(h, z).wait_recv()
-            total = PO[h, z] + PR[h, z].astype(F32)
+        def pair(h, k):
+            zt = (z + k) % NZ
+            part(h, zt).wait_recv()
+            return PO[h, zt] + PR[h, zt].astype(F32)
+
+        for h in range(2):
+            ZS.at[h, 0][...] = pair(h, 2).astype(BF)
+            zred(h, 0).start()
+            ZS.at[h, 1][...] = pair(h, behind).astype(BF)
+            zred(h, 1).start()
+        for h in range(2):
+            both = pair(h, ahead)
+            zred(h, 0).wait_recv()
+            ZS.at[h, 2][...] = (both + ZR[h, 0].astype(F32)).astype(BF)
+            zred(h, 2).start()
+        for h in range(2):
+            total = pair(h, 0)
             for k in (1, 3, 2):
                 res_in(h, k).wait_recv()
             total = total + R[h].astype(F32).reshape(NY * ROWS, 128)
-            for k in (1, 3, 2):
-                zred_in(h, k).wait_recv()
-                total = total + ZR[h, (z + k) % NZ].astype(F32)
-            hidden = total.astype(BF)
-            HP.at[h][...] = hidden.reshape(NY, ROWS, 128)
+            for i in (1, 2):
+                zred(h, i).wait_recv()
+                total = total + ZR[h, i].astype(F32)
+            HP.at[h][...] = total.astype(BF).reshape(NY, ROWS, 128)
 
             @pl.when(s < NX - 1)
             def _():
                 for k in (2, 1, 3, 0):
                     hop(h, ypeer(k)).start()
 
-        @pl.when(s % 2 == 1)
+            @pl.when(s == NX - 1)
+            def _():
+                emit(1, h)
+
+        @pl.when(s == 1)
         def _():
-            b = s // 2
-            sums = jnp.zeros((16, NY * ROWS), F32)
-            ones = jnp.ones((16, 128), BF)
-            nt = (((1,), (1,)), ((), ()))
-            for h in range(2):
-                wide = HP[h].astype(F32).reshape(NY * ROWS, 128)
-                square = wide * wide
-                top = square.astype(BF)
-                rest = (square - top.astype(F32)).astype(BF)
-                sums = sums + lax.dot_general(ones, top, nt, preferred_element_type=F32)
-                sums = sums + lax.dot_general(ones, rest, nt, preferred_element_type=F32)
-                col = d * 2048 + m * 256 + h * 128
-                Y.at[b][0:256, lane(col, 128)] = (wide * fgain[:, lane(col, 128)]).astype(BF)
-            top = sums.astype(BF).astype(F32)
-            row = lax.broadcasted_iota(jnp.int32, (16, NY * ROWS), 0)
-            packed = jnp.where(row == 0, top, jnp.where(row == 1, sums - top, 0.0))
-            Y.at[b][256:272, lane(d * 2048 + m * 256, 256)] = packed.astype(BF)
-
-    def piece(b, g, mm):
-        return Y.at[b, :, lane(g * 2048 + mm * 256, 256)]
-
-    def ycopy(b, g, mm, index, dev):
-        ref = piece(b, g, mm)
-        return rcopy(ref, ref, y_s.at[b, index], y_r.at[b, g * NM + mm], dev)
+            for h in range(2):
+                emit(0, h)
+
+    def emit(b, h):
+        nt = (((1,), (1,)), ((), ()))
+        wide = HP[h].astype(F32).reshape(NY * ROWS, 128)
+        square = wide * wide
+        top = square.astype(BF)
+        rest = (square - top.astype(F32)).astype(BF)
+        ones = jnp.ones((16, 128), BF)
+        sums = (lax.dot_general(ones, top, nt, preferred_element_type=F32)
+                + lax.dot_general(ones, rest, nt, preferred_element_type=F32))
+        cols = lane(d * 2048 + m * 256 + h * 128, 128)
+        Y.at[b][0:256, cols] = (wide * fgain[:, cols]).astype(BF)
+        top = sums.astype(BF).astype(F32)
+        low = sums - top
+        row = lax.broadcasted_iota(jnp.int32, (16, 128), 0)
+        packed = jnp.where(row == 0, top[:, :128], jnp.where(row == 1, low[:, :128],
+                 jnp.where(row == 2, top[:, 128:], jnp.where(row == 3, low[:, 128:], 0.0))))
+        Y.at[b][256:272, cols] = packed.astype(BF)
+        y_x(b, h, 1).start()
+        y_x(b, h, 3).start()
+        spread_own(b, h)
+
+    def ycopy(b, g, mm, h, index, dev):
+        ref = Y.at[b, :, lane(g * 2048 + mm * 256 + h * 128, 128)]
+        return rcopy(ref, ref, y_s.at[b, h, index], y_r.at[b, h, g * NM + mm], dev)
 
     def first_piece(k):
         return (jnp.where(c == 0, ypeer(k), d), jnp.where(c == 0, m, zpeer(k)))
@@ -347,68 +389,125 @@
         g, mm = second_piece(0, k)
         return (g, s, mm)
 
-    def y_x(b, k):
-        return ycopy(b, d, m, k, (d, (s + k) % NX, m))
-
-    def y_first(b, k):
-        return ycopy(b, d, m, 3 + k, first_dev(k))
-
-    def y_second(b, i, k):
+    back = (3, 1)
+
+    def y_x(b, h, k):
+        return ycopy(b, d, m, h, k, (d, (s + k) % NX, m))
+
+    def y_x_relay(b, h):
+        return ycopy(b, d, m, h, 2, (d, jnp.where(b == 0, 3, 1), m))
+
+    def y_first(b, h, k):
+        return ycopy(b, d, m, h, 3 + k, first_dev(k))
+
+    def y_first_relay(b, h):
+        g, mm = first_piece(back[h])
+        return ycopy(b, g, mm, h, 5, first_dev(4 - back[h]))
+
+    def y_second(b, h, i, k):
         g, mm = first_piece(i)
-        return ycopy(b, g, mm, 7 + i * 3 + k - 1, second_dev(k))
-
-    def y_fwd(b, i, k):
+        return ycopy(b, g, mm, h, 7 + i * 3 + k, second_dev(k))
+
+    def y_second_relay(b, h, i):
+        g, mm = second_piece(i, back[h])
+        return ycopy(b, g, mm, h, 9 + i * 3, second_dev(4 - back[h]))
+
+    def y_fwd(b, h, i, k):
         g, mm = second_piece(i, k) if k else first_piece(i)
-        return ycopy(b, g, mm, 19 + i * 4 + k, here)
-
-    def y_in(b, g, mm):
-        return ycopy(b, g, mm, 0, here)
+        return ycopy(b, g, mm, h, 20 + i * 4 + k, here)
+
+    def y_in(b, g, mm, h):
+        return ycopy(b, g, mm, h, 0, here)
+
+    def spread_own(b, h):
+        for k in (1, 3):
+            y_first(b, h, k).start()
+        for k in (1, 3):
+            y_second(b, h, 0, k).start()
+        y_fwd(b, h, 0, 0).start()
+
+    def relays_x(b, h):
+        from_zero = (s == 0) & ((b == 0) | (h == 0))
+        return from_zero | ((s == 2) & (b == 1) & (h == 1))
 
     def score(b):
         source = 2 * b + 1
 
-        @pl.when(s == source)
-        def _():
-            for k in (2, 1, 3):
-                y_x(b, k).start()
-
         @pl.when(s != source)
         def _():
-            y_in(b, d, m).wait_recv()
-
-        for k in (2, 1, 3):
-            y_first(b, k).start()
-        for k in (2, 1, 3):
-            y_second(b, 0, k).start()
-        y_fwd(b, 0, 0).start()
+            for h in range(2):
+                y_in(b, d, m, h).wait_recv()
+
+                @pl.when(relays_x(b, h))
+                def _():
+                    y_x_relay(b, h).start()
+
+                spread_own(b, h)
+
+        def arrived_first(i, h):
+            g, mm = first_piece(i)
+            y_in(b, g, mm, h).wait_recv()
+            if i == back[h]:
+                y_first_relay(b, h).start()
+            for k in (1, 3):
+                y_second(b, h, i, k).start()
+            y_fwd(b, h, i, 0).start()
+
+        def arrived_second(i, h, k):
+            g, mm = second_piece(i, k)
+            y_in(b, g, mm, h).wait_recv()
+            if k == back[h]:
+                y_second_relay(b, h, i).start()
+            y_fwd(b, h, i, k).start()
+
+        def arrived_ring(i):
+            for h in range(2):
+                arrived_second(i, h, back[h])
+            for h in range(2):
+                arrived_second(i, h, 4 - back[h])
+
+        for h in range(2):
+            arrived_first(back[h], h)
+        for h in range(2):
+            arrived_first(4 - back[h], h)
+        arrived_ring(0)
+        for h in range(2):
+            arrived_first(2, h)
         for i in (1, 3, 2):
-            g, mm = first_piece(i)
-            y_in(b, g, mm).wait_recv()
-            for k in (2, 1, 3):
-                y_second(b, i, k).start()
-            y_fwd(b, i, 0).start()
-        for i in (0, 1, 3, 2):
-            for k in (1, 3, 2):
-                g, mm = second_piece(i, k)
-                y_in(b, g, mm).wait_recv()
-                y_fwd(b, i, k).start()
-        for g in range(NY):
-            for zz in range(NZ):
-                y_in(b, g, zz * 2 + (1 - c)).wait_recv()
-
-        LT[...] = jnp.zeros_like(LT)
-
-        def dots(g, _):
+            arrived_ring(i)
+
+        def dots(k):
+            g = ypeer(k)
+            for h in range(2):
+                for zz in range(NZ):
+                    y_in(b, g, zz * 2 + (1 - c), h).wait_recv()
             cols = pl.ds(pl.multiple_of(g * 2048, 2048), 2048)
-            LT[...] += lax.dot_general(HEAD[:, cols], Y[b, 0:256, cols],
-                                       (((1,), (1,)), ((), ())), preferred_element_type=F32)
-            return 0
-
-        lax.fori_loop(0, NY, dots, 0)
-        wide = jnp.sum(Y[b, 256:272, :].astype(F32), axis=0, keepdims=True)
-        sums = wide[:, 0:256]
-        for i in range(1, NY * NM):
-            sums = sums + wide[:, i * 256:(i + 1) * 256]
+            term = lax.dot_general(HEAD[:, cols], Y[b, 0:256, cols],
+                                   (((1,), (1,)), ((), ())), preferred_element_type=F32)
+            LT[...] = LT[...] + term if k else term
+
+        def dots_of(j):
+            for h in range(2):
+                arrived_second(j, h, 2)
+            dots(j)
+
+        dots_of(0)
+        for h in range(2):
+            arrived_second(1, h, 2)
+        for h in range(2):
+            arrived_second(3, h, 2)
+        dots(1)
+        dots(3)
+        dots_of(2)
+        extra = Y[b, 256:272, :].astype(F32)
+        halves = []
+        for i in (0, 2):
+            wide = extra[i:i + 1] + extra[i + 1:i + 2]
+            total = wide[:, 0:128]
+            for j in range(1, 2 * NY * NM):
+                total = total + wide[:, j * 128:(j + 1) * 128]
+            halves.append(total)
+        sums = jnp.concatenate(halves, axis=1)
         r = lax.rsqrt(sums * (1.0 / D) + EPS)
         logits = LT[...] * r
         highest = jnp.max(logits, axis=0, keepdims=True)
@@ -501,18 +600,20 @@
 
     @pl.when(s == 0)
     def _():
-        for k in range(4):
-            (eb_z(k) if k else eb_fwd(0)).wait_send()
-        for k in range(1, 4):
-            eb_fwd(k).wait_send()
+        for k in (1, 3):
+            eb_z(k).wait_send()
+        eb_relay().wait_send()
+        for who in sends:
+            eb_fwd(who).wait_send()
 
     @pl.when(s > 0)
     def _():
         for h in range(2):
-            for k in range(1, 4):
+            for k in (1, 3):
                 ag_z(h, k).wait_send()
-            for k in range(4):
-                ag_fwd(h, k).wait_send()
+            ag_relay(h).wait_send()
+            for who in sends:
+                ag_fwd(h, who).wait_send()
 
     @pl.when(s < NX - 1)
     def _():
@@ -523,27 +624,38 @@
     for h in range(2):
         for k in range(1, 4):
             res(h, k).wait_send()
-            zred(h, k).wait_send()
+        for i in range(3):
+            zred(h, i).wait_send()
         for zz in range(NZ):
             part(h, zz).wait_send()
+    for k in (1, 3):
+        ctx(k).wait_send()
+    ctx_relay().wait_send()
     for k in range(1, 4):
-        ctx(k).wait_send()
         st_y(k).wait_send()
         st_x(k).wait_send()
     for k in range(1, 8):
         st_m(k).wait_send()
     for b in range(2):
-        @pl.when(s == 2 * b + 1)
-        def _():
-            for k in range(1, 4):
-                y_x(b, k).wait_send()
-        for k in range(1, 4):
-            y_first(b, k).wait_send()
-        for i in range(4):
-            for k in range(1, 4):
-                y_second(b, i, k).wait_send()
-            for k in range(4):
-                y_fwd(b, i, k).wait_send()
+        for h in range(2):
+            @pl.when(s == 2 * b + 1)
+            def _():
+                for k in (1, 3):
+                    y_x(b, h, k).wait_send()
+
+            @pl.when(relays_x(b, h))
+            def _():
+                y_x_relay(b, h).wait_send()
+
+            for k in (1, 3):
+                y_first(b, h, k).wait_send()
+            y_first_relay(b, h).wait_send()
+            for i in range(4):
+                for k in (1, 3):
+                    y_second(b, h, i, k).wait_send()
+                y_second_relay(b, h, i).wait_send()
+                for k in range(4):
+                    y_fwd(b, h, i, k).wait_send()
 
 
 def tables():
@@ -588,8 +700,8 @@
             pltpu.VMEM((2, NZ, NY * ROWS, 128), BF),
             pltpu.VMEM((2, NZ, NY * ROWS, 128), BF),
             pltpu.VMEM((2, NZ, NY * ROWS, 128), F32),
-            pltpu.VMEM((2, NZ, NY * ROWS, 128), BF),
-            pltpu.VMEM((2, NZ, NY * ROWS, 128), BF),
+            pltpu.VMEM((2, 3, NY * ROWS, 128), BF),
+            pltpu.VMEM((2, 3, NY * ROWS, 128), BF),
             pltpu.VMEM((2, NY, ROWS, 128), BF),
             pltpu.VMEM((2, 272, D), BF),
             pltpu.VMEM((vocab, 256), F32),
@@ -605,7 +717,7 @@
             dma((4,)), dma((4,)),
             dma((2, 4)), dma((2, 4)),
             dma((2, 4)), dma((2, 4)),
-            dma((2, 36)), dma((2, 32)),
+            dma((2, 2, 36)), dma((2, 2, 32)),
             dma((3, 8)), dma((3, 8)),
         ],
         compiler_params=pltpu.CompilerParams(

time: 178 us -> 189 us (1.062)
  Pallas kernels: 171 us -> 181 us
    pallas_call x1, Pallas kernels: 171 us -> 181 us  [per_device(): pl.pallas_call(kernel, out_shape=jax.ShapeDtypeStruct((8, 512), F32), in_...]
where the time goes in v2:
time: 189 us; the launch traced here: 188 us
  Pallas kernels  181 us (96%)
  local copies, waits for them, and re-layouts  5.99 us (3%)
    pallas_call x1, Pallas kernels, per_device(): pl.pallas_call(kernel, out_shape=jax.ShapeDtypeStruct((8, 512), F32), in_...  181 us

profile of v2, /device:TPU:1, one launch (start us, length us, event | category | flops | bytes accessed | tf_op | source)
XLA Modules:
  0.0 188.0 jit_solution(16727415543728140126)
XLA Ops:
  0.6 1.1 reshape.62
  1.7 0.7 copy.24
  2.4 0.8 reshape.64
  3.2 0.7 reshape.65.tgt
  3.9 0.0 copy-start.1
  3.9 0.0 copy-start
  3.9 181.1 %shard_map.140 = f32[8,512]{1,0:T(8,128)} custom-call(bf16[16,4096]{1,0:T(8,128)(2,1)} %bitcast.21, s32[8]{0:T(128)} %live.1, s32[1,256]{1,0:T(1,128)} %reshape.65.tgt, f32[1,8192]{1,0:T(1,128)} %gain.1, f32[1,8192]{1,0:T(1,128)} %bitcast.29, f32[64,128]{1,0:T(8,128)} %constant.45.clone.cosine, f32[64,128]{1,0:T(8,128)} %constant.46.clone.sine, ...), custom_call_target="tpu_custom_call" | custom-call | flops 8000000000 | bytes 24000000 | tf_op jit(solution)/shard_map/pallas_call | solution.py:684
  185.0 0.7 slice_reduce_fusion
  185.7 0.1 reshape_squeeze.3
  185.9 0.1 reshape.90
  186.0 0.0 copy-done.1
  186.0 0.1 compare_and_fusion
  186.1 0.6 gather_fusion.1
  186.7 0.0 copy-done
  186.7 0.6 gather_fusion
  187.3 0.1 iota_compare_fusion
  187.4 0.1 select_bitcast_fusion
  187.5 0.6 fusion
  (4 shorter events, 0.0 us)
Async XLA Ops:
  3.9 182.1 %copy-start.1 = (s32[8]{0:T(128)S(1)}, s32[8]{0:T(128)}, u32[]{:S(2)}) copy-start(s32[8]{0:T(128)} %param.16) | copy-start | bytes 100
  3.9 182.8 %copy-start = (s32[8]{0:T(128)S(1)}, s32[8]{0:T(128)}, u32[]{:S(2)}) copy-start(s32[8]{0:T(128)} %live.1) | copy-start | bytes 100

commit v3 on v2

--- a/solution.py
+++ b/solution.py
@@ -68,13 +68,11 @@
             wo_loads.append(pltpu.make_async_copy(
                 wo.at[:, mm * 256 + h * 128: mm * 256 + h * 128 + 128],
                 WO.at[h, :, mm * 128: mm * 128 + 128], w_sem.at[6 + h * NM + mm]))
-    head_load = pltpu.make_async_copy(head, HEAD, w_sem.at[22])
     for group in loads:
         for copy in group:
             copy.start()
     for copy in wo_loads:
         copy.start()
-    head_load.start()
 
     barrier = pltpu.get_barrier_semaphore()
     partners = []
@@ -88,6 +86,16 @@
     partners.append(here)
     for dev in partners:
         pl.semaphore_signal(barrier, inc=1, device_id=dev, device_id_type=MESH)
+    offsets = (0, 3, 1, 2)
+    for cc in range(2):
+        for j in range(4):
+            for i in range(4):
+                g, zz = (offsets[i], offsets[j]) if cc == 0 else (offsets[j], offsets[i])
+                col = ypeer(g) * 2048 + ((z + zz) % NZ) * 512 + cc * 256
+                pltpu.make_async_copy(head.at[:, lane(col, 256)],
+                                      HEAD.at[cc, j, :, i * 256:i * 256 + 256],
+                                      w_sem.at[22]).start()
+    head_load = pltpu.make_async_copy(HEAD, HEAD, w_sem.at[22])
     pl.semaphore_wait(barrier, len(partners))
 
     ahead = jnp.where(c == 0, 1, 3)
@@ -340,179 +348,166 @@
                 for k in (2, 1, 3, 0):
                     hop(h, ypeer(k)).start()
 
-            @pl.when(s == NX - 1)
-            def _():
-                emit(1, h)
-
-        @pl.when(s == 1)
+        @pl.when(s % 2 == 1)
         def _():
-            for h in range(2):
-                emit(0, h)
-
-    def emit(b, h):
+            emit(s // 2)
+
+    def emit(b):
         nt = (((1,), (1,)), ((), ()))
-        wide = HP[h].astype(F32).reshape(NY * ROWS, 128)
-        square = wide * wide
-        top = square.astype(BF)
-        rest = (square - top.astype(F32)).astype(BF)
         ones = jnp.ones((16, 128), BF)
-        sums = (lax.dot_general(ones, top, nt, preferred_element_type=F32)
-                + lax.dot_general(ones, rest, nt, preferred_element_type=F32))
-        cols = lane(d * 2048 + m * 256 + h * 128, 128)
-        Y.at[b][0:256, cols] = (wide * fgain[:, cols]).astype(BF)
+        sums = jnp.zeros((16, NY * ROWS), F32)
+        mine = Y.at[b, c, 0, 0]
+        for h in range(2):
+            wide = HP[h].astype(F32).reshape(NY * ROWS, 128)
+            square = wide * wide
+            top = square.astype(BF)
+            rest = (square - top.astype(F32)).astype(BF)
+            sums = sums + lax.dot_general(ones, top, nt, preferred_element_type=F32)
+            sums = sums + lax.dot_general(ones, rest, nt, preferred_element_type=F32)
+            cols = lane(d * 2048 + m * 256 + h * 128, 128)
+            mine[0:256, h * 128:h * 128 + 128] = (wide * fgain[:, cols]).astype(BF)
         top = sums.astype(BF).astype(F32)
-        low = sums - top
-        row = lax.broadcasted_iota(jnp.int32, (16, 128), 0)
-        packed = jnp.where(row == 0, top[:, :128], jnp.where(row == 1, low[:, :128],
-                 jnp.where(row == 2, top[:, 128:], jnp.where(row == 3, low[:, 128:], 0.0))))
-        Y.at[b][256:272, cols] = packed.astype(BF)
-        y_x(b, h, 1).start()
-        y_x(b, h, 3).start()
-        spread_own(b, h)
-
-    def ycopy(b, g, mm, h, index, dev):
-        ref = Y.at[b, :, lane(g * 2048 + mm * 256 + h * 128, 128)]
-        return rcopy(ref, ref, y_s.at[b, h, index], y_r.at[b, h, g * NM + mm], dev)
-
-    def first_piece(k):
-        return (jnp.where(c == 0, ypeer(k), d), jnp.where(c == 0, m, zpeer(k)))
-
-    def second_piece(i, k):
-        g0, m0 = first_piece(i)
-        return (jnp.where(c == 0, g0, ypeer(k)), jnp.where(c == 0, zpeer(k), m0))
+        row = lax.broadcasted_iota(jnp.int32, (16, NY * ROWS), 0)
+        packed = jnp.where(row == 0, top, jnp.where(row == 1, sums - top, 0.0))
+        mine[256:272, :] = packed.astype(BF)
+        y_x(b, 1).start()
+        y_x(b, 3).start()
+        spread_own(b)
 
     def first_dev(k):
-        g, mm = first_piece(k)
-        return (g, s, mm)
+        return (jnp.where(c == 0, ypeer(k), d), s, jnp.where(c == 0, m, zpeer(k)))
 
     def second_dev(k):
-        g, mm = second_piece(0, k)
-        return (g, s, mm)
-
-    back = (3, 1)
-
-    def y_x(b, h, k):
-        return ycopy(b, d, m, h, k, (d, (s + k) % NX, m))
-
-    def y_x_relay(b, h):
-        return ycopy(b, d, m, h, 2, (d, jnp.where(b == 0, 3, 1), m))
-
-    def y_first(b, h, k):
-        return ycopy(b, d, m, h, 3 + k, first_dev(k))
-
-    def y_first_relay(b, h):
-        g, mm = first_piece(back[h])
-        return ycopy(b, g, mm, h, 5, first_dev(4 - back[h]))
-
-    def y_second(b, h, i, k):
-        g, mm = first_piece(i)
-        return ycopy(b, g, mm, h, 7 + i * 3 + k, second_dev(k))
-
-    def y_second_relay(b, h, i):
-        g, mm = second_piece(i, back[h])
-        return ycopy(b, g, mm, h, 9 + i * 3, second_dev(4 - back[h]))
-
-    def y_fwd(b, h, i, k):
-        g, mm = second_piece(i, k) if k else first_piece(i)
-        return ycopy(b, g, mm, h, 20 + i * 4 + k, here)
-
-    def y_in(b, g, mm, h):
-        return ycopy(b, g, mm, h, 0, here)
-
-    def spread_own(b, h):
+        return (jnp.where(c == 0, d, ypeer(k)), s, jnp.where(c == 0, zpeer(k), m))
+
+    def ycopy(src, dst, b, i, j, dev):
+        return rcopy(src, dst, y_s.at[b, i], y_r.at[b, j], dev)
+
+    def y_x(b, k):
+        ref = Y.at[b, c, 0, 0]
+        return ycopy(ref, ref, b, k, 0, (d, (s + k) % NX, m))
+
+    cut = (pl.ds(0, 144), pl.ds(144, 128))
+
+    def y_x_relay(b, half):
+        ref = Y.at[b, c, 0, 0, cut[half]]
+        return ycopy(ref, ref, b, 4 + half, 0, (d, jnp.where(b == 0, 3, 1), m))
+
+    def relays_x(b, half):
+        return (s == 0) if half == 0 else (s == jnp.where(b == 0, 0, 2))
+
+    def y_first(b, k):
+        slot = 1 if k == 1 else 2
+        return ycopy(Y.at[b, c, 0, 0], Y.at[b, c, 0, slot], b, 5 + k, slot, first_dev(k))
+
+    def y_first_relay(b, half):
+        slot, k = ((1, 1), (2, 3))[half]
+        return ycopy(Y.at[b, c, 0, slot, cut[half]], Y.at[b, c, 0, 3, cut[half]],
+                     b, 9 + half, 3, first_dev(k))
+
+    def y_opposite(b):
+        ref = Y.at[b, c, 0, 3]
+        return ycopy(ref, ref, b, 9, 3, here)
+
+    sets = (pl.ds(0, 1), pl.ds(1, 2), pl.ds(3, 1))
+
+    def y_second(b, part_no, k):
+        slot = 1 if k == 1 else 2
+        return ycopy(Y.at[b, c, 0, sets[part_no]], Y.at[b, c, slot, sets[part_no]],
+                     b, 11 + part_no * 2 + (slot - 1), 1 + 3 * slot + part_no, second_dev(k))
+
+    def y_second_relay(b, i):
+        slot, k = (1, 1) if i < 2 else (2, 3)
+        return ycopy(Y.at[b, c, slot, i], Y.at[b, c, 3, i], b, 17 + i, 10 + i, second_dev(k))
+
+    forwards = ((0, 0, 1), (0, 1, 2), (0, 3, 1), (1, 0, 4), (2, 0, 4), (3, 0, 2), (3, 2, 2))
+
+    def y_fwd(b, n, who):
+        j, i, size = forwards[n]
+        ref = Y.at[b, who, j, pl.ds(i, size)]
+        return ycopy(ref, ref, b, 21 + n, 14 + n, here)
+
+    def spread_own(b):
         for k in (1, 3):
-            y_first(b, h, k).start()
+            y_first(b, k).start()
         for k in (1, 3):
-            y_second(b, h, 0, k).start()
-        y_fwd(b, h, 0, 0).start()
-
-    def relays_x(b, h):
-        from_zero = (s == 0) & ((b == 0) | (h == 0))
-        return from_zero | ((s == 2) & (b == 1) & (h == 1))
+            y_second(b, 0, k).start()
+        y_fwd(b, 0, c).start()
+
+    def dots(b, cc, j, start):
+        pieces = jnp.concatenate([Y[b, cc, j, i, 0:256, :] for i in range(4)], axis=1)
+        term = lax.dot_general(HEAD[cc, j], pieces, (((1,), (1,)), ((), ())),
+                               preferred_element_type=F32)
+        LT[...] = term if start else LT[...] + term
 
     def score(b):
         source = 2 * b + 1
 
         @pl.when(s != source)
         def _():
-            for h in range(2):
-                y_in(b, d, m, h).wait_recv()
-
-                @pl.when(relays_x(b, h))
+            y_x(b, 1).wait_recv()
+            for half in range(2):
+                @pl.when(relays_x(b, half))
                 def _():
-                    y_x_relay(b, h).start()
-
-                spread_own(b, h)
-
-        def arrived_first(i, h):
-            g, mm = first_piece(i)
-            y_in(b, g, mm, h).wait_recv()
-            if i == back[h]:
-                y_first_relay(b, h).start()
-            for k in (1, 3):
-                y_second(b, h, i, k).start()
-            y_fwd(b, h, i, 0).start()
-
-        def arrived_second(i, h, k):
-            g, mm = second_piece(i, k)
-            y_in(b, g, mm, h).wait_recv()
-            if k == back[h]:
-                y_second_relay(b, h, i).start()
-            y_fwd(b, h, i, k).start()
-
-        def arrived_ring(i):
-            for h in range(2):
-                arrived_second(i, h, back[h])
-            for h in range(2):
-                arrived_second(i, h, 4 - back[h])
-
-        for h in range(2):
-            arrived_first(back[h], h)
-        for h in range(2):
-            arrived_first(4 - back[h], h)
-        arrived_ring(0)
-        for h in range(2):
-            arrived_first(2, h)
-        for i in (1, 3, 2):
-            arrived_ring(i)
-
-        def dots(k):
-            g = ypeer(k)
-            for h in range(2):
-                for zz in range(NZ):
-                    y_in(b, g, zz * 2 + (1 - c), h).wait_recv()
-            cols = pl.ds(pl.multiple_of(g * 2048, 2048), 2048)
-            term = lax.dot_general(HEAD[:, cols], Y[b, 0:256, cols],
-                                   (((1,), (1,)), ((), ())), preferred_element_type=F32)
-            LT[...] = LT[...] + term if k else term
-
-        def dots_of(j):
-            for h in range(2):
-                arrived_second(j, h, 2)
-            dots(j)
-
-        dots_of(0)
-        for h in range(2):
-            arrived_second(1, h, 2)
-        for h in range(2):
-            arrived_second(3, h, 2)
-        dots(1)
-        dots(3)
-        dots_of(2)
-        extra = Y[b, 256:272, :].astype(F32)
-        halves = []
-        for i in (0, 2):
-            wide = extra[i:i + 1] + extra[i + 1:i + 2]
-            total = wide[:, 0:128]
-            for j in range(1, 2 * NY * NM):
-                total = total + wide[:, j * 128:(j + 1) * 128]
-            halves.append(total)
-        sums = jnp.concatenate(halves, axis=1)
+                    y_x_relay(b, half).start()
+            spread_own(b)
+
+        y_first(b, 1).wait_recv()
+        y_first_relay(b, 0).start()
+        y_first(b, 3).wait_recv()
+        y_first_relay(b, 1).start()
+        for k in (1, 3):
+            y_second(b, 1, k).start()
+        y_fwd(b, 1, c).start()
+        y_second(b, 0, 1).wait_recv()
+        y_second_relay(b, 0).start()
+        y_second(b, 0, 3).wait_recv()
+        y_opposite(b).wait_recv()
+        for k in (1, 3):
+            y_second(b, 2, k).start()
+        y_fwd(b, 2, c).start()
+        y_second(b, 1, 1).wait_recv()
+        y_second_relay(b, 1).start()
+        y_second(b, 1, 3).wait_recv()
+        y_second_relay(b, 2).start()
+        y_second(b, 2, 3).wait_recv()
+        y_second_relay(b, 3).start()
+        y_fwd(b, 4, c).start()
+        y_second(b, 2, 1).wait_recv()
+        y_fwd(b, 3, c).start()
+
+        dots(b, c, 0, True)
+        for n in range(3):
+            y_fwd(b, n, 1 - c).wait_recv()
+        dots(b, 1 - c, 0, False)
+        dots(b, c, 2, False)
+        dots(b, c, 1, False)
+        y_second_relay(b, 0).wait_recv()
+        y_second_relay(b, 1).wait_recv()
+        y_fwd(b, 5, c).start()
+        y_fwd(b, 4, 1 - c).wait_recv()
+        dots(b, 1 - c, 2, False)
+        y_second_relay(b, 2).wait_recv()
+        y_second_relay(b, 3).wait_recv()
+        y_fwd(b, 6, c).start()
+        y_fwd(b, 3, 1 - c).wait_recv()
+        dots(b, 1 - c, 1, False)
+        dots(b, c, 3, False)
+        y_fwd(b, 5, 1 - c).wait_recv()
+        y_fwd(b, 6, 1 - c).wait_recv()
+        dots(b, 1 - c, 3, False)
+
+        extra = jnp.zeros((16, 256), F32)
+        for cc in range(2):
+            for j in range(4):
+                for i in range(4):
+                    extra = extra + Y[b, cc, j, i, 256:272, :].astype(F32)
+        sums = jnp.sum(extra, axis=0, keepdims=True)
         r = lax.rsqrt(sums * (1.0 / D) + EPS)
         logits = LT[...] * r
         highest = jnp.max(logits, axis=0, keepdims=True)
         summed = jnp.sum(jnp.exp(logits - highest), axis=0, keepdims=True)
-        vocab = HEAD.shape[0]
+        vocab = HEAD.shape[2]
         wanted = tgt[...] - ((d * NX + s) * NM + m) * vocab
         index = lax.broadcasted_iota(jnp.int32, logits.shape, 0)
         picked = jnp.sum(jnp.where(index == wanted, logits, 0.0), axis=0, keepdims=True)
@@ -637,25 +632,25 @@
     for k in range(1, 8):
         st_m(k).wait_send()
     for b in range(2):
-        for h in range(2):
-            @pl.when(s == 2 * b + 1)
+        @pl.when(s == 2 * b + 1)
+        def _():
+            for k in (1, 3):
+                y_x(b, k).wait_send()
+
+        for half in range(2):
+            @pl.when((s != 2 * b + 1) & relays_x(b, half))
             def _():
-                for k in (1, 3):
-                    y_x(b, h, k).wait_send()
-
-            @pl.when(relays_x(b, h))
-            def _():
-                y_x_relay(b, h).wait_send()
-
-            for k in (1, 3):
-                y_first(b, h, k).wait_send()
-            y_first_relay(b, h).wait_send()
-            for i in range(4):
-                for k in (1, 3):
-                    y_second(b, h, i, k).wait_send()
-                y_second_relay(b, h, i).wait_send()
-                for k in range(4):
-                    y_fwd(b, h, i, k).wait_send()
+                y_x_relay(b, half).wait_send()
+
+            y_first_relay(b, half).wait_send()
+        for k in (1, 3):
+            y_first(b, k).wait_send()
+            for n in range(3):
+                y_second(b, n, k).wait_send()
+        for i in range(4):
+            y_second_relay(b, i).wait_send()
+        for n in range(7):
+            y_fwd(b, n, c).wait_send()
 
 
 def tables():
@@ -689,7 +684,7 @@
         scratch_shapes=[
             pltpu.VMEM((2, 32, 128, 768), BF),
             pltpu.VMEM((2, QW, 1024), BF),
-            pltpu.VMEM((vocab, D), BF),
+            pltpu.VMEM((2, 4, vocab, 1024), BF),
             pltpu.VMEM((NM, 16, 4096), BF),
             pltpu.VMEM((2, NM, NY, ROWS, 128), BF),
             pltpu.VMEM((2, NY, ROWS, 1024), BF),
@@ -703,7 +698,7 @@
             pltpu.VMEM((2, 3, NY * ROWS, 128), BF),
             pltpu.VMEM((2, 3, NY * ROWS, 128), BF),
             pltpu.VMEM((2, NY, ROWS, 128), BF),
-            pltpu.VMEM((2, 272, D), BF),
+            pltpu.VMEM((2, 2, 4, 4, 272, 256), BF),
             pltpu.VMEM((vocab, 256), F32),
             pltpu.VMEM((8, 512), F32),
             pltpu.VMEM((NY, 8, 512), F32),
@@ -717,7 +712,7 @@
             dma((4,)), dma((4,)),
             dma((2, 4)), dma((2, 4)),
             dma((2, 4)), dma((2, 4)),
-            dma((2, 2, 36)), dma((2, 2, 32)),
+            dma((2, 28)), dma((2, 21)),
             dma((3, 8)), dma((3, 8)),
         ],
         compiler_params=pltpu.CompilerParams(

time: 189 us -> 188 us (level)
  no operation moved by 1% of the time
where the time goes in v3:
time: 188 us; the launch traced here: 187 us
  Pallas kernels  180 us (96%)
  local copies, waits for them, and re-layouts  5.99 us (3%)
    pallas_call x1, Pallas kernels, per_device(): pl.pallas_call(kernel, out_shape=jax.ShapeDtypeStruct((8, 512), F32), in_...  180 us

profile of v3, /device:TPU:1, one launch (start us, length us, event | category | flops | bytes accessed | tf_op | source)
XLA Modules:
  0.0 187.4 jit_solution(2306888739069838911)
XLA Ops:
  0.6 1.1 reshape.62
  1.7 0.7 copy.24
  2.4 0.8 reshape.64
  3.2 0.7 reshape.65.tgt
  3.9 0.0 copy-start.1
  3.9 0.0 copy-start
  3.9 180.5 %shard_map.140 = f32[8,512]{1,0:T(8,128)} custom-call(bf16[16,4096]{1,0:T(8,128)(2,1)} %bitcast.21, s32[8]{0:T(128)} %live.1, s32[1,256]{1,0:T(1,128)} %reshape.65.tgt, f32[1,8192]{1,0:T(1,128)} %gain.1, f32[1,8192]{1,0:T(1,128)} %bitcast.29, f32[64,128]{1,0:T(8,128)} %constant.45.clone.cosine, f32[64,128]{1,0:T(8,128)} %constant.46.clone.sine, ...), custom_call_target="tpu_custom_call" | custom-call | flops 8000000000 | bytes 24000000 | tf_op jit(solution)/shard_map/pallas_call | solution.py:679
  184.3 0.7 slice_reduce_fusion
  185.1 0.1 reshape_squeeze.3
  185.2 0.1 reshape.90
  185.3 0.0 copy-done.1
  185.3 0.1 compare_and_fusion
  185.4 0.6 gather_fusion.1
  186.0 0.0 copy-done
  186.0 0.6 gather_fusion
  186.6 0.1 iota_compare_fusion
  186.7 0.1 select_bitcast_fusion
  186.8 0.6 fusion
  (4 shorter events, 0.0 us)
Async XLA Ops:
  3.9 181.5 %copy-start.1 = (s32[8]{0:T(128)S(1)}, s32[8]{0:T(128)}, u32[]{:S(2)}) copy-start(s32[8]{0:T(128)} %param.16) | copy-start | bytes 100
  3.9 182.1 %copy-start = (s32[8]{0:T(128)S(1)}, s32[8]{0:T(128)}, u32[]{:S(2)}) copy-start(s32[8]{0:T(128)} %live.1) | copy-start | bytes 100

commit v4 on v3

--- a/solution.py
+++ b/solution.py
@@ -26,7 +26,8 @@
 
 
 def kernel(
-    emb, live, tgt, gain, fgain, cosine, sine, wq, wk, wv, wo, head, out,
+    emb, live, source_of, targets, gain, fgain, cosine, sine, wq, wk, wv, wo, head,
+    exit_out, final_out,
     W, WO, HEAD, EB, X, XN, SS, QA, R, C, PS, PR, PO, ZS, ZR, HP, Y, LT, STO, SA, SB, SC,
     w_sem, eb_s, eb_r, hop_s, hop_r, ag_s, ag_r, res_s, res_r, ctx_s, ctx_r, ps_s, ps_r,
     zz_s, zz_r, y_s, y_r, st_s, st_r,
@@ -98,29 +99,20 @@
     head_load = pltpu.make_async_copy(HEAD, HEAD, w_sem.at[22])
     pl.semaphore_wait(barrier, len(partners))
 
-    ahead = jnp.where(c == 0, 1, 3)
-    behind = jnp.where(c == 0, 3, 1)
-    steps = {"behind": behind, "ahead": ahead, "far": 2, "own": 0}
-    sends = {"own": 4, "behind": 5, "ahead": 6, "far": 7}
-
     def eb_z(k):
         return rcopy(EB.at[m], EB.at[m], eb_s.at[k], eb_r.at[m], (d, s, zpeer(k)))
 
-    def eb_in(who):
-        mk = zpeer(steps[who])
-        return rcopy(EB.at[mk], EB.at[mk], eb_s.at[0], eb_r.at[mk], here)
-
-    def eb_relay():
-        mk = zpeer(behind)
-        return rcopy(EB.at[mk], EB.at[mk], eb_s.at[2], eb_r.at[mk], (d, s, zpeer(ahead)))
-
-    def eb_fwd(who):
-        mk = zpeer(steps[who])
-        return rcopy(EB.at[mk], EB.at[mk], eb_s.at[sends[who]], eb_r.at[mk], here)
+    def eb_z_in(k):
+        mk = zpeer(k)
+        return rcopy(EB.at[mk], EB.at[mk], eb_s.at[k], eb_r.at[mk], (d, s, zpeer(k)))
+
+    def eb_fwd(k):
+        mk = zpeer(k)
+        return rcopy(EB.at[mk], EB.at[mk], eb_s.at[4 + k], eb_r.at[mk], here)
 
     def eb_sib_in(k):
         mk = zother(k)
-        return rcopy(EB.at[mk], EB.at[mk], eb_s.at[0], eb_r.at[mk], here)
+        return rcopy(EB.at[mk], EB.at[mk], eb_s.at[4 + k], eb_r.at[mk], here)
 
     def hop(h, g):
         return rcopy(HP.at[h, g], X.at[h, m, d], hop_s.at[h, g], hop_r.at[h, d],
@@ -133,22 +125,17 @@
     def ag_z(h, k):
         return rcopy(X.at[h, m], X.at[h, m], ag_s.at[h, k], ag_r.at[h, m], (d, s, zpeer(k)))
 
-    def ag_in(h, who):
-        mk = zpeer(steps[who])
-        return rcopy(X.at[h, mk], X.at[h, mk], ag_s.at[h, 0], ag_r.at[h, mk], here)
-
-    def ag_relay(h):
-        mk = zpeer(behind)
-        return rcopy(X.at[h, mk], X.at[h, mk], ag_s.at[h, 2], ag_r.at[h, mk],
-                     (d, s, zpeer(ahead)))
-
-    def ag_fwd(h, who):
-        mk = zpeer(steps[who])
-        return rcopy(X.at[h, mk], X.at[h, mk], ag_s.at[h, sends[who]], ag_r.at[h, mk], here)
+    def ag_z_in(h, k):
+        mk = zpeer(k)
+        return rcopy(X.at[h, mk], X.at[h, mk], ag_s.at[h, k], ag_r.at[h, mk], (d, s, zpeer(k)))
+
+    def ag_fwd(h, k):
+        mk = zpeer(k)
+        return rcopy(X.at[h, mk], X.at[h, mk], ag_s.at[h, 4 + k], ag_r.at[h, mk], here)
 
     def ag_sib_in(h, k):
         mk = zother(k)
-        return rcopy(X.at[h, mk], X.at[h, mk], ag_s.at[h, 0], ag_r.at[h, mk], here)
+        return rcopy(X.at[h, mk], X.at[h, mk], ag_s.at[h, 4 + k], ag_r.at[h, mk], here)
 
     def res(h, k):
         g = ypeer(k)
@@ -163,18 +150,13 @@
 
     def ctx_in(k):
         g = ypeer(k)
-        return rcopy(C.at[g], C.at[g], ctx_s.at[0], ctx_r.at[g], here)
-
-    def ctx_relay():
-        g = ypeer(behind)
-        return rcopy(C.at[g], C.at[g], ctx_s.at[2], ctx_r.at[g], (ypeer(ahead), s, m))
+        return rcopy(C.at[g], C.at[g], ctx_s.at[k], ctx_r.at[g], (g, s, m))
 
     def part(h, zz):
         return rcopy(PS.at[h, zz], PR.at[h, zz], ps_s.at[h, zz], ps_r.at[h, zz], here)
 
-    def zred(h, i):
-        return rcopy(ZS.at[h, i], ZR.at[h, i], zz_s.at[h, i], zz_r.at[h, i],
-                     (d, s, zpeer(behind if i == 1 else ahead)))
+    def zred(h, k):
+        return rcopy(ZS.at[h, k], ZR.at[h, k], zz_s.at[h, k], zz_r.at[h, k], (d, s, zpeer(k)))
 
     def norm_block(h, g, mm, x):
         col = g * 2048 + mm * 256 + h * 128
@@ -186,17 +168,13 @@
 
         @pl.when(s == 0)
         def _():
-            EB.at[m][...] = emb[...]
-            eb_z(1).start()
-            eb_z(3).start()
-            eb_fwd("own").start()
-            eb_in("behind").wait_recv()
-            eb_relay().start()
-            eb_fwd("behind").start()
-            eb_in("ahead").wait_recv()
-            eb_fwd("ahead").start()
-            eb_in("far").wait_recv()
-            eb_fwd("far").start()
+            rows = jnp.concatenate([emb[0], emb[1]], axis=0).astype(F32)
+            EB.at[m][...] = jnp.concatenate([rows[:, :4096], rows[:, 4096:]], axis=0).astype(BF)
+            for k in (2, 1, 3, 0):
+                (eb_z(k) if k else eb_fwd(0)).start()
+            for k in (1, 3, 2):
+                eb_z_in(k).wait_recv()
+                eb_fwd(k).start()
             for k in range(4):
                 eb_sib_in(k).wait_recv()
 
@@ -224,21 +202,15 @@
             for h in range(2):
                 for g in range(NY):
                     hop_in(h, g).wait_recv()
-                ag_z(h, 1).start()
-                ag_z(h, 3).start()
-                ag_fwd(h, "own").start()
+                for k in (2, 1, 3, 0):
+                    (ag_z(h, k) if k else ag_fwd(h, 0)).start()
             for h in range(2):
-                ag_in(h, "behind").wait_recv()
-                ag_relay(h).start()
-                ag_fwd(h, "behind").start()
-            for h in range(2):
-                ag_in(h, "ahead").wait_recv()
-                ag_fwd(h, "ahead").start()
                 for k in (2, 1, 3):
                     res(h, k).start()
             for h in range(2):
-                ag_in(h, "far").wait_recv()
-                ag_fwd(h, "far").start()
+                for k in (1, 3, 2):
+                    ag_z_in(h, k).wait_recv()
+                    ag_fwd(h, k).start()
 
         QA[...] = jnp.zeros_like(QA)
         for h in range(2):
@@ -293,22 +265,20 @@
         mixed = jnp.dot(probs, value, preferred_element_type=F32).astype(BF)
         for j in range(4):
             C.at[d][:, j * HD:(j + 1) * HD] = mixed[j * ROWS:(j + 1) * ROWS]
-        ctx(1).start()
-        ctx(3).start()
+        for k in (2, 1, 3):
+            ctx(k).start()
+
         for h in range(2):
             R.at[h, d][...] = X[h, m, d]
         for copy in wo_loads:
             copy.wait()
-        ctx_in(behind).wait_recv()
-        ctx_relay().start()
-        ctx_in(ahead).wait_recv()
-        ctx_in(2).wait_recv()
+        for k in (1, 3, 2):
+            ctx_in(k).wait_recv()
 
         context = C[...].reshape(NY * ROWS, QW)
         for h in range(2):
             def project(i, _):
-                step = jnp.where(i == 0, 2, jnp.where(i == 1, behind, jnp.where(i == 2, ahead, 0)))
-                zz = (z + step) % NZ
+                zz = (z + jnp.where(i == 0, 2, jnp.where(i == 1, 1, jnp.where(i == 2, 3, 0)))) % NZ
                 p = jnp.dot(context, WO[h, :, lane(zz * 256, 256)], preferred_element_type=F32)
                 low, high = p[:, :128], p[:, 128:]
                 PO.at[h, zz][...] = jnp.where(c == 0, low, high)
@@ -324,23 +294,17 @@
             return PO[h, zt] + PR[h, zt].astype(F32)
 
         for h in range(2):
-            ZS.at[h, 0][...] = pair(h, 2).astype(BF)
-            zred(h, 0).start()
-            ZS.at[h, 1][...] = pair(h, behind).astype(BF)
-            zred(h, 1).start()
-        for h in range(2):
-            both = pair(h, ahead)
-            zred(h, 0).wait_recv()
-            ZS.at[h, 2][...] = (both + ZR[h, 0].astype(F32)).astype(BF)
-            zred(h, 2).start()
+            for k in (2, 1, 3):
+                ZS.at[h, k][...] = pair(h, k).astype(BF)
+                zred(h, k).start()
         for h in range(2):
             total = pair(h, 0)
             for k in (1, 3, 2):
                 res_in(h, k).wait_recv()
             total = total + R[h].astype(F32).reshape(NY * ROWS, 128)
-            for i in (1, 2):
-                zred(h, i).wait_recv()
-                total = total + ZR[h, i].astype(F32)
+            for k in (1, 3, 2):
+                zred(h, k).wait_recv()
+                total = total + ZR[h, k].astype(F32)
             HP.at[h][...] = total.astype(BF).reshape(NY, ROWS, 128)
 
             @pl.when(s < NX - 1)
@@ -439,6 +403,19 @@
         term = lax.dot_general(HEAD[cc, j], pieces, (((1,), (1,)), ((), ())),
                                preferred_element_type=F32)
         LT[...] = term if start else LT[...] + term
+
+    def row_slot(lanes):
+        return (lanes // 64) * 2 + (lanes // 4) % 2, ((lanes // 8) % 8) * 4 + lanes % 4
+
+    def wanted_rows():
+        slot, position = row_slot(lax.broadcasted_iota(jnp.int32, (32, 256), 1))
+        place = (position == lax.broadcasted_iota(jnp.int32, (32, 256), 0)).astype(BF)
+        tokens = targets[...]
+        top = jnp.dot((tokens // 256).astype(F32).astype(BF), place, preferred_element_type=F32)
+        low = jnp.dot((tokens % 256).astype(F32).astype(BF), place, preferred_element_type=F32)
+        every = top * 256.0 + low
+        keep = slot[0:8] == lax.broadcasted_iota(jnp.int32, (8, 256), 0)
+        return jnp.sum(jnp.where(keep, every, 0.0), axis=0, keepdims=True)
 
     def score(b):
         source = 2 * b + 1
@@ -508,8 +485,9 @@
         highest = jnp.max(logits, axis=0, keepdims=True)
         summed = jnp.sum(jnp.exp(logits - highest), axis=0, keepdims=True)
         vocab = HEAD.shape[2]
-        wanted = tgt[...] - ((d * NX + s) * NM + m) * vocab
-        index = lax.broadcasted_iota(jnp.int32, logits.shape, 0)
+        first = ((d * NX + s) * NM + m) * vocab
+        index = (lax.broadcasted_iota(jnp.int32, logits.shape, 0) + first).astype(F32)
+        wanted = wanted_rows()
         picked = jnp.sum(jnp.where(index == wanted, logits, 0.0), axis=0, keepdims=True)
         lanes = pl.ds(pl.multiple_of(b * 256, 256), 256)
         rows = lax.broadcasted_iota(jnp.int32, (8, 256), 0)
@@ -591,24 +569,47 @@
     for k in (1, 3, 2):
         st_x_in(k).wait_recv()
     highest, summed, picked = merge(SC, NX)
-    out[...] = jnp.broadcast_to(picked - (highest + jnp.log(summed)), out.shape)
+    logprob = picked - (highest + jnp.log(summed))
+    terms = []
+    for e in range(2):
+        rest = logprob[:, e * 256:e * 256 + 256]
+        for _ in range(3):
+            term = rest.astype(BF).astype(F32)
+            terms.append(term)
+            rest = rest - term
+    row = lax.broadcasted_iota(jnp.int32, (16, 256), 0)
+    stack = jnp.zeros((16, 256), F32)
+    for j, term in enumerate(terms):
+        stack = jnp.where(row == j, term, stack)
+    stack = stack.astype(BF)
+    slot, position = row_slot(lax.broadcasted_iota(jnp.int32, (256, 32), 0))
+    place = lax.broadcasted_iota(jnp.int32, (256, 32), 1)
+    results = []
+    for i in range(2):
+        chosen = source_of[2 * d + i]
+        take = ((slot == chosen) & (position == place)).astype(BF)
+        got = jnp.dot(stack, take, preferred_element_type=F32)
+        alive = lax.broadcasted_iota(jnp.int32, (1, 32), 1) < live[chosen]
+        results.append([jnp.where(alive, got[j:j + 1] + got[j + 1:j + 2] + got[j + 2:j + 3], 0.0)
+                        for j in (0, 3)])
+    for e, ref in enumerate((exit_out, final_out)):
+        first = lax.broadcasted_iota(jnp.int32, (2, 32), 0) == 0
+        ref[...] = jnp.where(first, results[0][e], results[1][e])
 
     @pl.when(s == 0)
     def _():
-        for k in (1, 3):
-            eb_z(k).wait_send()
-        eb_relay().wait_send()
-        for who in sends:
-            eb_fwd(who).wait_send()
+        for k in range(4):
+            (eb_z(k) if k else eb_fwd(0)).wait_send()
+        for k in range(1, 4):
+            eb_fwd(k).wait_send()
 
     @pl.when(s > 0)
     def _():
         for h in range(2):
-            for k in (1, 3):
+            for k in range(1, 4):
                 ag_z(h, k).wait_send()
-            ag_relay(h).wait_send()
-            for who in sends:
-                ag_fwd(h, who).wait_send()
+            for k in range(4):
+                ag_fwd(h, k).wait_send()
 
     @pl.when(s < NX - 1)
     def _():
@@ -619,14 +620,11 @@
     for h in range(2):
         for k in range(1, 4):
             res(h, k).wait_send()
-        for i in range(3):
-            zred(h, i).wait_send()
+            zred(h, k).wait_send()
         for zz in range(NZ):
             part(h, zz).wait_send()
-    for k in (1, 3):
+    for k in range(1, 4):
         ctx(k).wait_send()
-    ctx_relay().wait_send()
-    for k in range(1, 4):
         st_y(k).wait_send()
         st_x(k).wait_send()
     for k in range(1, 8):
@@ -667,20 +665,17 @@
 def per_device(
     embeds, targets, lengths, source, attn_gain, w_query, w_key, w_value, w_out, final_gain, head
 ):
-    d = lax.axis_index("dp")
     vocab = head.shape[0]
-    emb = embeds.reshape(8, 2, 4096).transpose(1, 0, 2).reshape(16, 4096)
-    tgt = targets.reshape(NY, 2, NM, 4).transpose(0, 2, 1, 3).reshape(1, NY * ROWS)
     cos, sin = tables()
     vmem = pl.BlockSpec(memory_space=pltpu.VMEM)
     hbm = pl.BlockSpec(memory_space=pl.ANY)
     smem = pl.BlockSpec(memory_space=pltpu.SMEM)
     dma = pltpu.SemaphoreType.DMA
-    stats = pl.pallas_call(
+    return pl.pallas_call(
         kernel,
-        out_shape=jax.ShapeDtypeStruct((8, 512), F32),
-        in_specs=[vmem, smem, vmem, vmem, vmem, vmem, vmem, hbm, hbm, hbm, hbm, hbm],
-        out_specs=vmem,
+        out_shape=[jax.ShapeDtypeStruct((2, 32), F32)] * 2,
+        in_specs=[vmem, smem, smem, vmem, vmem, vmem, vmem, vmem, hbm, hbm, hbm, hbm, hbm],
+        out_specs=[vmem, vmem],
         scratch_shapes=[
             pltpu.VMEM((2, 32, 128, 768), BF),
             pltpu.VMEM((2, QW, 1024), BF),
@@ -695,8 +690,8 @@
             pltpu.VMEM((2, NZ, NY * ROWS, 128), BF),
             pltpu.VMEM((2, NZ, NY * ROWS, 128), BF),
             pltpu.VMEM((2, NZ, NY * ROWS, 128), F32),
-            pltpu.VMEM((2, 3, NY * ROWS, 128), BF),
-            pltpu.VMEM((2, 3, NY * ROWS, 128), BF),
+            pltpu.VMEM((2, NZ, NY * ROWS, 128), BF),
+            pltpu.VMEM((2, NZ, NY * ROWS, 128), BF),
             pltpu.VMEM((2, NY, ROWS, 128), BF),
             pltpu.VMEM((2, 2, 4, 4, 272, 256), BF),
             pltpu.VMEM((vocab, 256), F32),
@@ -720,17 +715,10 @@
         cost_estimate=pl.CostEstimate(flops=8_000_000_000, bytes_accessed=24_000_000,
                                       transcendentals=300_000),
     )(
-        emb, lengths, tgt, attn_gain, final_gain.reshape(1, D), jnp.asarray(cos), jnp.asarray(sin),
+        embeds, lengths, source, targets, attn_gain, final_gain.reshape(1, D), jnp.asarray(cos), jnp.asarray(sin),
         w_query.reshape(32, 2, 128, 512), w_key.reshape(32, 2, 128, 128),
         w_value.reshape(32, 2, 128, 128), w_out.reshape(512, 2048), head,
     )
-    slots = stats[0].reshape(2, NY, NM, 2, 4).transpose(0, 1, 3, 2, 4).reshape(2, 8, 32)
-    chosen = lax.dynamic_slice_in_dim(source, d * 2, 2, 0)
-    live = jnp.take(lengths, chosen, axis=0)
-    picked = jnp.take(slots, chosen, axis=1)
-    valid = jnp.arange(32)[None, :] < live[:, None]
-    result = jnp.where(valid[None], picked, F32(0.0))
-    return (result[0], result[1])
 
 
 def solution(mesh):

time: 188 us -> 170 us (0.904)
  Pallas kernels: 180 us -> 167 us
  local copies, waits for them, and re-layouts: 5.99 us -> 2.44 us
    pallas_call x1, Pallas kernels: 180 us -> 167 us  [per_device(): pl.pallas_call(kernel, out_shape=[jax.ShapeDtypeStruct((2, 32), F32)] * 2...]
    reshape x6 -> x0, local copies, waits for them, and re-layouts: 3.3 us -> none  [the longest x2 1.77 us: per_device(): emb = embeds.reshape(8, 2, 4096).transpose(1, 0, 2).reshape(16, 4096)]
    unnamed x4 -> x2, local copies, waits for them, and re-layouts: 0.01 us -> 2.44 us
where the time goes in v4:
time: 170 us
  Pallas kernels  167 us (98%)
  local copies, waits for them, and re-layouts  2.44 us (1%)
    pallas_call x1, Pallas kernels, per_device(): pl.pallas_call(kernel, out_shape=[jax.ShapeDtypeStruct((2, 32), F32)] * 2...  167 us

profile of v4, /device:TPU:1, one launch (start us, length us, event | category | flops | bytes accessed | tf_op | source)
XLA Modules:
  0.0 170.0 jit_solution(10818663269055175555)
XLA Ops:
  0.6 166.9 %shard_map.140 = (f32[2,32]{1,0:T(2,128)}, f32[2,32]{1,0:T(2,128)}) custom-call(bf16[2,4,8192]{2,1,0:T(4,128)(2,1)} %emb.1, s32[8]{0:T(128)} %live.1, s32[8]{0:T(128)} %source_of.1, s32[8,32]{1,0:T(8,128)} %targets.1, f32[1,8192]{1,0:T(1,128)} %gain.1, f32[1,8192]{1,0:T(1,128)} %bitcast.9, f32[64,128]{1,0:T(8,128)} %constant.4.clone.cosine, ...), custom_call_target="tpu_custom_call" | custom-call | flops 8000000000 | bytes 24000000 | tf_op jit(solution)/shard_map/pallas_call | solution.py:674
  167.6 1.2 copy.17
  168.8 1.2 copy.18

commit v5 on v4

--- a/solution.py
+++ b/solution.py
@@ -28,8 +28,8 @@
 def kernel(
     emb, live, source_of, targets, gain, fgain, cosine, sine, wq, wk, wv, wo, head,
     exit_out, final_out,
-    W, WO, HEAD, EB, X, XN, SS, QA, R, C, PS, PR, PO, ZS, ZR, HP, Y, LT, STO, SA, SB, SC,
-    w_sem, eb_s, eb_r, hop_s, hop_r, ag_s, ag_r, res_s, res_r, ctx_s, ctx_r, ps_s, ps_r,
+    W, WO, HEAD, EB, X, G, NG, RX, MASK, SS, QA, R, C, PS, PR, PO, ZS, ZR, HP, SUMS, Y, LT, STO, SA, SB, SC,
+    w_sem, ng_s, ng_r, eb_s, eb_r, hop_s, hop_r, ag_s, ag_r, res_s, res_r, ctx_s, ctx_r, ps_s, ps_r,
     zz_s, zz_r, y_s, y_r, st_s, st_r,
 ):
     d = lax.axis_index("dp")
@@ -97,7 +97,23 @@
                                       HEAD.at[cc, j, :, i * 256:i * 256 + 256],
                                       w_sem.at[22]).start()
     head_load = pltpu.make_async_copy(HEAD, HEAD, w_sem.at[22])
+    shape = (4 * ROWS, ROWS)
+    rq = lax.broadcasted_iota(jnp.int32, shape, 0) % ROWS
+    rk = lax.broadcasted_iota(jnp.int32, shape, 1)
+    slot_q, slot_k = (rq // 4) % 2, (rk // 4) % 2
+    pos_q, pos_k = (rq // 8) * 4 + rq % 4, (rk // 8) * 4 + rk % 4
+    live_k = jnp.where(slot_k == 0, live[2 * d], live[2 * d + 1])
+    allowed = (slot_q == slot_k) & (pos_k <= pos_q) & (pos_k < live_k)
+    MASK[...] = jnp.where(allowed, F32(0.0), F32(-1e30))
     pl.semaphore_wait(barrier, len(partners))
+
+    def next_gain():
+        return rcopy(gain.at[:, lane(d * 2048 + m * 256, 256)], NG, ng_s, ng_r,
+                     (d, (s + 3) % NX, m))
+
+    @pl.when(s > 0)
+    def _():
+        next_gain().start()
 
     def eb_z(k):
         return rcopy(EB.at[m], EB.at[m], eb_s.at[k], eb_r.at[m], (d, s, zpeer(k)))
@@ -114,36 +130,44 @@
         mk = zother(k)
         return rcopy(EB.at[mk], EB.at[mk], eb_s.at[4 + k], eb_r.at[mk], here)
 
+    rows_of = (pl.ds(0, ROWS), pl.ds(0, ROWS + 16))
+
     def hop(h, g):
-        return rcopy(HP.at[h, g], X.at[h, m, d], hop_s.at[h, g], hop_r.at[h, d],
-                     (g, (s + 1) % NX, m))
+        return rcopy(G.at[h, g, rows_of[h]], X.at[h, m, d, rows_of[h]], hop_s.at[h, g],
+                     hop_r.at[h, d], (g, (s + 1) % NX, m))
 
     def hop_in(h, g):
-        return rcopy(HP.at[h, g], X.at[h, m, g], hop_s.at[h, g], hop_r.at[h, g],
-                     (g, (s + 1) % NX, m))
+        return rcopy(G.at[h, g, rows_of[h]], X.at[h, m, g, rows_of[h]], hop_s.at[h, g],
+                     hop_r.at[h, g], (g, (s + 1) % NX, m))
+
+    def hop_raw(h):
+        return rcopy(HP.at[h], R.at[h], hop_s.at[h, 4], hop_r.at[h, 4], (d, (s + 1) % NX, m))
+
+    def slab(h, mm):
+        return X.at[h, mm, :, rows_of[h]]
 
     def ag_z(h, k):
-        return rcopy(X.at[h, m], X.at[h, m], ag_s.at[h, k], ag_r.at[h, m], (d, s, zpeer(k)))
+        return rcopy(slab(h, m), slab(h, m), ag_s.at[h, k], ag_r.at[h, m], (d, s, zpeer(k)))
 
     def ag_z_in(h, k):
         mk = zpeer(k)
-        return rcopy(X.at[h, mk], X.at[h, mk], ag_s.at[h, k], ag_r.at[h, mk], (d, s, zpeer(k)))
+        return rcopy(slab(h, mk), slab(h, mk), ag_s.at[h, k], ag_r.at[h, mk], (d, s, zpeer(k)))
 
     def ag_fwd(h, k):
         mk = zpeer(k)
-        return rcopy(X.at[h, mk], X.at[h, mk], ag_s.at[h, 4 + k], ag_r.at[h, mk], here)
+        return rcopy(slab(h, mk), slab(h, mk), ag_s.at[h, 4 + k], ag_r.at[h, mk], here)
 
     def ag_sib_in(h, k):
         mk = zother(k)
-        return rcopy(X.at[h, mk], X.at[h, mk], ag_s.at[h, 4 + k], ag_r.at[h, mk], here)
+        return rcopy(slab(h, mk), slab(h, mk), ag_s.at[h, 4 + k], ag_r.at[h, mk], here)
 
     def res(h, k):
         g = ypeer(k)
-        return rcopy(X.at[h, m, g], R.at[h, d], res_s.at[h, k], res_r.at[h, d], (g, s, m))
+        return rcopy(RX.at[h, g], R.at[h, d], res_s.at[h, k], res_r.at[h, d], (g, s, m))
 
     def res_in(h, k):
         g = ypeer(k)
-        return rcopy(X.at[h, m, g], R.at[h, g], res_s.at[h, k], res_r.at[h, g], (g, s, m))
+        return rcopy(RX.at[h, g], R.at[h, g], res_s.at[h, k], res_r.at[h, g], (g, s, m))
 
     def ctx(k):
         return rcopy(C.at[d], C.at[d], ctx_s.at[k], ctx_r.at[d], (ypeer(k), s, m))
@@ -158,14 +182,7 @@
     def zred(h, k):
         return rcopy(ZS.at[h, k], ZR.at[h, k], zz_s.at[h, k], zz_r.at[h, k], (d, s, zpeer(k)))
 
-    def norm_block(h, g, mm, x):
-        col = g * 2048 + mm * 256 + h * 128
-        scaled = (x * gain[:, lane(col, 128)]).astype(BF)
-        XN.at[h, g][:, lane(mm * 128, 128)] = scaled
-
     def layer():
-        SS[...] = jnp.zeros_like(SS)
-
         @pl.when(s == 0)
         def _():
             rows = jnp.concatenate([emb[0], emb[1]], axis=0).astype(F32)
@@ -178,24 +195,32 @@
             for k in range(4):
                 eb_sib_in(k).wait_recv()
 
-            def body(i, _):
-                dl = i // 16
-                mm = (i // 2) % 8
-                h = i % 2
-                x = EB[:, :, lane(dl * 2048 + mm * 256 + h * 128, 128)]
-                xf = x.astype(F32)
-                for half in range(2):
-                    xs = xf[:, half * 8: half * 8 + 8, :].reshape(ROWS, 128)
-                    g = half * 2 + dl
-                    norm_block(h, g, mm, xs)
-                    X.at[h, mm, g][...] = xs.astype(BF)
-                    SS[...] += xs * xs
-                return 0
-
-            lax.fori_loop(0, 32, body, 0)
+            def block(dl, mm, h):
+                return EB[:, :, lane(dl * 2048 + mm * 256 + h * 128, 128)].astype(F32)
+
+            def body(mm, total):
+                for dl in range(2):
+                    for h in range(2):
+                        xf = block(dl, mm, h)
+                        for half in range(2):
+                            xs = xf[:, half * 8: half * 8 + 8, :].reshape(ROWS, 128)
+                            g = half * 2 + dl
+                            cols = lane(g * 2048 + mm * 256 + h * 128, 128)
+                            X.at[h, mm, g][0:ROWS, :] = (xs * gain[:, cols]).astype(BF)
+                            total = total + xs * xs
+                return total
+
+            SS[...] = lax.fori_loop(0, NM, body, jnp.zeros((ROWS, 128), F32))
+            for dl in range(2):
+                for h in range(2):
+                    xf = block(dl, m, h)
+                    for half in range(2):
+                        xs = xf[:, half * 8: half * 8 + 8, :].reshape(ROWS, 128)
+                        RX.at[h, half * 2 + dl][...] = xs.astype(BF)
             for h in range(2):
                 for k in (2, 1, 3):
                     res(h, k).start()
+                R.at[h, d][...] = RX[h, d]
 
         @pl.when(s > 0)
         def _():
@@ -205,38 +230,41 @@
                 for k in (2, 1, 3, 0):
                     (ag_z(h, k) if k else ag_fwd(h, 0)).start()
             for h in range(2):
-                for k in (2, 1, 3):
-                    res(h, k).start()
-            for h in range(2):
                 for k in (1, 3, 2):
                     ag_z_in(h, k).wait_recv()
                     ag_fwd(h, k).start()
 
-        QA[...] = jnp.zeros_like(QA)
+        def multiply(h, who, start):
+            term = None
+            for g in range(NY):
+                x = jnp.concatenate([X[h, 2 * zz + who, g, 0:ROWS] for zz in range(NZ)], axis=1)
+                w = jnp.concatenate([W[h, g * 8 + 2 * zz + who] for zz in range(NZ)], axis=0)
+                one = jnp.dot(x, w, preferred_element_type=F32)
+                term = one if term is None else term + one
+            QA[...] = term if start else QA[...] + term
+
         for h in range(2):
+            for copy in loads[h]:
+                copy.wait()
+            multiply(h, c, h == 0)
+
             @pl.when(s > 0)
             def _():
                 for k in range(4):
                     ag_sib_in(h, k).wait_recv()
 
-                def body(mm, _):
-                    for g in range(NY):
-                        xf = X[h, mm, g].astype(F32)
-                        norm_block(h, g, mm, xf)
-                        SS[...] += xf * xf
-                    return 0
-
-                lax.fori_loop(0, NM, body, 0)
-
-            for copy in loads[h]:
-                copy.wait()
-
-            def dots(g, _):
-                w = W[h, pl.ds(g * 8, 8)].reshape(1024, 768)
-                QA[...] += jnp.dot(XN[h, g], w, preferred_element_type=F32)
-                return 0
-
-            lax.fori_loop(0, NY, dots, 0)
+            multiply(h, 1 - c, False)
+
+        @pl.when(s > 0)
+        def _():
+            total = jnp.zeros((16, 128), F32)
+            for mm in range(NM):
+                for g in range(NY):
+                    total = total + X[1, mm, g, ROWS:ROWS + 16].astype(F32)
+            total = total[0:1] + total[1:2]
+            mine = (lax.broadcasted_iota(jnp.int32, (ROWS, 128), 1)
+                    == lax.broadcasted_iota(jnp.int32, (ROWS, 128), 0) + (d % 2) * ROWS)
+            SS[...] = jnp.where(mine, total, 0.0)
 
         r = lax.rsqrt(jnp.sum(SS[...], axis=1, keepdims=True) * (1.0 / D) + EPS)
         cos = cosine[...]
@@ -251,14 +279,7 @@
         value = (QA[:, 640:768] * r).astype(BF)
         scores = lax.dot_general(query, key, (((1,), (1,)), ((), ())),
                                  preferred_element_type=F32) * (HD ** -0.5)
-        shape = (4 * ROWS, ROWS)
-        rq = lax.broadcasted_iota(jnp.int32, shape, 0) % ROWS
-        rk = lax.broadcasted_iota(jnp.int32, shape, 1)
-        slot_q, slot_k = (rq // 4) % 2, (rk // 4) % 2
-        pos_q, pos_k = (rq // 8) * 4 + rq % 4, (rk // 8) * 4 + rk % 4
-        live_k = jnp.where(slot_k == 0, live[2 * d], live[2 * d + 1])
-        allowed = (slot_q == slot_k) & (pos_k <= pos_q) & (pos_k < live_k)
-        scores = jnp.where(allowed, scores, F32(-1e30))
+        scores = scores + MASK[...]
         highest = jnp.max(scores, axis=-1, keepdims=True)
         weights = jnp.exp(scores - highest)
         probs = (weights / jnp.sum(weights, axis=-1, keepdims=True)).astype(BF)
@@ -268,8 +289,6 @@
         for k in (2, 1, 3):
             ctx(k).start()
 
-        for h in range(2):
-            R.at[h, d][...] = X[h, m, d]
         for copy in wo_loads:
             copy.wait()
         for k in (1, 3, 2):
@@ -277,16 +296,13 @@
 
         context = C[...].reshape(NY * ROWS, QW)
         for h in range(2):
-            def project(i, _):
-                zz = (z + jnp.where(i == 0, 2, jnp.where(i == 1, 1, jnp.where(i == 2, 3, 0)))) % NZ
+            for k in (2, 1, 3, 0):
+                zz = (z + k) % NZ
                 p = jnp.dot(context, WO[h, :, lane(zz * 256, 256)], preferred_element_type=F32)
                 low, high = p[:, :128], p[:, 128:]
                 PO.at[h, zz][...] = jnp.where(c == 0, low, high)
                 PS.at[h, zz][...] = jnp.where(c == 0, high, low).astype(BF)
                 part(h, zz).start()
-                return 0
-
-            lax.fori_loop(0, NZ, project, 0)
 
         def pair(h, k):
             zt = (z + k) % NZ
@@ -297,43 +313,70 @@
             for k in (2, 1, 3):
                 ZS.at[h, k][...] = pair(h, k).astype(BF)
                 zred(h, k).start()
+        @pl.when(s == 0)
+        def _():
+            for h in range(2):
+                for k in (1, 3, 2):
+                    res_in(h, k).wait_recv()
+
+        @pl.when(s > 0)
+        def _():
+            for h in range(2):
+                hop_raw(h).wait_recv()
+
+        @pl.when(s < NX - 1)
+        def _():
+            next_gain().wait_recv()
+
+        sums = jnp.zeros((16, NY * ROWS), F32)
         for h in range(2):
             total = pair(h, 0)
-            for k in (1, 3, 2):
-                res_in(h, k).wait_recv()
             total = total + R[h].astype(F32).reshape(NY * ROWS, 128)
             for k in (1, 3, 2):
                 zred(h, k).wait_recv()
                 total = total + ZR[h, k].astype(F32)
-            HP.at[h][...] = total.astype(BF).reshape(NY, ROWS, 128)
+            hidden = total.astype(BF)
+            HP.at[h][...] = hidden.reshape(NY, ROWS, 128)
+            wide = hidden.astype(F32)
+            scaled = (wide * NG[:, h * 128:h * 128 + 128]).astype(BF)
+            G.at[h][:, 0:ROWS, :] = scaled.reshape(NY, ROWS, 128)
+            square = wide * wide
+            top = square.astype(BF)
+            rest = (square - top.astype(F32)).astype(BF)
+            ones = jnp.ones((16, 128), BF)
+            nt = (((1,), (1,)), ((), ()))
+            sums = sums + lax.dot_general(ones, top, nt, preferred_element_type=F32)
+            sums = sums + lax.dot_general(ones, rest, nt, preferred_element_type=F32)
+            if h == 1:
+                top = sums.astype(BF).astype(F32)
+                row = lax.broadcasted_iota(jnp.int32, (16, NY * ROWS), 0)
+                packed = jnp.where(row == 0, top, jnp.where(row == 1, sums - top, 0.0)).astype(BF)
+                for g in range(NY):
+                    tile = g // 2 * 128
+                    G.at[1, g][ROWS:ROWS + 16, :] = packed[:, tile:tile + 128]
+                SUMS[...] = packed
 
             @pl.when(s < NX - 1)
             def _():
                 for k in (2, 1, 3, 0):
                     hop(h, ypeer(k)).start()
 
+        @pl.when(s < NX - 1)
+        def _():
+            for h in range(2):
+                hop_raw(h).start()
+
         @pl.when(s % 2 == 1)
         def _():
             emit(s // 2)
 
     def emit(b):
-        nt = (((1,), (1,)), ((), ()))
-        ones = jnp.ones((16, 128), BF)
-        sums = jnp.zeros((16, NY * ROWS), F32)
         mine = Y.at[b, c, 0, 0]
         for h in range(2):
             wide = HP[h].astype(F32).reshape(NY * ROWS, 128)
-            square = wide * wide
-            top = square.astype(BF)
-            rest = (square - top.astype(F32)).astype(BF)
-            sums = sums + lax.dot_general(ones, top, nt, preferred_element_type=F32)
-            sums = sums + lax.dot_general(ones, rest, nt, preferred_element_type=F32)
             cols = lane(d * 2048 + m * 256 + h * 128, 128)
             mine[0:256, h * 128:h * 128 + 128] = (wide * fgain[:, cols]).astype(BF)
-        top = sums.astype(BF).astype(F32)
-        row = lax.broadcasted_iota(jnp.int32, (16, NY * ROWS), 0)
-        packed = jnp.where(row == 0, top, jnp.where(row == 1, sums - top, 0.0))
-        mine[256:272, :] = packed.astype(BF)
+        mine[256:272, :] = SUMS[...]
         y_x(b, 1).start()
         y_x(b, 3).start()
         spread_own(b)
@@ -616,10 +659,20 @@
         for h in range(2):
             for k in range(4):
                 hop(h, ypeer(k)).wait_send()
+            hop_raw(h).wait_send()
+
+    @pl.when(s == 0)
+    def _():
+        for h in range(2):
+            for k in range(1, 4):
+                res(h, k).wait_send()
+
+    @pl.when(s > 0)
+    def _():
+        next_gain().wait_send()
 
     for h in range(2):
         for k in range(1, 4):
-            res(h, k).wait_send()
             zred(h, k).wait_send()
         for zz in range(NZ):
             part(h, zz).wait_send()
@@ -681,8 +734,11 @@
             pltpu.VMEM((2, QW, 1024), BF),
             pltpu.VMEM((2, 4, vocab, 1024), BF),
             pltpu.VMEM((NM, 16, 4096), BF),
-            pltpu.VMEM((2, NM, NY, ROWS, 128), BF),
-            pltpu.VMEM((2, NY, ROWS, 1024), BF),
+            pltpu.VMEM((2, NM, NY, ROWS + 16, 128), BF),
+            pltpu.VMEM((2, NY, ROWS + 16, 128), BF),
+            pltpu.VMEM((1, 256), F32),
+            pltpu.VMEM((2, NY, ROWS, 128), BF),
+            pltpu.VMEM((4 * ROWS, ROWS), F32),
             pltpu.VMEM((ROWS, 128), F32),
             pltpu.VMEM((ROWS, 768), F32),
             pltpu.VMEM((2, NY, ROWS, 128), BF),
@@ -693,6 +749,7 @@
             pltpu.VMEM((2, NZ, NY * ROWS, 128), BF),
             pltpu.VMEM((2, NZ, NY * ROWS, 128), BF),
             pltpu.VMEM((2, NY, ROWS, 128), BF),
+            pltpu.VMEM((16, NY * ROWS), BF),
             pltpu.VMEM((2, 2, 4, 4, 272, 256), BF),
             pltpu.VMEM((vocab, 256), F32),
             pltpu.VMEM((8, 512), F32),
@@ -700,8 +757,9 @@
             pltpu.VMEM((NM, 8, 512), F32),
             pltpu.VMEM((NX, 8, 512), F32),
             dma((23,)),
+            dma, dma,
             dma((8,)), dma((8,)),
-            dma((2, 4)), dma((2, 4)),
+            dma((2, 5)), dma((2, 5)),
             dma((2, 8)), dma((2, 8)),
             dma((2, 4)), dma((2, 4)),
             dma((4,)), dma((4,)),

time: 170 us -> 167 us (0.982)
  Pallas kernels: 167 us -> 164 us
    pallas_call x1, Pallas kernels: 167 us -> 164 us  [per_device(): pl.pallas_call(kernel, out_shape=[jax.ShapeDtypeStruct((2, 32), F32)] * 2...]
where the time goes in v5:
time: 167 us
  Pallas kernels  164 us (98%)
  local copies, waits for them, and re-layouts  2.44 us (1%)
    pallas_call x1, Pallas kernels, per_device(): pl.pallas_call(kernel, out_shape=[jax.ShapeDtypeStruct((2, 32), F32)] * 2...  164 us

profile of v5, /device:TPU:1, one launch (start us, length us, event | category | flops | bytes accessed | tf_op | source)
XLA Modules:
  0.0 167.0 jit_solution(15730857921081201898)
XLA Ops:
  0.6 163.9 %shard_map.140 = (f32[2,32]{1,0:T(2,128)}, f32[2,32]{1,0:T(2,128)}) custom-call(bf16[2,4,8192]{2,1,0:T(4,128)(2,1)} %emb.1, s32[8]{0:T(128)} %live.1, s32[8]{0:T(128)} %source_of.1, s32[8,32]{1,0:T(8,128)} %targets.1, f32[1,8192]{1,0:T(1,128)} %gain.1, f32[1,8192]{1,0:T(1,128)} %bitcast.9, f32[64,128]{1,0:T(8,128)} %constant.4.clone.cosine, ...), custom_call_target="tpu_custom_call" | custom-call | flops 8000000000 | bytes 24000000 | tf_op jit(solution)/shard_map/pallas_call | solution.py:727
  164.6 1.2 copy.17
  165.8 1.2 copy.18

commit v6 on v5

--- a/solution.py
+++ b/solution.py
@@ -14,6 +14,8 @@
 NZ = 4
 NM = 8
 ROWS = 64
+LIVE = 192
+PIECE = LIVE + 16
 D = 8192
 QW = 512
 MESH = pl.DeviceIdType.MESH
@@ -27,8 +29,8 @@
 
 def kernel(
     emb, live, source_of, targets, gain, fgain, cosine, sine, wq, wk, wv, wo, head,
-    exit_out, final_out,
-    W, WO, HEAD, EB, X, G, NG, RX, MASK, SS, QA, R, C, PS, PR, PO, ZS, ZR, HP, SUMS, Y, LT, STO, SA, SB, SC,
+    out,
+    W, WO, HEAD, EB, X, G, NG, RX, MASK, SEL, SS, QA, R, C, PS, PR, PO, ZS, ZR, HP, SUMS, Y, LT, STO, SA, SB, SC,
     w_sem, ng_s, ng_r, eb_s, eb_r, hop_s, hop_r, ag_s, ag_r, res_s, res_r, ctx_s, ctx_r, ps_s, ps_r,
     zz_s, zz_r, y_s, y_r, st_s, st_r,
 ):
@@ -105,6 +107,25 @@
     live_k = jnp.where(slot_k == 0, live[2 * d], live[2 * d + 1])
     allowed = (slot_q == slot_k) & (pos_k <= pos_q) & (pos_k < live_k)
     MASK[...] = jnp.where(allowed, F32(0.0), F32(-1e30))
+
+    def row_slot(lanes):
+        return (lanes // 64) * 2 + (lanes // 4) % 2, ((lanes // 8) % 8) * 4 + lanes % 4
+
+    def first_row(slot):
+        start = jnp.zeros_like(slot)
+        for other in range(8):
+            start = start + jnp.where(slot > other, live[other], 0)
+        return start
+
+    def live_of(slot):
+        count = jnp.zeros_like(slot)
+        for other in range(8):
+            count = count + jnp.where(slot == other, live[other], 0)
+        return count
+
+    slot, position = row_slot(lax.broadcasted_iota(jnp.int32, (8, 256), 1))
+    packed_at = jnp.where(position < live_of(slot), first_row(slot) + position, 999)[0:1]
+    SEL[...] = (lax.broadcasted_iota(jnp.int32, (256, 256), 0) == packed_at).astype(F32).astype(BF)
     pl.semaphore_wait(barrier, len(partners))
 
     def next_gain():
@@ -372,13 +393,18 @@
 
     def emit(b):
         mine = Y.at[b, c, 0, 0]
+        nt = (((1,), (1,)), ((), ()))
         for h in range(2):
             wide = HP[h].astype(F32).reshape(NY * ROWS, 128)
             cols = lane(d * 2048 + m * 256 + h * 128, 128)
-            mine[0:256, h * 128:h * 128 + 128] = (wide * fgain[:, cols]).astype(BF)
-        mine[256:272, :] = SUMS[...]
-        y_x(b, 1).start()
-        y_x(b, 3).start()
+            scaled = (wide * fgain[:, cols]).astype(BF)
+            live_rows = jnp.dot(SEL[0:LIVE], scaled, preferred_element_type=F32)
+            mine[0:LIVE, h * 128:h * 128 + 128] = live_rows.astype(BF)
+        squares = lax.dot_general(SUMS[...], SEL[...], nt, preferred_element_type=F32)
+        mine[LIVE:PIECE, :] = squares.astype(BF)
+        for half in range(2):
+            y_x(b, half, 1).start()
+            y_x(b, 1 - half, 3).start()
         spread_own(b)
 
     def first_dev(k):
@@ -390,22 +416,27 @@
     def ycopy(src, dst, b, i, j, dev):
         return rcopy(src, dst, y_s.at[b, i], y_r.at[b, j], dev)
 
-    def y_x(b, k):
-        ref = Y.at[b, c, 0, 0]
-        return ycopy(ref, ref, b, k, 0, (d, (s + k) % NX, m))
-
-    cut = (pl.ds(0, 144), pl.ds(144, 128))
+    cut = (pl.ds(0, 96), pl.ds(96, PIECE - 96))
+
+    def own(b, rows):
+        return Y.at[b, c, 0, 0, rows]
+
+    def y_x(b, half, k):
+        ref = own(b, cut[half])
+        return ycopy(ref, ref, b, k + half, (0, 21)[half], (d, (s + k) % NX, m))
 
     def y_x_relay(b, half):
-        ref = Y.at[b, c, 0, 0, cut[half]]
-        return ycopy(ref, ref, b, 4 + half, 0, (d, jnp.where(b == 0, 3, 1), m))
+        ref = own(b, cut[half])
+        return ycopy(ref, ref, b, 28 + half, (0, 21)[half], (d, jnp.where(b == 0, 3, 1), m))
 
     def relays_x(b, half):
         return (s == 0) if half == 0 else (s == jnp.where(b == 0, 0, 2))
 
+    whole = pl.ds(0, PIECE)
+
     def y_first(b, k):
         slot = 1 if k == 1 else 2
-        return ycopy(Y.at[b, c, 0, 0], Y.at[b, c, 0, slot], b, 5 + k, slot, first_dev(k))
+        return ycopy(own(b, whole), Y.at[b, c, 0, slot, whole], b, 5 + k, slot, first_dev(k))
 
     def y_first_relay(b, half):
         slot, k = ((1, 1), (2, 3))[half]
@@ -413,25 +444,26 @@
                      b, 9 + half, 3, first_dev(k))
 
     def y_opposite(b):
-        ref = Y.at[b, c, 0, 3]
+        ref = Y.at[b, c, 0, 3, whole]
         return ycopy(ref, ref, b, 9, 3, here)
 
     sets = (pl.ds(0, 1), pl.ds(1, 2), pl.ds(3, 1))
 
     def y_second(b, part_no, k):
         slot = 1 if k == 1 else 2
-        return ycopy(Y.at[b, c, 0, sets[part_no]], Y.at[b, c, slot, sets[part_no]],
+        return ycopy(Y.at[b, c, 0, sets[part_no], whole], Y.at[b, c, slot, sets[part_no], whole],
                      b, 11 + part_no * 2 + (slot - 1), 1 + 3 * slot + part_no, second_dev(k))
 
     def y_second_relay(b, i):
         slot, k = (1, 1) if i < 2 else (2, 3)
-        return ycopy(Y.at[b, c, slot, i], Y.at[b, c, 3, i], b, 17 + i, 10 + i, second_dev(k))
+        return ycopy(Y.at[b, c, slot, i, whole], Y.at[b, c, 3, i, whole],
+                     b, 17 + i, 10 + i, second_dev(k))
 
     forwards = ((0, 0, 1), (0, 1, 2), (0, 3, 1), (1, 0, 4), (2, 0, 4), (3, 0, 2), (3, 2, 2))
 
     def y_fwd(b, n, who):
         j, i, size = forwards[n]
-        ref = Y.at[b, who, j, pl.ds(i, size)]
+        ref = Y.at[b, who, j, pl.ds(i, size), whole]
         return ycopy(ref, ref, b, 21 + n, 14 + n, here)
 
     def spread_own(b):
@@ -447,29 +479,42 @@
                                preferred_element_type=F32)
         LT[...] = term if start else LT[...] + term
 
-    def row_slot(lanes):
-        return (lanes // 64) * 2 + (lanes // 4) % 2, ((lanes // 8) % 8) * 4 + lanes % 4
-
     def wanted_rows():
         slot, position = row_slot(lax.broadcasted_iota(jnp.int32, (32, 256), 1))
         place = (position == lax.broadcasted_iota(jnp.int32, (32, 256), 0)).astype(BF)
         tokens = targets[...]
-        top = jnp.dot((tokens // 256).astype(F32).astype(BF), place, preferred_element_type=F32)
-        low = jnp.dot((tokens % 256).astype(F32).astype(BF), place, preferred_element_type=F32)
-        every = top * 256.0 + low
+        nt = (((1,), (1,)), ((), ()))
         keep = slot[0:8] == lax.broadcasted_iota(jnp.int32, (8, 256), 0)
-        return jnp.sum(jnp.where(keep, every, 0.0), axis=0, keepdims=True)
-
-    def score(b):
+        parts = []
+        for term in (tokens // 256, tokens % 256):
+            every = jnp.dot(term.astype(F32).astype(BF), place, preferred_element_type=F32)
+            mine = jnp.sum(jnp.where(keep, every, 0.0), axis=0, keepdims=True)
+            spread = jnp.broadcast_to(mine, (16, 256)).astype(BF)
+            parts.append(lax.dot_general(spread, SEL[...], nt, preferred_element_type=F32)[0:1])
+        return parts[0] * 256.0 + parts[1]
+
+    def gather(b):
         source = 2 * b + 1
 
         @pl.when(s != source)
         def _():
-            y_x(b, 1).wait_recv()
-            for half in range(2):
+            def take(half):
+                y_x(b, half, 1).wait_recv()
+
                 @pl.when(relays_x(b, half))
                 def _():
                     y_x_relay(b, half).start()
+
+            @pl.when(s == 2)
+            def _():
+                take(1)
+                take(0)
+
+            @pl.when(s != 2)
+            def _():
+                take(0)
+                take(1)
+
             spread_own(b)
 
         y_first(b, 1).wait_recv()
@@ -496,6 +541,7 @@
         y_second(b, 2, 1).wait_recv()
         y_fwd(b, 3, c).start()
 
+    def finish(b):
         dots(b, c, 0, True)
         for n in range(3):
             y_fwd(b, n, 1 - c).wait_recv()
@@ -521,7 +567,7 @@
         for cc in range(2):
             for j in range(4):
                 for i in range(4):
-                    extra = extra + Y[b, cc, j, i, 256:272, :].astype(F32)
+                    extra = extra + Y[b, cc, j, i, LIVE:PIECE, :].astype(F32)
         sums = jnp.sum(extra, axis=0, keepdims=True)
         r = lax.rsqrt(sums * (1.0 / D) + EPS)
         logits = LT[...] * r
@@ -532,45 +578,49 @@
         index = (lax.broadcasted_iota(jnp.int32, logits.shape, 0) + first).astype(F32)
         wanted = wanted_rows()
         picked = jnp.sum(jnp.where(index == wanted, logits, 0.0), axis=0, keepdims=True)
-        lanes = pl.ds(pl.multiple_of(b * 256, 256), 256)
-        rows = lax.broadcasted_iota(jnp.int32, (8, 256), 0)
-        STO[:, lanes] = jnp.where(rows == 0, highest,
-                                  jnp.where(rows == 1, summed,
-                                            jnp.where(rows == 2, picked, 0.0)))
+        alive = lax.broadcasted_iota(jnp.int32, (1, 256), 1) < LIVE
+        for n, value in enumerate((highest, summed, picked)):
+            value = jnp.where(alive, value, 1.0)
+            for half in range(2):
+                STO[pl.ds(n * 4 + b * 2 + half, 1), :] = value[:, half * 128:half * 128 + 128]
 
     def step(t, _):
-        place = jnp.where(s == NX - 1, 1, 0)
+        last = s == NX - 1
+        place = jnp.where(last, 1, 0)
 
         @pl.when(t == place)
         def _():
             layer()
 
-        @pl.when(t != place)
-        def _():
-            @pl.when((t == 0) | ((t == 1) & (s != NX - 1)))
+        @pl.when(jnp.where(last, (t == 0) | (t == 2), (t == 1) | (t == 3)))
+        def _():
+            gather(jnp.where(t < 2, 0, 1))
+
+        @pl.when(jnp.where(last, t >= 3, (t == 2) | (t == 4)))
+        def _():
+            @pl.when(t == jnp.where(last, 3, 2))
             def _():
                 head_load.wait()
-            score(jnp.where(t == 2, 1, 0))
+            finish(jnp.where(t == 4, 1, 0))
         return 0
 
-    lax.fori_loop(0, 3, step, 0)
+    STO[...] = jnp.zeros_like(STO)
+    lax.fori_loop(0, 5, step, 0)
 
     def merge(ref, count):
         parts = [ref[j] for j in range(count)]
-        highest = parts[0][0:1]
+        highest = parts[0][0:4]
         for p in parts[1:]:
-            highest = jnp.maximum(highest, p[0:1])
+            highest = jnp.maximum(highest, p[0:4])
         summed = jnp.zeros_like(highest)
         picked = jnp.zeros_like(highest)
         for p in parts:
-            summed = summed + p[1:2] * jnp.exp(p[0:1] - highest)
-            picked = picked + p[2:3]
+            summed = summed + p[4:8] * jnp.exp(p[0:4] - highest)
+            picked = picked + p[8:12]
         return highest, summed, picked
 
     def stacked(highest, summed, picked):
-        rows = lax.broadcasted_iota(jnp.int32, (8, 512), 0)
-        return jnp.where(rows == 0, highest,
-                         jnp.where(rows == 1, summed, jnp.where(rows == 2, picked, 0.0)))
+        return jnp.concatenate([highest, summed, picked, jnp.zeros_like(picked)], axis=0)
 
     def st_y(k):
         return rcopy(SA.at[d], SA.at[d], st_s.at[0, k], st_r.at[0, d], (ypeer(k), s, m))
@@ -615,7 +665,7 @@
     logprob = picked - (highest + jnp.log(summed))
     terms = []
     for e in range(2):
-        rest = logprob[:, e * 256:e * 256 + 256]
+        rest = jnp.concatenate([logprob[2 * e:2 * e + 1], logprob[2 * e + 1:2 * e + 2]], axis=1)
         for _ in range(3):
             term = rest.astype(BF).astype(F32)
             terms.append(term)
@@ -625,19 +675,20 @@
     for j, term in enumerate(terms):
         stack = jnp.where(row == j, term, stack)
     stack = stack.astype(BF)
-    slot, position = row_slot(lax.broadcasted_iota(jnp.int32, (256, 32), 0))
+    index = lax.broadcasted_iota(jnp.int32, (256, 32), 0)
     place = lax.broadcasted_iota(jnp.int32, (256, 32), 1)
     results = []
     for i in range(2):
         chosen = source_of[2 * d + i]
-        take = ((slot == chosen) & (position == place)).astype(BF)
+        start = 0
+        for other in range(8):
+            start = start + jnp.where(chosen > other, live[other], 0)
+        take = ((index == start + place) & (place < live[chosen])).astype(F32).astype(BF)
         got = jnp.dot(stack, take, preferred_element_type=F32)
-        alive = lax.broadcasted_iota(jnp.int32, (1, 32), 1) < live[chosen]
-        results.append([jnp.where(alive, got[j:j + 1] + got[j + 1:j + 2] + got[j + 2:j + 3], 0.0)
-                        for j in (0, 3)])
-    for e, ref in enumerate((exit_out, final_out)):
+        results.append([got[j:j + 1] + got[j + 1:j + 2] + got[j + 2:j + 3] for j in (0, 3)])
+    for e in range(2):
         first = lax.broadcasted_iota(jnp.int32, (2, 32), 0) == 0
-        ref[...] = jnp.where(first, results[0][e], results[1][e])
+        out.at[e][...] = jnp.where(first, results[0][e], results[1][e])
 
     @pl.when(s == 0)
     def _():
@@ -685,8 +736,9 @@
     for b in range(2):
         @pl.when(s == 2 * b + 1)
         def _():
-            for k in (1, 3):
-                y_x(b, k).wait_send()
+            for half in range(2):
+                for k in (1, 3):
+                    y_x(b, half, k).wait_send()
 
         for half in range(2):
             @pl.when((s != 2 * b + 1) & relays_x(b, half))
@@ -724,11 +776,11 @@
     hbm = pl.BlockSpec(memory_space=pl.ANY)
     smem = pl.BlockSpec(memory_space=pltpu.SMEM)
     dma = pltpu.SemaphoreType.DMA
-    return pl.pallas_call(
+    stats = pl.pallas_call(
         kernel,
-        out_shape=[jax.ShapeDtypeStruct((2, 32), F32)] * 2,
+        out_shape=jax.ShapeDtypeStruct((2, 2, 32), F32),
         in_specs=[vmem, smem, smem, vmem, vmem, vmem, vmem, vmem, hbm, hbm, hbm, hbm, hbm],
-        out_specs=[vmem, vmem],
+        out_specs=vmem,
         scratch_shapes=[
             pltpu.VMEM((2, 32, 128, 768), BF),
             pltpu.VMEM((2, QW, 1024), BF),
@@ -739,6 +791,7 @@
             pltpu.VMEM((1, 256), F32),
             pltpu.VMEM((2, NY, ROWS, 128), BF),
             pltpu.VMEM((4 * ROWS, ROWS), F32),
+            pltpu.VMEM((256, 256), BF),
             pltpu.VMEM((ROWS, 128), F32),
             pltpu.VMEM((ROWS, 768), F32),
             pltpu.VMEM((2, NY, ROWS, 128), BF),
@@ -750,12 +803,12 @@
             pltpu.VMEM((2, NZ, NY * ROWS, 128), BF),
             pltpu.VMEM((2, NY, ROWS, 128), BF),
             pltpu.VMEM((16, NY * ROWS), BF),
-            pltpu.VMEM((2, 2, 4, 4, 272, 256), BF),
+            pltpu.VMEM((2, 2, 4, 4, 256, 256), BF),
             pltpu.VMEM((vocab, 256), F32),
-            pltpu.VMEM((8, 512), F32),
-            pltpu.VMEM((NY, 8, 512), F32),
-            pltpu.VMEM((NM, 8, 512), F32),
-            pltpu.VMEM((NX, 8, 512), F32),
+            pltpu.VMEM((16, 128), F32),
+            pltpu.VMEM((NY, 16, 128), F32),
+            pltpu.VMEM((NM, 16, 128), F32),
+            pltpu.VMEM((NX, 16, 128), F32),
             dma((23,)),
             dma, dma,
             dma((8,)), dma((8,)),
@@ -765,7 +818,7 @@
             dma((4,)), dma((4,)),
             dma((2, 4)), dma((2, 4)),
             dma((2, 4)), dma((2, 4)),
-            dma((2, 28)), dma((2, 21)),
+            dma((2, 30)), dma((2, 22)),
             dma((3, 8)), dma((3, 8)),
         ],
         compiler_params=pltpu.CompilerParams(
@@ -777,6 +830,7 @@
         w_query.reshape(32, 2, 128, 512), w_key.reshape(32, 2, 128, 128),
         w_value.reshape(32, 2, 128, 128), w_out.reshape(512, 2048), head,
     )
+    return (stats[0], stats[1])
 
 
 def solution(mesh):

time: 167 us -> 163 us (0.976)
  Pallas kernels: 164 us -> 161 us
    pallas_call x1, Pallas kernels: 164 us -> 161 us  [per_device(): pl.pallas_call(kernel, out_shape=jax.ShapeDtypeStruct((2, 2, 32), F32), i...]
    unnamed x2 -> x0, local copies, waits for them, and re-layouts: 2.44 us -> none
where the time goes in v6:
time: 163 us
  Pallas kernels  161 us (99%)
    pallas_call x1, Pallas kernels, per_device(): pl.pallas_call(kernel, out_shape=jax.ShapeDtypeStruct((2, 2, 32), F32), i...  161 us

profile of v6, /device:TPU:1, one launch (start us, length us, event | category | flops | bytes accessed | tf_op | source)
XLA Modules:
  0.0 163.2 jit_solution(18329233600195620314)
XLA Ops:
  0.6 161.3 %shard_map.140 = f32[2,2,32]{2,1,0:T(2,128)} custom-call(bf16[2,4,8192]{2,1,0:T(4,128)(2,1)} %emb.1, s32[8]{0:T(128)} %live.1, s32[8]{0:T(128)} %source_of.1, s32[8,32]{1,0:T(8,128)} %targets.1, f32[1,8192]{1,0:T(1,128)} %gain.1, f32[1,8192]{1,0:T(1,128)} %bitcast.13, f32[64,128]{1,0:T(8,128)} %constant.4.clone.cosine, f32[64,128]{1,0:T(8,128)} %constant.5.clone.sine, ...), custom_call_target="tpu_custom_call" | custom-call | flops 8000000000 | bytes 24000000 | tf_op jit(solution)/shard_map/pallas_call | solution.py:779
  161.9 1.2 slice_bitcast_fusion

commit v7 on v6

--- a/solution.py
+++ b/solution.py
@@ -30,7 +30,7 @@
 def kernel(
     emb, live, source_of, targets, gain, fgain, cosine, sine, wq, wk, wv, wo, head,
     out,
-    W, WO, HEAD, EB, X, G, NG, RX, MASK, SEL, SS, QA, R, C, PS, PR, PO, ZS, ZR, HP, SUMS, Y, LT, STO, SA, SB, SC,
+    W, WO, HEAD, EB, X, G, NG, RX, MASK, SEL, SS, QA, R, C, PS, PR, PO, ZS, ZR, HP, Y, LT, STO, SA, SB, SC,
     w_sem, ng_s, ng_r, eb_s, eb_r, hop_s, hop_r, ag_s, ag_r, res_s, res_r, ctx_s, ctx_r, ps_s, ps_r,
     zz_s, zz_r, y_s, y_r, st_s, st_r,
 ):
@@ -59,23 +59,18 @@
     here = (d, s, sib)
 
     loads = []
-    for h in range(2):
+    for g in range(NY):
+        blocks = pl.ds(g * NM, NM)
         loads.append([
-            pltpu.make_async_copy(wq.at[:, h], W.at[h, :, :, 0:512], w_sem.at[3 * h]),
-            pltpu.make_async_copy(wk.at[:, h], W.at[h, :, :, 512:640], w_sem.at[3 * h + 1]),
-            pltpu.make_async_copy(wv.at[:, h], W.at[h, :, :, 640:768], w_sem.at[3 * h + 2]),
+            pltpu.make_async_copy(wq.at[blocks], W.at[blocks, :, 0:512], w_sem.at[3 * g]),
+            pltpu.make_async_copy(wk.at[blocks], W.at[blocks, :, 512:640], w_sem.at[3 * g + 1]),
+            pltpu.make_async_copy(wv.at[blocks], W.at[blocks, :, 640:768], w_sem.at[3 * g + 2]),
         ])
-    wo_loads = []
-    for h in range(2):
-        for mm in range(NM):
-            wo_loads.append(pltpu.make_async_copy(
-                wo.at[:, mm * 256 + h * 128: mm * 256 + h * 128 + 128],
-                WO.at[h, :, mm * 128: mm * 128 + 128], w_sem.at[6 + h * NM + mm]))
+    wo_load = pltpu.make_async_copy(wo, WO, w_sem.at[12])
     for group in loads:
         for copy in group:
             copy.start()
-    for copy in wo_loads:
-        copy.start()
+    wo_load.start()
 
     barrier = pltpu.get_barrier_semaphore()
     partners = []
@@ -97,8 +92,8 @@
                 col = ypeer(g) * 2048 + ((z + zz) % NZ) * 512 + cc * 256
                 pltpu.make_async_copy(head.at[:, lane(col, 256)],
                                       HEAD.at[cc, j, :, i * 256:i * 256 + 256],
-                                      w_sem.at[22]).start()
-    head_load = pltpu.make_async_copy(HEAD, HEAD, w_sem.at[22])
+                                      w_sem.at[13]).start()
+    head_load = pltpu.make_async_copy(HEAD, HEAD, w_sem.at[13])
     shape = (4 * ROWS, ROWS)
     rq = lax.broadcasted_iota(jnp.int32, shape, 0) % ROWS
     rk = lax.broadcasted_iota(jnp.int32, shape, 1)
@@ -136,155 +131,168 @@
     def _():
         next_gain().start()
 
-    def eb_z(k):
-        return rcopy(EB.at[m], EB.at[m], eb_s.at[k], eb_r.at[m], (d, s, zpeer(k)))
-
-    def eb_z_in(k):
+    def eb_z(q, k):
+        return rcopy(EB.at[q, m], EB.at[q, m], eb_s.at[q, k], eb_r.at[q, m], (d, s, zpeer(k)))
+
+    def eb_z_in(q, k):
         mk = zpeer(k)
-        return rcopy(EB.at[mk], EB.at[mk], eb_s.at[k], eb_r.at[mk], (d, s, zpeer(k)))
-
-    def eb_fwd(k):
+        return rcopy(EB.at[q, mk], EB.at[q, mk], eb_s.at[q, k], eb_r.at[q, mk], here)
+
+    def eb_fwd(q, k):
         mk = zpeer(k)
-        return rcopy(EB.at[mk], EB.at[mk], eb_s.at[4 + k], eb_r.at[mk], here)
-
-    def eb_sib_in(k):
+        return rcopy(EB.at[q, mk], EB.at[q, mk], eb_s.at[q, 4 + k], eb_r.at[q, mk], here)
+
+    def eb_sib_in(q, k):
         mk = zother(k)
-        return rcopy(EB.at[mk], EB.at[mk], eb_s.at[4 + k], eb_r.at[mk], here)
-
-    rows_of = (pl.ds(0, ROWS), pl.ds(0, ROWS + 16))
-
-    def hop(h, g):
-        return rcopy(G.at[h, g, rows_of[h]], X.at[h, m, d, rows_of[h]], hop_s.at[h, g],
-                     hop_r.at[h, d], (g, (s + 1) % NX, m))
-
-    def hop_in(h, g):
-        return rcopy(G.at[h, g, rows_of[h]], X.at[h, m, g, rows_of[h]], hop_s.at[h, g],
-                     hop_r.at[h, g], (g, (s + 1) % NX, m))
-
-    def hop_raw(h):
-        return rcopy(HP.at[h], R.at[h], hop_s.at[h, 4], hop_r.at[h, 4], (d, (s + 1) % NX, m))
-
-    def slab(h, mm):
-        return X.at[h, mm, :, rows_of[h]]
-
-    def ag_z(h, k):
-        return rcopy(slab(h, m), slab(h, m), ag_s.at[h, k], ag_r.at[h, m], (d, s, zpeer(k)))
-
-    def ag_z_in(h, k):
+        return rcopy(EB.at[q, mk], EB.at[q, mk], eb_s.at[q, 4 + k], eb_r.at[q, mk], here)
+
+    def hop(g):
+        return rcopy(G.at[g], X.at[d, m], hop_s.at[g], hop_r.at[d], (g, (s + 1) % NX, m))
+
+    def hop_in(g):
+        return rcopy(G.at[g], X.at[g, m], hop_s.at[g], hop_r.at[g], (g, (s + 1) % NX, m))
+
+    def hop_raw():
+        return rcopy(HP, R, hop_s.at[4], hop_r.at[4], (d, (s + 1) % NX, m))
+
+    def ag_z(g, k):
+        return rcopy(X.at[g, m], X.at[g, m], ag_s.at[g, k], ag_r.at[g, m], (d, s, zpeer(k)))
+
+    def ag_z_in(g, k):
         mk = zpeer(k)
-        return rcopy(slab(h, mk), slab(h, mk), ag_s.at[h, k], ag_r.at[h, mk], (d, s, zpeer(k)))
-
-    def ag_fwd(h, k):
+        return rcopy(X.at[g, mk], X.at[g, mk], ag_s.at[g, k], ag_r.at[g, mk], here)
+
+    def ag_fwd(g, k):
         mk = zpeer(k)
-        return rcopy(slab(h, mk), slab(h, mk), ag_s.at[h, 4 + k], ag_r.at[h, mk], here)
-
-    def ag_sib_in(h, k):
+        return rcopy(X.at[g, mk], X.at[g, mk], ag_s.at[g, 4 + k], ag_r.at[g, mk], here)
+
+    def ag_sib_in(g, k):
         mk = zother(k)
-        return rcopy(slab(h, mk), slab(h, mk), ag_s.at[h, 4 + k], ag_r.at[h, mk], here)
-
-    def res(h, k):
+        return rcopy(X.at[g, mk], X.at[g, mk], ag_s.at[g, 4 + k], ag_r.at[g, mk], here)
+
+    def res(k):
         g = ypeer(k)
-        return rcopy(RX.at[h, g], R.at[h, d], res_s.at[h, k], res_r.at[h, d], (g, s, m))
-
-    def res_in(h, k):
+        return rcopy(RX.at[g], R.at[d], res_s.at[k], res_r.at[d], (g, s, m))
+
+    def res_in(k):
         g = ypeer(k)
-        return rcopy(RX.at[h, g], R.at[h, g], res_s.at[h, k], res_r.at[h, g], (g, s, m))
+        return rcopy(RX.at[g], R.at[g], res_s.at[k], res_r.at[g], here)
 
     def ctx(k):
         return rcopy(C.at[d], C.at[d], ctx_s.at[k], ctx_r.at[d], (ypeer(k), s, m))
 
     def ctx_in(k):
         g = ypeer(k)
-        return rcopy(C.at[g], C.at[g], ctx_s.at[k], ctx_r.at[g], (g, s, m))
-
-    def part(h, zz):
-        return rcopy(PS.at[h, zz], PR.at[h, zz], ps_s.at[h, zz], ps_r.at[h, zz], here)
-
-    def zred(h, k):
-        return rcopy(ZS.at[h, k], ZR.at[h, k], zz_s.at[h, k], zz_r.at[h, k], (d, s, zpeer(k)))
+        return rcopy(C.at[g], C.at[g], ctx_s.at[k], ctx_r.at[g], here)
+
+    def part(g):
+        return rcopy(PS.at[g], PR.at[g], ps_s.at[g], ps_r.at[g], here)
+
+    def zred(g, k):
+        return rcopy(ZS.at[g, k], ZR.at[g, k], zz_s.at[g, k], zz_r.at[g, k], (d, s, zpeer(k)))
 
     def layer():
+        def multiply(g, who, start=False):
+            x = jnp.concatenate([X[g, 2 * zz + who, 0:ROWS] for zz in range(NZ)], axis=1)
+            w = jnp.concatenate([W[g * NM + 2 * zz + who] for zz in range(NZ)], axis=0)
+            term = jnp.dot(x, w, preferred_element_type=F32)
+            QA[...] = term if start else QA[...] + term
+
         @pl.when(s == 0)
         def _():
             rows = jnp.concatenate([emb[0], emb[1]], axis=0).astype(F32)
-            EB.at[m][...] = jnp.concatenate([rows[:, :4096], rows[:, 4096:]], axis=0).astype(BF)
-            for k in (2, 1, 3, 0):
-                (eb_z(k) if k else eb_fwd(0)).start()
-            for k in (1, 3, 2):
-                eb_z_in(k).wait_recv()
-                eb_fwd(k).start()
-            for k in range(4):
-                eb_sib_in(k).wait_recv()
-
-            def block(dl, mm, h):
-                return EB[:, :, lane(dl * 2048 + mm * 256 + h * 128, 128)].astype(F32)
-
-            def body(mm, total):
-                for dl in range(2):
-                    for h in range(2):
-                        xf = block(dl, mm, h)
-                        for half in range(2):
-                            xs = xf[:, half * 8: half * 8 + 8, :].reshape(ROWS, 128)
-                            g = half * 2 + dl
-                            cols = lane(g * 2048 + mm * 256 + h * 128, 128)
-                            X.at[h, mm, g][0:ROWS, :] = (xs * gain[:, cols]).astype(BF)
-                            total = total + xs * xs
-                return total
-
-            SS[...] = lax.fori_loop(0, NM, body, jnp.zeros((ROWS, 128), F32))
-            for dl in range(2):
-                for h in range(2):
-                    xf = block(dl, m, h)
-                    for half in range(2):
-                        xs = xf[:, half * 8: half * 8 + 8, :].reshape(ROWS, 128)
-                        RX.at[h, half * 2 + dl][...] = xs.astype(BF)
-            for h in range(2):
-                for k in (2, 1, 3):
-                    res(h, k).start()
-                R.at[h, d][...] = RX[h, d]
+            for q in range(2):
+                EB.at[q, m][...] = jnp.concatenate(
+                    [rows[:, q * 2048:q * 2048 + 2048], rows[:, q * 2048 + 4096:q * 2048 + 6144]],
+                    axis=0).astype(BF)
+                for k in (2, 1, 3, 0):
+                    (eb_z(q, k) if k else eb_fwd(q, 0)).start()
+            for q in range(2):
+                for k in (1, 3, 2):
+                    eb_z_in(q, k).wait_recv()
+                    eb_fwd(q, k).start()
+            SS[...] = jnp.zeros_like(SS)
+            for q in range(2):
+                for k in range(4):
+                    eb_sib_in(q, k).wait_recv()
+
+                def blocks(mm):
+                    x = EB[q, :, :, lane(mm * 256, 256)].astype(F32)
+                    return [x[:, i * 8:i * 8 + 8, :].reshape(ROWS, 256) for i in range(2)]
+
+                def body(mm, total):
+                    for half, xs in enumerate(blocks(mm)):
+                        g = half * 2 + q
+                        cols = lane(g * 2048 + mm * 256, 256)
+                        X.at[g, mm][0:ROWS, :] = (xs * gain[:, cols]).astype(BF)
+                        square = xs * xs
+                        total = total + square[:, 0:128] + square[:, 128:256]
+                    return total
+
+                SS[...] = lax.fori_loop(0, NM, body, SS[...])
+                for half, xs in enumerate(blocks(m)):
+                    RX.at[half * 2 + q][...] = xs.astype(BF)
+            for k in (2, 1, 3):
+                res(k).start()
+            R.at[d][...] = RX[d]
+            for group in loads:
+                for copy in group:
+                    copy.wait()
+            QA[...] = jnp.zeros_like(QA)
+
+            def both(g, _):
+                multiply(g, 0)
+                multiply(g, 1)
+                return 0
+
+            lax.fori_loop(0, NY, both, 0)
 
         @pl.when(s > 0)
         def _():
-            for h in range(2):
-                for g in range(NY):
-                    hop_in(h, g).wait_recv()
-                for k in (2, 1, 3, 0):
-                    (ag_z(h, k) if k else ag_fwd(h, 0)).start()
-            for h in range(2):
-                for k in (1, 3, 2):
-                    ag_z_in(h, k).wait_recv()
-                    ag_fwd(h, k).start()
-
-        def multiply(h, who, start):
-            term = None
-            for g in range(NY):
-                x = jnp.concatenate([X[h, 2 * zz + who, g, 0:ROWS] for zz in range(NZ)], axis=1)
-                w = jnp.concatenate([W[h, g * 8 + 2 * zz + who] for zz in range(NZ)], axis=0)
-                one = jnp.dot(x, w, preferred_element_type=F32)
-                term = one if term is None else term + one
-            QA[...] = term if start else QA[...] + term
-
-        for h in range(2):
-            for copy in loads[h]:
-                copy.wait()
-            multiply(h, c, h == 0)
-
-            @pl.when(s > 0)
-            def _():
-                for k in range(4):
-                    ag_sib_in(h, k).wait_recv()
-
-            multiply(h, 1 - c, False)
-
-        @pl.when(s > 0)
-        def _():
-            total = jnp.zeros((16, 128), F32)
+            def arrived(k):
+                g = ypeer(k)
+                hop_in(g).wait_recv()
+                for j in (2, 1, 3, 0):
+                    (ag_z(g, j) if j else ag_fwd(g, 0)).start()
+
+            def hand_on(k):
+                g = ypeer(k)
+                for j in (1, 3, 2):
+                    ag_z_in(g, j).wait_recv()
+                    ag_fwd(g, j).start()
+
+            def other_half(k):
+                g = ypeer(k)
+                for j in range(4):
+                    ag_sib_in(g, j).wait_recv()
+                multiply(g, 1 - c)
+
+            for group in loads:
+                for copy in group:
+                    copy.wait()
+            arrived(0)
+            arrived(3)
+            arrived(1)
+            hand_on(0)
+            arrived(2)
+            multiply(d, c, True)
+            hand_on(3)
+            hand_on(1)
+            other_half(0)
+            multiply(ypeer(3), c)
+            multiply(ypeer(1), c)
+            hand_on(2)
+            other_half(3)
+            other_half(1)
+            multiply(ypeer(2), c)
+            other_half(2)
+            total = jnp.zeros((16, 256), F32)
             for mm in range(NM):
                 for g in range(NY):
-                    total = total + X[1, mm, g, ROWS:ROWS + 16].astype(F32)
-            total = total[0:1] + total[1:2]
+                    total = total + X[g, mm, ROWS:ROWS + 16].astype(F32)
+            total = total[0:1, 0:128] + total[1:2, 0:128]
             mine = (lax.broadcasted_iota(jnp.int32, (ROWS, 128), 1)
-                    == lax.broadcasted_iota(jnp.int32, (ROWS, 128), 0) + (d % 2) * ROWS)
+                    == lax.broadcasted_iota(jnp.int32, (ROWS, 128), 0))
             SS[...] = jnp.where(mine, total, 0.0)
 
         r = lax.rsqrt(jnp.sum(SS[...], axis=1, keepdims=True) * (1.0 / D) + EPS)
@@ -310,82 +318,81 @@
         for k in (2, 1, 3):
             ctx(k).start()
 
-        for copy in wo_loads:
-            copy.wait()
-        for k in (1, 3, 2):
-            ctx_in(k).wait_recv()
-
-        context = C[...].reshape(NY * ROWS, QW)
-        for h in range(2):
-            for k in (2, 1, 3, 0):
-                zz = (z + k) % NZ
-                p = jnp.dot(context, WO[h, :, lane(zz * 256, 256)], preferred_element_type=F32)
-                low, high = p[:, :128], p[:, 128:]
-                PO.at[h, zz][...] = jnp.where(c == 0, low, high)
-                PS.at[h, zz][...] = jnp.where(c == 0, high, low).astype(BF)
-                part(h, zz).start()
-
-        def pair(h, k):
-            zt = (z + k) % NZ
-            part(h, zt).wait_recv()
-            return PO[h, zt] + PR[h, zt].astype(F32)
-
-        for h in range(2):
+        wo_load.wait()
+
+        def project(g):
+            for zz in range(NZ):
+                p = jnp.dot(C[g], WO[:, zz * 512:zz * 512 + 512], preferred_element_type=F32)
+                low, high = p[:, :256], p[:, 256:]
+                PO.at[g, zz][...] = jnp.where(c == 0, low, high)
+                PS.at[g, zz][...] = jnp.where(c == 0, high, low).astype(BF)
+            part(g).start()
+
+        def pair(g):
+            part(g).wait_recv()
             for k in (2, 1, 3):
-                ZS.at[h, k][...] = pair(h, k).astype(BF)
-                zred(h, k).start()
-        @pl.when(s == 0)
-        def _():
-            for h in range(2):
-                for k in (1, 3, 2):
-                    res_in(h, k).wait_recv()
-
-        @pl.when(s > 0)
-        def _():
-            for h in range(2):
-                hop_raw(h).wait_recv()
-
-        @pl.when(s < NX - 1)
-        def _():
-            next_gain().wait_recv()
-
-        sums = jnp.zeros((16, NY * ROWS), F32)
-        for h in range(2):
-            total = pair(h, 0)
-            total = total + R[h].astype(F32).reshape(NY * ROWS, 128)
+                zt = (z + k) % NZ
+                ZS.at[g, k][...] = (PO[g, zt] + PR[g, zt].astype(F32)).astype(BF)
+                zred(g, k).start()
+
+        def total_of(g):
+            total = PO[g, z] + PR[g, z].astype(F32) + R[g].astype(F32)
             for k in (1, 3, 2):
-                zred(h, k).wait_recv()
-                total = total + ZR[h, k].astype(F32)
+                zred(g, k).wait_recv()
+                total = total + ZR[g, k].astype(F32)
             hidden = total.astype(BF)
-            HP.at[h][...] = hidden.reshape(NY, ROWS, 128)
+            HP.at[g][...] = hidden
             wide = hidden.astype(F32)
-            scaled = (wide * NG[:, h * 128:h * 128 + 128]).astype(BF)
-            G.at[h][:, 0:ROWS, :] = scaled.reshape(NY, ROWS, 128)
+            G.at[g][0:ROWS, :] = (wide * NG[...]).astype(BF)
             square = wide * wide
             top = square.astype(BF)
             rest = (square - top.astype(F32)).astype(BF)
-            ones = jnp.ones((16, 128), BF)
+            ones = jnp.ones((16, 256), BF)
             nt = (((1,), (1,)), ((), ()))
-            sums = sums + lax.dot_general(ones, top, nt, preferred_element_type=F32)
-            sums = sums + lax.dot_general(ones, rest, nt, preferred_element_type=F32)
-            if h == 1:
-                top = sums.astype(BF).astype(F32)
-                row = lax.broadcasted_iota(jnp.int32, (16, NY * ROWS), 0)
-                packed = jnp.where(row == 0, top, jnp.where(row == 1, sums - top, 0.0)).astype(BF)
-                for g in range(NY):
-                    tile = g // 2 * 128
-                    G.at[1, g][ROWS:ROWS + 16, :] = packed[:, tile:tile + 128]
-                SUMS[...] = packed
+            sums = (lax.dot_general(ones, top, nt, preferred_element_type=F32)
+                    + lax.dot_general(ones, rest, nt, preferred_element_type=F32))
+            top = sums.astype(BF).astype(F32)
+            row = lax.broadcasted_iota(jnp.int32, (16, ROWS), 0)
+            packed = jnp.where(row == 0, top, jnp.where(row == 1, sums - top, 0.0))
+            packed = jnp.concatenate([packed, jnp.zeros_like(packed)], axis=1).astype(BF)
+            G.at[g][ROWS:ROWS + 16, 0:128] = packed
 
             @pl.when(s < NX - 1)
             def _():
-                for k in (2, 1, 3, 0):
-                    hop(h, ypeer(k)).start()
+                hop(g).start()
+
+        project(d)
+
+        @pl.when(s == 0)
+        def _():
+            for k in (1, 3, 2):
+                res_in(k).wait_recv()
+
+        @pl.when(s > 0)
+        def _():
+            hop_raw().wait_recv()
 
         @pl.when(s < NX - 1)
         def _():
-            for h in range(2):
-                hop_raw(h).start()
+            next_gain().wait_recv()
+
+        pair(d)
+        for k in (1, 3):
+            ctx_in(k).wait_recv()
+            project(ypeer(k))
+        pair(ypeer(1))
+        pair(ypeer(3))
+        total_of(d)
+        ctx_in(2).wait_recv()
+        project(ypeer(2))
+        total_of(ypeer(1))
+        pair(ypeer(2))
+        total_of(ypeer(3))
+        total_of(ypeer(2))
+
+        @pl.when(s < NX - 1)
+        def _():
+            hop_raw().start()
 
         @pl.when(s % 2 == 1)
         def _():
@@ -394,13 +401,21 @@
     def emit(b):
         mine = Y.at[b, c, 0, 0]
         nt = (((1,), (1,)), ((), ()))
-        for h in range(2):
-            wide = HP[h].astype(F32).reshape(NY * ROWS, 128)
-            cols = lane(d * 2048 + m * 256 + h * 128, 128)
-            scaled = (wide * fgain[:, cols]).astype(BF)
-            live_rows = jnp.dot(SEL[0:LIVE], scaled, preferred_element_type=F32)
-            mine[0:LIVE, h * 128:h * 128 + 128] = live_rows.astype(BF)
-        squares = lax.dot_general(SUMS[...], SEL[...], nt, preferred_element_type=F32)
+        wide = HP[...].reshape(NY * ROWS, 256).astype(F32)
+        cols = lane(d * 2048 + m * 256, 256)
+        scaled = (wide * fgain[:, cols]).astype(BF)
+        live_rows = jnp.dot(SEL[0:LIVE], scaled, preferred_element_type=F32)
+        mine[0:LIVE, :] = live_rows.astype(BF)
+        square = wide * wide
+        top = square.astype(BF)
+        rest = (square - top.astype(F32)).astype(BF)
+        ones = jnp.ones((16, 256), BF)
+        sums = (lax.dot_general(ones, top, nt, preferred_element_type=F32)
+                + lax.dot_general(ones, rest, nt, preferred_element_type=F32))
+        top = sums.astype(BF).astype(F32)
+        row = lax.broadcasted_iota(jnp.int32, (16, NY * ROWS), 0)
+        packed = jnp.where(row == 0, top, jnp.where(row == 1, sums - top, 0.0)).astype(BF)
+        squares = lax.dot_general(packed, SEL[...], nt, preferred_element_type=F32)
         mine[LIVE:PIECE, :] = squares.astype(BF)
         for half in range(2):
             y_x(b, half, 1).start()
@@ -692,41 +707,33 @@
 
     @pl.when(s == 0)
     def _():
-        for k in range(4):
-            (eb_z(k) if k else eb_fwd(0)).wait_send()
+        for q in range(2):
+            for k in range(1, 4):
+                eb_z(q, k).wait_send()
+            for k in range(4):
+                eb_fwd(q, k).wait_send()
         for k in range(1, 4):
-            eb_fwd(k).wait_send()
+            res(k).wait_send()
 
     @pl.when(s > 0)
     def _():
-        for h in range(2):
+        for g in range(NY):
             for k in range(1, 4):
-                ag_z(h, k).wait_send()
+                ag_z(g, k).wait_send()
             for k in range(4):
-                ag_fwd(h, k).wait_send()
+                ag_fwd(g, k).wait_send()
+        next_gain().wait_send()
 
     @pl.when(s < NX - 1)
     def _():
-        for h in range(2):
-            for k in range(4):
-                hop(h, ypeer(k)).wait_send()
-            hop_raw(h).wait_send()
-
-    @pl.when(s == 0)
-    def _():
-        for h in range(2):
-            for k in range(1, 4):
-                res(h, k).wait_send()
-
-    @pl.when(s > 0)
-    def _():
-        next_gain().wait_send()
-
-    for h in range(2):
+        for g in range(NY):
+            hop(g).wait_send()
+        hop_raw().wait_send()
+
+    for g in range(NY):
         for k in range(1, 4):
-            zred(h, k).wait_send()
-        for zz in range(NZ):
-            part(h, zz).wait_send()
+            zred(g, k).wait_send()
+        part(g).wait_send()
     for k in range(1, 4):
         ctx(k).wait_send()
         st_y(k).wait_send()
@@ -782,42 +789,41 @@
         in_specs=[vmem, smem, smem, vmem, vmem, vmem, vmem, vmem, hbm, hbm, hbm, hbm, hbm],
         out_specs=vmem,
         scratch_shapes=[
-            pltpu.VMEM((2, 32, 128, 768), BF),
-            pltpu.VMEM((2, QW, 1024), BF),
+            pltpu.VMEM((32, 256, 768), BF),
+            pltpu.VMEM((QW, 2048), BF),
             pltpu.VMEM((2, 4, vocab, 1024), BF),
-            pltpu.VMEM((NM, 16, 4096), BF),
-            pltpu.VMEM((2, NM, NY, ROWS + 16, 128), BF),
-            pltpu.VMEM((2, NY, ROWS + 16, 128), BF),
+            pltpu.VMEM((2, NM, 16, 2048), BF),
+            pltpu.VMEM((NY, NM, ROWS + 16, 256), BF),
+            pltpu.VMEM((NY, ROWS + 16, 256), BF),
             pltpu.VMEM((1, 256), F32),
-            pltpu.VMEM((2, NY, ROWS, 128), BF),
+            pltpu.VMEM((NY, ROWS, 256), BF),
             pltpu.VMEM((4 * ROWS, ROWS), F32),
             pltpu.VMEM((256, 256), BF),
             pltpu.VMEM((ROWS, 128), F32),
             pltpu.VMEM((ROWS, 768), F32),
-            pltpu.VMEM((2, NY, ROWS, 128), BF),
+            pltpu.VMEM((NY, ROWS, 256), BF),
             pltpu.VMEM((NY, ROWS, QW), BF),
-            pltpu.VMEM((2, NZ, NY * ROWS, 128), BF),
-            pltpu.VMEM((2, NZ, NY * ROWS, 128), BF),
-            pltpu.VMEM((2, NZ, NY * ROWS, 128), F32),
-            pltpu.VMEM((2, NZ, NY * ROWS, 128), BF),
-            pltpu.VMEM((2, NZ, NY * ROWS, 128), BF),
-            pltpu.VMEM((2, NY, ROWS, 128), BF),
-            pltpu.VMEM((16, NY * ROWS), BF),
+            pltpu.VMEM((NY, NZ, ROWS, 256), BF),
+            pltpu.VMEM((NY, NZ, ROWS, 256), BF),
+            pltpu.VMEM((NY, NZ, ROWS, 256), F32),
+            pltpu.VMEM((NY, NZ, ROWS, 256), BF),
+            pltpu.VMEM((NY, NZ, ROWS, 256), BF),
+            pltpu.VMEM((NY, ROWS, 256), BF),
             pltpu.VMEM((2, 2, 4, 4, 256, 256), BF),
             pltpu.VMEM((vocab, 256), F32),
             pltpu.VMEM((16, 128), F32),
             pltpu.VMEM((NY, 16, 128), F32),
             pltpu.VMEM((NM, 16, 128), F32),
             pltpu.VMEM((NX, 16, 128), F32),
-            dma((23,)),
+            dma((14,)),
             dma, dma,
-            dma((8,)), dma((8,)),
-            dma((2, 5)), dma((2, 5)),
             dma((2, 8)), dma((2, 8)),
-            dma((2, 4)), dma((2, 4)),
+            dma((5,)), dma((5,)),
+            dma((4, 8)), dma((4, 8)),
             dma((4,)), dma((4,)),
-            dma((2, 4)), dma((2, 4)),
-            dma((2, 4)), dma((2, 4)),
+            dma((4,)), dma((4,)),
+            dma((4,)), dma((4,)),
+            dma((4, 4)), dma((4, 4)),
             dma((2, 30)), dma((2, 22)),
             dma((3, 8)), dma((3, 8)),
         ],
@@ -827,8 +833,8 @@
                                       transcendentals=300_000),
     )(
         embeds, lengths, source, targets, attn_gain, final_gain.reshape(1, D), jnp.asarray(cos), jnp.asarray(sin),
-        w_query.reshape(32, 2, 128, 512), w_key.reshape(32, 2, 128, 128),
-        w_value.reshape(32, 2, 128, 128), w_out.reshape(512, 2048), head,
+        w_query.reshape(32, 256, 512), w_key.reshape(32, 256, 128),
+        w_value.reshape(32, 256, 128), w_out.reshape(512, 2048), head,
     )
     return (stats[0], stats[1])
 

time: 163 us -> 154 us (0.945)
  Pallas kernels: 161 us -> 152 us
    pallas_call x1, Pallas kernels: 161 us -> 152 us  [per_device(): pl.pallas_call(kernel, out_shape=jax.ShapeDtypeStruct((2, 2, 32), F32), i...]
where the time goes in v7:
time: 154 us
  Pallas kernels  152 us (99%)
    pallas_call x1, Pallas kernels, per_device(): pl.pallas_call(kernel, out_shape=jax.ShapeDtypeStruct((2, 2, 32), F32), i...  152 us

profile of v7, /device:TPU:1, one launch (start us, length us, event | category | flops | bytes accessed | tf_op | source)
XLA Modules:
  0.0 154.3 jit_solution(3120494516685238052)
XLA Ops:
  0.6 152.4 %shard_map.140 = f32[2,2,32]{2,1,0:T(2,128)} custom-call(bf16[2,4,8192]{2,1,0:T(4,128)(2,1)} %emb.1, s32[8]{0:T(128)} %live.1, s32[8]{0:T(128)} %source_of.1, s32[8,32]{1,0:T(8,128)} %targets.1, f32[1,8192]{1,0:T(1,128)} %gain.1, f32[1,8192]{1,0:T(1,128)} %bitcast.13, f32[64,128]{1,0:T(8,128)} %constant.4.clone.cosine, f32[64,128]{1,0:T(8,128)} %constant.5.clone.sine, ...), custom_call_target="tpu_custom_call" | custom-call | flops 8000000000 | bytes 24000000 | tf_op jit(solution)/shard_map/pallas_call | solution.py:786
  153.1 1.2 slice_bitcast_fusion

commit v8 on v7

--- a/solution.py
+++ b/solution.py
@@ -28,9 +28,9 @@
 
 
 def kernel(
-    emb, live, source_of, targets, gain, fgain, cosine, sine, wq, wk, wv, wo, head,
+    emb_in, live, source_of, targets_in, gain, fgain_in, cosine_in, sine_in, wq, wk, wv, wo, head,
     out,
-    W, WO, HEAD, EB, X, G, NG, RX, MASK, SEL, SS, QA, R, C, PS, PR, PO, ZS, ZR, HP, Y, LT, STO, SA, SB, SC,
+    emb, targets, gains, fgain, cosine, sine, W, WO, HEAD, EB, X, G, NG, RX, MASK, SEL, SS, QA, R, C, PS, PR, PO, ZS, ZR, HP, Y, LT, STO, SA, SB, SC,
     w_sem, ng_s, ng_r, eb_s, eb_r, hop_s, hop_r, ag_s, ag_r, res_s, res_r, ctx_s, ctx_r, ps_s, ps_r,
     zz_s, zz_r, y_s, y_r, st_s, st_r,
 ):
@@ -58,6 +58,26 @@
 
     here = (d, s, sib)
 
+    barrier = pltpu.get_barrier_semaphore()
+    partners = []
+    for k in range(1, 4):
+        partners.append((ypeer(k), s, m))
+        partners.append((d, (s + k) % NX, m))
+        partners.append((d, s, zpeer(k)))
+        partners.append((d, s, zother(k)))
+        partners.append((ypeer(k), (s + 1) % NX, m))
+        partners.append((ypeer(k), (s + 3) % NX, m))
+    partners.append(here)
+    for dev in partners:
+        pl.semaphore_signal(barrier, inc=1, device_id=dev, device_id_type=MESH)
+    small = [
+        pltpu.make_async_copy(src, dst, w_sem.at[14 + n])
+        for n, (src, dst) in enumerate((
+            (emb_in, emb), (gain, gains), (cosine_in, cosine), (sine_in, sine),
+            (fgain_in, fgain), (targets_in, targets)))
+    ]
+    for copy in small:
+        copy.start()
     loads = []
     for g in range(NY):
         blocks = pl.ds(g * NM, NM)
@@ -70,57 +90,58 @@
     for group in loads:
         for copy in group:
             copy.start()
-    wo_load.start()
-
-    barrier = pltpu.get_barrier_semaphore()
-    partners = []
-    for k in range(1, 4):
-        partners.append((ypeer(k), s, m))
-        partners.append((d, (s + k) % NX, m))
-        partners.append((d, s, zpeer(k)))
-        partners.append((d, s, zother(k)))
-        partners.append((ypeer(k), (s + 1) % NX, m))
-        partners.append((ypeer(k), (s + 3) % NX, m))
-    partners.append(here)
-    for dev in partners:
-        pl.semaphore_signal(barrier, inc=1, device_id=dev, device_id_type=MESH)
-    offsets = (0, 3, 1, 2)
-    for cc in range(2):
-        for j in range(4):
-            for i in range(4):
-                g, zz = (offsets[i], offsets[j]) if cc == 0 else (offsets[j], offsets[i])
-                col = ypeer(g) * 2048 + ((z + zz) % NZ) * 512 + cc * 256
-                pltpu.make_async_copy(head.at[:, lane(col, 256)],
-                                      HEAD.at[cc, j, :, i * 256:i * 256 + 256],
-                                      w_sem.at[13]).start()
+
     head_load = pltpu.make_async_copy(HEAD, HEAD, w_sem.at[13])
-    shape = (4 * ROWS, ROWS)
-    rq = lax.broadcasted_iota(jnp.int32, shape, 0) % ROWS
-    rk = lax.broadcasted_iota(jnp.int32, shape, 1)
-    slot_q, slot_k = (rq // 4) % 2, (rk // 4) % 2
-    pos_q, pos_k = (rq // 8) * 4 + rq % 4, (rk // 8) * 4 + rk % 4
-    live_k = jnp.where(slot_k == 0, live[2 * d], live[2 * d + 1])
-    allowed = (slot_q == slot_k) & (pos_k <= pos_q) & (pos_k < live_k)
-    MASK[...] = jnp.where(allowed, F32(0.0), F32(-1e30))
+
+    def prepare():
+        wo_load.start()
+        offsets = (0, 3, 1, 2)
+        for cc in range(2):
+            for j in range(4):
+                for i in range(4):
+                    g, zz = (offsets[i], offsets[j]) if cc == 0 else (offsets[j], offsets[i])
+                    col = ypeer(g) * 2048 + ((z + zz) % NZ) * 512 + cc * 256
+                    pltpu.make_async_copy(head.at[:, lane(col, 256)],
+                                          HEAD.at[cc, j, :, i * 256:i * 256 + 256],
+                                          w_sem.at[13]).start()
+        shape = (4 * ROWS, ROWS)
+        rq = lax.broadcasted_iota(jnp.int32, shape, 0) % ROWS
+        rk = lax.broadcasted_iota(jnp.int32, shape, 1)
+        slot_q, slot_k = (rq // 4) % 2, (rk // 4) % 2
+        pos_q, pos_k = (rq // 8) * 4 + rq % 4, (rk // 8) * 4 + rk % 4
+        live_k = jnp.where(slot_k == 0, live[2 * d], live[2 * d + 1])
+        allowed = (slot_q == slot_k) & (pos_k <= pos_q) & (pos_k < live_k)
+        MASK[...] = jnp.where(allowed, F32(0.0), F32(-1e30))
+
+        def first_row(slot):
+            start = jnp.zeros_like(slot)
+            for other in range(8):
+                start = start + jnp.where(slot > other, live[other], 0)
+            return start
+
+        def live_of(slot):
+            count = jnp.zeros_like(slot)
+            for other in range(8):
+                count = count + jnp.where(slot == other, live[other], 0)
+            return count
+
+        slot, position = row_slot(lax.broadcasted_iota(jnp.int32, (8, 256), 1))
+        packed_at = jnp.where(position < live_of(slot), first_row(slot) + position, 999)[0:1]
+        SEL[...] = (lax.broadcasted_iota(jnp.int32, (256, 256), 0) == packed_at).astype(F32).astype(BF)
 
     def row_slot(lanes):
         return (lanes // 64) * 2 + (lanes // 4) % 2, ((lanes // 8) % 8) * 4 + lanes % 4
 
-    def first_row(slot):
-        start = jnp.zeros_like(slot)
-        for other in range(8):
-            start = start + jnp.where(slot > other, live[other], 0)
-        return start
-
-    def live_of(slot):
-        count = jnp.zeros_like(slot)
-        for other in range(8):
-            count = count + jnp.where(slot == other, live[other], 0)
-        return count
-
-    slot, position = row_slot(lax.broadcasted_iota(jnp.int32, (8, 256), 1))
-    packed_at = jnp.where(position < live_of(slot), first_row(slot) + position, 999)[0:1]
-    SEL[...] = (lax.broadcasted_iota(jnp.int32, (256, 256), 0) == packed_at).astype(F32).astype(BF)
+    small[0].wait()
+
+    @pl.when(s == 0)
+    def _():
+        rows = jnp.concatenate([emb[0], emb[1]], axis=0).astype(F32)
+        for q in range(2):
+            EB.at[q, m][...] = jnp.concatenate(
+                [rows[:, q * 2048:q * 2048 + 2048], rows[:, q * 2048 + 4096:q * 2048 + 6144]],
+                axis=0).astype(BF)
+
     pl.semaphore_wait(barrier, len(partners))
 
     def next_gain():
@@ -200,17 +221,11 @@
 
         @pl.when(s == 0)
         def _():
-            rows = jnp.concatenate([emb[0], emb[1]], axis=0).astype(F32)
-            for q in range(2):
-                EB.at[q, m][...] = jnp.concatenate(
-                    [rows[:, q * 2048:q * 2048 + 2048], rows[:, q * 2048 + 4096:q * 2048 + 6144]],
-                    axis=0).astype(BF)
-                for k in (2, 1, 3, 0):
-                    (eb_z(q, k) if k else eb_fwd(q, 0)).start()
             for q in range(2):
                 for k in (1, 3, 2):
                     eb_z_in(q, k).wait_recv()
                     eb_fwd(q, k).start()
+            QA[...] = jnp.zeros_like(QA)
             SS[...] = jnp.zeros_like(SS)
             for q in range(2):
                 for k in range(4):
@@ -224,7 +239,7 @@
                     for half, xs in enumerate(blocks(mm)):
                         g = half * 2 + q
                         cols = lane(g * 2048 + mm * 256, 256)
-                        X.at[g, mm][0:ROWS, :] = (xs * gain[:, cols]).astype(BF)
+                        X.at[g, mm][0:ROWS, :] = (xs * gains[:, cols]).astype(BF)
                         square = xs * xs
                         total = total + square[:, 0:128] + square[:, 128:256]
                     return total
@@ -232,20 +247,19 @@
                 SS[...] = lax.fori_loop(0, NM, body, SS[...])
                 for half, xs in enumerate(blocks(m)):
                     RX.at[half * 2 + q][...] = xs.astype(BF)
+                for g in (q, q + 2):
+                    for copy in loads[g]:
+                        copy.wait()
+
+                def both(i, _):
+                    multiply(2 * i + q, 0)
+                    multiply(2 * i + q, 1)
+                    return 0
+
+                lax.fori_loop(0, 2, both, 0)
             for k in (2, 1, 3):
                 res(k).start()
             R.at[d][...] = RX[d]
-            for group in loads:
-                for copy in group:
-                    copy.wait()
-            QA[...] = jnp.zeros_like(QA)
-
-            def both(g, _):
-                multiply(g, 0)
-                multiply(g, 1)
-                return 0
-
-            lax.fori_loop(0, NY, both, 0)
 
         @pl.when(s > 0)
         def _():
@@ -417,9 +431,8 @@
         packed = jnp.where(row == 0, top, jnp.where(row == 1, sums - top, 0.0)).astype(BF)
         squares = lax.dot_general(packed, SEL[...], nt, preferred_element_type=F32)
         mine[LIVE:PIECE, :] = squares.astype(BF)
-        for half in range(2):
-            y_x(b, half, 1).start()
-            y_x(b, 1 - half, 3).start()
+        for k in (2, 1, 3):
+            y_x(b, k).start()
         spread_own(b)
 
     def first_dev(k):
@@ -431,36 +444,17 @@
     def ycopy(src, dst, b, i, j, dev):
         return rcopy(src, dst, y_s.at[b, i], y_r.at[b, j], dev)
 
-    cut = (pl.ds(0, 96), pl.ds(96, PIECE - 96))
-
     def own(b, rows):
         return Y.at[b, c, 0, 0, rows]
 
-    def y_x(b, half, k):
-        ref = own(b, cut[half])
-        return ycopy(ref, ref, b, k + half, (0, 21)[half], (d, (s + k) % NX, m))
-
-    def y_x_relay(b, half):
-        ref = own(b, cut[half])
-        return ycopy(ref, ref, b, 28 + half, (0, 21)[half], (d, jnp.where(b == 0, 3, 1), m))
-
-    def relays_x(b, half):
-        return (s == 0) if half == 0 else (s == jnp.where(b == 0, 0, 2))
+    def y_x(b, k):
+        return ycopy(own(b, whole), own(b, whole), b, k, 0, (d, (s + k) % NX, m))
 
     whole = pl.ds(0, PIECE)
 
     def y_first(b, k):
-        slot = 1 if k == 1 else 2
+        slot = (1, 3, 2)[k - 1]
         return ycopy(own(b, whole), Y.at[b, c, 0, slot, whole], b, 5 + k, slot, first_dev(k))
-
-    def y_first_relay(b, half):
-        slot, k = ((1, 1), (2, 3))[half]
-        return ycopy(Y.at[b, c, 0, slot, cut[half]], Y.at[b, c, 0, 3, cut[half]],
-                     b, 9 + half, 3, first_dev(k))
-
-    def y_opposite(b):
-        ref = Y.at[b, c, 0, 3, whole]
-        return ycopy(ref, ref, b, 9, 3, here)
 
     sets = (pl.ds(0, 1), pl.ds(1, 2), pl.ds(3, 1))
 
@@ -482,7 +476,7 @@
         return ycopy(ref, ref, b, 21 + n, 14 + n, here)
 
     def spread_own(b):
-        for k in (1, 3):
+        for k in (2, 1, 3):
             y_first(b, k).start()
         for k in (1, 3):
             y_second(b, 0, k).start()
@@ -513,36 +507,18 @@
 
         @pl.when(s != source)
         def _():
-            def take(half):
-                y_x(b, half, 1).wait_recv()
-
-                @pl.when(relays_x(b, half))
-                def _():
-                    y_x_relay(b, half).start()
-
-            @pl.when(s == 2)
-            def _():
-                take(1)
-                take(0)
-
-            @pl.when(s != 2)
-            def _():
-                take(0)
-                take(1)
-
+            y_x(b, 1).wait_recv()
             spread_own(b)
 
         y_first(b, 1).wait_recv()
-        y_first_relay(b, 0).start()
         y_first(b, 3).wait_recv()
-        y_first_relay(b, 1).start()
         for k in (1, 3):
             y_second(b, 1, k).start()
         y_fwd(b, 1, c).start()
         y_second(b, 0, 1).wait_recv()
         y_second_relay(b, 0).start()
         y_second(b, 0, 3).wait_recv()
-        y_opposite(b).wait_recv()
+        y_first(b, 2).wait_recv()
         for k in (1, 3):
             y_second(b, 2, k).start()
         y_fwd(b, 2, c).start()
@@ -619,6 +595,15 @@
             finish(jnp.where(t == 4, 1, 0))
         return 0
 
+    @pl.when(s == 0)
+    def _():
+        for q in range(2):
+            for k in (2, 1, 3, 0):
+                (eb_z(q, k) if k else eb_fwd(q, 0)).start()
+
+    prepare()
+    for copy in small[1:]:
+        copy.wait()
     STO[...] = jnp.zeros_like(STO)
     lax.fori_loop(0, 5, step, 0)
 
@@ -743,18 +728,12 @@
     for b in range(2):
         @pl.when(s == 2 * b + 1)
         def _():
-            for half in range(2):
-                for k in (1, 3):
-                    y_x(b, half, k).wait_send()
-
-        for half in range(2):
-            @pl.when((s != 2 * b + 1) & relays_x(b, half))
-            def _():
-                y_x_relay(b, half).wait_send()
-
-            y_first_relay(b, half).wait_send()
+            for k in (1, 2, 3):
+                y_x(b, k).wait_send()
+
+        for k in (1, 2, 3):
+            y_first(b, k).wait_send()
         for k in (1, 3):
-            y_first(b, k).wait_send()
             for n in range(3):
                 y_second(b, n, k).wait_send()
         for i in range(4):
@@ -786,9 +765,15 @@
     stats = pl.pallas_call(
         kernel,
         out_shape=jax.ShapeDtypeStruct((2, 2, 32), F32),
-        in_specs=[vmem, smem, smem, vmem, vmem, vmem, vmem, vmem, hbm, hbm, hbm, hbm, hbm],
+        in_specs=[hbm, smem, smem] + [hbm] * 10,
         out_specs=vmem,
         scratch_shapes=[
+            pltpu.VMEM((2, 4, D), BF),
+            pltpu.VMEM((8, 32), jnp.int32),
+            pltpu.VMEM((1, D), F32),
+            pltpu.VMEM((1, D), F32),
+            pltpu.VMEM((ROWS, HD), F32),
+            pltpu.VMEM((ROWS, HD), F32),
             pltpu.VMEM((32, 256, 768), BF),
             pltpu.VMEM((QW, 2048), BF),
             pltpu.VMEM((2, 4, vocab, 1024), BF),
@@ -815,7 +800,7 @@
             pltpu.VMEM((NY, 16, 128), F32),
             pltpu.VMEM((NM, 16, 128), F32),
             pltpu.VMEM((NX, 16, 128), F32),
-            dma((14,)),
+            dma((20,)),
             dma, dma,
             dma((2, 8)), dma((2, 8)),
             dma((5,)), dma((5,)),

time: 154 us -> 154 us (level)
  no operation moved by 1% of the time
where the time goes in v8:
time: 154 us
  Pallas kernels  152 us (99%)
    pallas_call x1, Pallas kernels, per_device(): pl.pallas_call(kernel, out_shape=jax.ShapeDtypeStruct((2, 2, 32), F32), i...  152 us

profile of v8, /device:TPU:1, one launch (start us, length us, event | category | flops | bytes accessed | tf_op | source)
XLA Modules:
  0.0 154.3 jit_solution(16257424123138853616)
XLA Ops:
  0.6 152.4 %shard_map.140 = f32[2,2,32]{2,1,0:T(2,128)} custom-call(bf16[2,4,8192]{2,1,0:T(4,128)(2,1)} %emb_in.1, s32[8]{0:T(128)} %live.1, s32[8]{0:T(128)} %source_of.1, s32[8,32]{1,0:T(8,128)} %targets_in.1, f32[1,8192]{1,0:T(1,128)} %gain.1, f32[1,8192]{1,0:T(1,128)} %bitcast.13, f32[64,128]{1,0:T(8,128)} %constant.4.clone.cosine_in, ...), custom_call_target="tpu_custom_call" | custom-call | flops 8000000000 | bytes 24000000 | tf_op jit(solution)/shard_map/pallas_call | solution.py:765
  153.0 1.2 slice_bitcast_fusion

commit v9 on v8

--- a/solution.py
+++ b/solution.py
@@ -30,8 +30,8 @@
 def kernel(
     emb_in, live, source_of, targets_in, gain, fgain_in, cosine_in, sine_in, wq, wk, wv, wo, head,
     out,
-    emb, targets, gains, fgain, cosine, sine, W, WO, HEAD, EB, X, G, NG, RX, MASK, SEL, SS, QA, R, C, PS, PR, PO, ZS, ZR, HP, Y, LT, STO, SA, SB, SC,
-    w_sem, ng_s, ng_r, eb_s, eb_r, hop_s, hop_r, ag_s, ag_r, res_s, res_r, ctx_s, ctx_r, ps_s, ps_r,
+    emb, targets, gains, fgain, cosine, sine, W, WO, HEAD, EB, XE, X, G, NG, RX, MASK, SEL, SS, QA, QR, R, C, PS, PR, PO, ZS, ZR, HP, Y, LT, STO, SA, SB, SC,
+    w_sem, sw_s, sw_r, qr_s, qr_r, ng_s, ng_r, eb_s, eb_r, hop_s, hop_r, ag_s, ag_r, res_s, res_r, ctx_s, ctx_r, ps_s, ps_r,
     zz_s, zz_r, y_s, y_r, st_s, st_r,
 ):
     d = lax.axis_index("dp")
@@ -78,18 +78,26 @@
     ]
     for copy in small:
         copy.start()
-    loads = []
-    for g in range(NY):
-        blocks = pl.ds(g * NM, NM)
-        loads.append([
-            pltpu.make_async_copy(wq.at[blocks], W.at[blocks, :, 0:512], w_sem.at[3 * g]),
-            pltpu.make_async_copy(wk.at[blocks], W.at[blocks, :, 512:640], w_sem.at[3 * g + 1]),
-            pltpu.make_async_copy(wv.at[blocks], W.at[blocks, :, 640:768], w_sem.at[3 * g + 2]),
-        ])
+    parts = ((wq, pl.ds(0, 512)), (wk, pl.ds(512, 128)), (wv, pl.ds(640, 128)))
+
+    def load(n, first):
+        src, lanes = parts[n]
+        take = 1 if first else jnp.where(s == 0, 0, c)
+        return pltpu.make_async_copy(src.at[:, take], W.at[first, :, :, lanes],
+                                     w_sem.at[3 * first + n])
+
+    def swap(n):
+        src, lanes = parts[n]
+        return rcopy(src.at[:, 1 - c], W.at[1, :, :, lanes], sw_s.at[n], sw_r.at[n], here)
+
     wo_load = pltpu.make_async_copy(wo, WO, w_sem.at[12])
-    for group in loads:
-        for copy in group:
-            copy.start()
+    for n in range(3):
+        load(n, 0).start()
+
+    @pl.when(s == 0)
+    def _():
+        for n in range(3):
+            load(n, 1).start()
 
     head_load = pltpu.make_async_copy(HEAD, HEAD, w_sem.at[13])
 
@@ -151,6 +159,8 @@
     @pl.when(s > 0)
     def _():
         next_gain().start()
+        for n in range(3):
+            swap(n).start()
 
     def eb_z(q, k):
         return rcopy(EB.at[q, m], EB.at[q, m], eb_s.at[q, k], eb_r.at[q, m], (d, s, zpeer(k)))
@@ -168,28 +178,23 @@
         return rcopy(EB.at[q, mk], EB.at[q, mk], eb_s.at[q, 4 + k], eb_r.at[q, mk], here)
 
     def hop(g):
-        return rcopy(G.at[g], X.at[d, m], hop_s.at[g], hop_r.at[d], (g, (s + 1) % NX, m))
+        return rcopy(G.at[g], X.at[d, z], hop_s.at[g], hop_r.at[d], (g, (s + 1) % NX, m))
 
     def hop_in(g):
-        return rcopy(G.at[g], X.at[g, m], hop_s.at[g], hop_r.at[g], (g, (s + 1) % NX, m))
+        return rcopy(G.at[g], X.at[g, z], hop_s.at[g], hop_r.at[g], (g, (s + 1) % NX, m))
 
     def hop_raw():
         return rcopy(HP, R, hop_s.at[4], hop_r.at[4], (d, (s + 1) % NX, m))
 
     def ag_z(g, k):
-        return rcopy(X.at[g, m], X.at[g, m], ag_s.at[g, k], ag_r.at[g, m], (d, s, zpeer(k)))
+        return rcopy(X.at[g, z], X.at[g, z], ag_s.at[g, k], ag_r.at[g, z], (d, s, zpeer(k)))
 
     def ag_z_in(g, k):
-        mk = zpeer(k)
-        return rcopy(X.at[g, mk], X.at[g, mk], ag_s.at[g, k], ag_r.at[g, mk], here)
-
-    def ag_fwd(g, k):
-        mk = zpeer(k)
-        return rcopy(X.at[g, mk], X.at[g, mk], ag_s.at[g, 4 + k], ag_r.at[g, mk], here)
-
-    def ag_sib_in(g, k):
-        mk = zother(k)
-        return rcopy(X.at[g, mk], X.at[g, mk], ag_s.at[g, 4 + k], ag_r.at[g, mk], here)
+        zk = (z + k) % NZ
+        return rcopy(X.at[g, zk], X.at[g, zk], ag_s.at[g, k], ag_r.at[g, zk], here)
+
+    def sums_out():
+        return rcopy(QA.at[1], QR, qr_s, qr_r, here)
 
     def res(k):
         g = ypeer(k)
@@ -213,11 +218,10 @@
         return rcopy(ZS.at[g, k], ZR.at[g, k], zz_s.at[g, k], zz_r.at[g, k], (d, s, zpeer(k)))
 
     def layer():
-        def multiply(g, who, start=False):
-            x = jnp.concatenate([X[g, 2 * zz + who, 0:ROWS] for zz in range(NZ)], axis=1)
-            w = jnp.concatenate([W[g * NM + 2 * zz + who] for zz in range(NZ)], axis=0)
+        def multiply(x, which, rows, n, start=False):
+            w = W[which, pl.ds(rows * NZ, NZ)].reshape(4 * 256, 768)
             term = jnp.dot(x, w, preferred_element_type=F32)
-            QA[...] = term if start else QA[...] + term
+            QA.at[n][:, 0:768] = term if start else QA[n, :, 0:768] + term
 
         @pl.when(s == 0)
         def _():
@@ -226,6 +230,7 @@
                     eb_z_in(q, k).wait_recv()
                     eb_fwd(q, k).start()
             QA[...] = jnp.zeros_like(QA)
+            QR[...] = jnp.zeros_like(QR)
             SS[...] = jnp.zeros_like(SS)
             for q in range(2):
                 for k in range(4):
@@ -239,7 +244,7 @@
                     for half, xs in enumerate(blocks(mm)):
                         g = half * 2 + q
                         cols = lane(g * 2048 + mm * 256, 256)
-                        X.at[g, mm][0:ROWS, :] = (xs * gains[:, cols]).astype(BF)
+                        XE.at[g, mm][...] = (xs * gains[:, cols]).astype(BF)
                         square = xs * xs
                         total = total + square[:, 0:128] + square[:, 128:256]
                     return total
@@ -247,13 +252,16 @@
                 SS[...] = lax.fori_loop(0, NM, body, SS[...])
                 for half, xs in enumerate(blocks(m)):
                     RX.at[half * 2 + q][...] = xs.astype(BF)
-                for g in (q, q + 2):
-                    for copy in loads[g]:
-                        copy.wait()
+                if q == 0:
+                    for n in range(3):
+                        load(n, 0).wait()
+                        load(n, 1).wait()
 
                 def both(i, _):
-                    multiply(2 * i + q, 0)
-                    multiply(2 * i + q, 1)
+                    g = 2 * i + q
+                    for who in range(2):
+                        x = jnp.concatenate([XE[g, 2 * zz + who] for zz in range(NZ)], axis=1)
+                        multiply(x, who, g, 0)
                     return 0
 
                 lax.fori_loop(0, 2, both, 0)
@@ -266,60 +274,60 @@
             def arrived(k):
                 g = ypeer(k)
                 hop_in(g).wait_recv()
-                for j in (2, 1, 3, 0):
-                    (ag_z(g, j) if j else ag_fwd(g, 0)).start()
-
-            def hand_on(k):
+                for j in (2, 1, 3):
+                    ag_z(g, j).start()
+
+            def columns(k):
                 g = ypeer(k)
                 for j in (1, 3, 2):
                     ag_z_in(g, j).wait_recv()
-                    ag_fwd(g, j).start()
-
-            def other_half(k):
-                g = ypeer(k)
-                for j in range(4):
-                    ag_sib_in(g, j).wait_recv()
-                multiply(g, 1 - c)
-
-            for group in loads:
-                for copy in group:
-                    copy.wait()
+                return jnp.concatenate([X[g, zz, 0:ROWS] for zz in range(NZ)], axis=1)
+
+            def both(k, start=False):
+                x = columns(k)
+                multiply(x, 1, ypeer(k), 1, start)
+                multiply(x, 0, ypeer(k), 0, start)
+
+            for n in range(3):
+                load(n, 0).wait()
+                swap(n).wait_recv()
             arrived(0)
             arrived(3)
             arrived(1)
-            hand_on(0)
             arrived(2)
-            multiply(d, c, True)
-            hand_on(3)
-            hand_on(1)
-            other_half(0)
-            multiply(ypeer(3), c)
-            multiply(ypeer(1), c)
-            hand_on(2)
-            other_half(3)
-            other_half(1)
-            multiply(ypeer(2), c)
-            other_half(2)
+            both(0, True)
+            both(3)
+            both(1)
+            x = columns(2)
+            multiply(x, 1, ypeer(2), 1)
             total = jnp.zeros((16, 256), F32)
-            for mm in range(NM):
+            for zz in range(NZ):
                 for g in range(NY):
-                    total = total + X[g, mm, ROWS:ROWS + 16].astype(F32)
+                    total = total + X[g, zz, ROWS:ROWS + 16].astype(F32)
             total = total[0:1, 0:128] + total[1:2, 0:128]
             mine = (lax.broadcasted_iota(jnp.int32, (ROWS, 128), 1)
                     == lax.broadcasted_iota(jnp.int32, (ROWS, 128), 0))
-            SS[...] = jnp.where(mine, total, 0.0)
+            squares = jnp.where(mine, total, 0.0)
+            QA.at[1][:, 768:896] = squares
+            sums_out().start()
+            multiply(x, 0, ypeer(2), 0)
+            sums_out().wait_recv()
+            SS[...] = squares + QR[:, 768:896]
 
         r = lax.rsqrt(jnp.sum(SS[...], axis=1, keepdims=True) * (1.0 / D) + EPS)
         cos = cosine[...]
         sin = sine[...]
 
+        def summed(first, last):
+            return QA[0, :, first:last] + QR[:, first:last]
+
         def rope(x):
             return (x * cos + pltpu.roll(x, 64, 1) * sin).astype(BF)
 
         query = jnp.concatenate(
-            [rope(QA[:, j * HD:(j + 1) * HD] * r) for j in range(4)], axis=0)
-        key = rope(QA[:, 512:640] * r)
-        value = (QA[:, 640:768] * r).astype(BF)
+            [rope(summed(j * HD, (j + 1) * HD) * r) for j in range(4)], axis=0)
+        key = rope(summed(512, 640) * r)
+        value = (summed(640, 768) * r).astype(BF)
         scores = lax.dot_general(query, key, (((1,), (1,)), ((), ())),
                                  preferred_element_type=F32) * (HD ** -0.5)
         scores = scores + MASK[...]
@@ -705,8 +713,9 @@
         for g in range(NY):
             for k in range(1, 4):
                 ag_z(g, k).wait_send()
-            for k in range(4):
-                ag_fwd(g, k).wait_send()
+        sums_out().wait_send()
+        for n in range(3):
+            swap(n).wait_send()
         next_gain().wait_send()
 
     @pl.when(s < NX - 1)
@@ -774,18 +783,20 @@
             pltpu.VMEM((1, D), F32),
             pltpu.VMEM((ROWS, HD), F32),
             pltpu.VMEM((ROWS, HD), F32),
-            pltpu.VMEM((32, 256, 768), BF),
+            pltpu.VMEM((2, 16, 256, 768), BF),
             pltpu.VMEM((QW, 2048), BF),
             pltpu.VMEM((2, 4, vocab, 1024), BF),
             pltpu.VMEM((2, NM, 16, 2048), BF),
-            pltpu.VMEM((NY, NM, ROWS + 16, 256), BF),
+            pltpu.VMEM((NY, NM, ROWS, 256), BF),
+            pltpu.VMEM((NY, NZ, ROWS + 16, 256), BF),
             pltpu.VMEM((NY, ROWS + 16, 256), BF),
             pltpu.VMEM((1, 256), F32),
             pltpu.VMEM((NY, ROWS, 256), BF),
             pltpu.VMEM((4 * ROWS, ROWS), F32),
             pltpu.VMEM((256, 256), BF),
             pltpu.VMEM((ROWS, 128), F32),
-            pltpu.VMEM((ROWS, 768), F32),
+            pltpu.VMEM((2, ROWS, 896), F32),
+            pltpu.VMEM((ROWS, 896), F32),
             pltpu.VMEM((NY, ROWS, 256), BF),
             pltpu.VMEM((NY, ROWS, QW), BF),
             pltpu.VMEM((NY, NZ, ROWS, 256), BF),
@@ -801,6 +812,8 @@
             pltpu.VMEM((NM, 16, 128), F32),
             pltpu.VMEM((NX, 16, 128), F32),
             dma((20,)),
+            dma((3,)), dma((3,)),
+            dma, dma,
             dma, dma,
             dma((2, 8)), dma((2, 8)),
             dma((5,)), dma((5,)),
@@ -818,8 +831,8 @@
                                       transcendentals=300_000),
     )(
         embeds, lengths, source, targets, attn_gain, final_gain.reshape(1, D), jnp.asarray(cos), jnp.asarray(sin),
-        w_query.reshape(32, 256, 512), w_key.reshape(32, 256, 128),
-        w_value.reshape(32, 256, 128), w_out.reshape(512, 2048), head,
+        w_query.reshape(16, 2, 256, 512), w_key.reshape(16, 2, 256, 128),
+        w_value.reshape(16, 2, 256, 128), w_out.reshape(512, 2048), head,
     )
     return (stats[0], stats[1])
 

time: 154 us -> 153 us (level)
    pallas_call x1, Pallas kernels: 152 us -> 151 us  [per_device(): pl.pallas_call(kernel, out_shape=jax.ShapeDtypeStruct((2, 2, 32), F32), i...]
where the time goes in v9:
time: 153 us
  Pallas kernels  151 us (99%)
    pallas_call x1, Pallas kernels, per_device(): pl.pallas_call(kernel, out_shape=jax.ShapeDtypeStruct((2, 2, 32), F32), i...  151 us

profile of v9, /device:TPU:1, one launch (start us, length us, event | category | flops | bytes accessed | tf_op | source)
XLA Modules:
  0.0 152.7 jit_solution(7530070264830492651)
XLA Ops:
  0.6 150.8 %shard_map.140 = f32[2,2,32]{2,1,0:T(2,128)} custom-call(bf16[2,4,8192]{2,1,0:T(4,128)(2,1)} %emb_in.1, s32[8]{0:T(128)} %live.1, s32[8]{0:T(128)} %source_of.1, s32[8,32]{1,0:T(8,128)} %targets_in.1, f32[1,8192]{1,0:T(1,128)} %gain.1, f32[1,8192]{1,0:T(1,128)} %bitcast.13, f32[64,128]{1,0:T(8,128)} %constant.4.clone.cosine_in, ...), custom_call_target="tpu_custom_call" | custom-call | flops 8000000000 | bytes 24000000 | tf_op jit(solution)/shard_map/pallas_call | solution.py:774
  151.4 1.2 slice_bitcast_fusion

commit v10 on v9

--- a/solution.py
+++ b/solution.py
@@ -30,8 +30,8 @@
 def kernel(
     emb_in, live, source_of, targets_in, gain, fgain_in, cosine_in, sine_in, wq, wk, wv, wo, head,
     out,
-    emb, targets, gains, fgain, cosine, sine, W, WO, HEAD, EB, XE, X, G, NG, RX, MASK, SEL, SS, QA, QR, R, C, PS, PR, PO, ZS, ZR, HP, Y, LT, STO, SA, SB, SC,
-    w_sem, sw_s, sw_r, qr_s, qr_r, ng_s, ng_r, eb_s, eb_r, hop_s, hop_r, ag_s, ag_r, res_s, res_r, ctx_s, ctx_r, ps_s, ps_r,
+    emb, targets, gains, fgain, cosine, sine, W, WO, HEAD, EB, XE, X, RX, MASK, SEL, SS, QA, QR, R, C, PS, PR, PO, ZS, ZR, HP, Y, LT, STO, SA, SB,
+    w_sem, sw_s, sw_r, qr_s, qr_r, eb_s, eb_r, hop_s, hop_r, ag_s, ag_r, res_s, res_r, ctx_s, ctx_r, ps_s, ps_r,
     zz_s, zz_r, y_s, y_r, st_s, st_r,
 ):
     d = lax.axis_index("dp")
@@ -67,6 +67,7 @@
         partners.append((d, s, zother(k)))
         partners.append((ypeer(k), (s + 1) % NX, m))
         partners.append((ypeer(k), (s + 3) % NX, m))
+        partners.append((ypeer(k), (s + 2) % NX, m))
     partners.append(here)
     for dev in partners:
         pl.semaphore_signal(barrier, inc=1, device_id=dev, device_id_type=MESH)
@@ -137,6 +138,32 @@
         packed_at = jnp.where(position < live_of(slot), first_row(slot) + position, 999)[0:1]
         SEL[...] = (lax.broadcasted_iota(jnp.int32, (256, 256), 0) == packed_at).astype(F32).astype(BF)
 
+        @pl.when(s > 0)
+        def _():
+            for n in range(3):
+                load(n, 0).wait()
+                swap(n).wait_recv()
+            for copy in small[1:2]:
+                copy.wait()
+            diagonal = (lax.broadcasted_iota(jnp.int32, (256, 256), 0)
+                        == lax.broadcasted_iota(jnp.int32, (256, 256), 1))
+
+            def scale(i, _):
+                cols = lane((i // NZ) * 2048 + ((i % NZ) * 2 + c) * 256, 256)
+                column = jnp.sum(jnp.where(diagonal, gains[:, cols], 0.0), axis=1, keepdims=True)
+                for which in range(2):
+                    W.at[which, i][...] = (W[which, i].astype(F32) * column).astype(BF)
+                return 0
+
+            lax.fori_loop(0, 16, scale, 0)
+
+        @pl.when(s == 0)
+        def _():
+            for copy in small[1:2]:
+                copy.wait()
+        for copy in small[2:]:
+            copy.wait()
+
     def row_slot(lanes):
         return (lanes // 64) * 2 + (lanes // 4) % 2, ((lanes // 8) % 8) * 4 + lanes % 4
 
@@ -152,13 +179,8 @@
 
     pl.semaphore_wait(barrier, len(partners))
 
-    def next_gain():
-        return rcopy(gain.at[:, lane(d * 2048 + m * 256, 256)], NG, ng_s, ng_r,
-                     (d, (s + 3) % NX, m))
-
     @pl.when(s > 0)
     def _():
-        next_gain().start()
         for n in range(3):
             swap(n).start()
 
@@ -178,10 +200,10 @@
         return rcopy(EB.at[q, mk], EB.at[q, mk], eb_s.at[q, 4 + k], eb_r.at[q, mk], here)
 
     def hop(g):
-        return rcopy(G.at[g], X.at[d, z], hop_s.at[g], hop_r.at[d], (g, (s + 1) % NX, m))
+        return rcopy(HP.at[g], X.at[d, z], hop_s.at[g], hop_r.at[d], (g, (s + 1) % NX, m))
 
     def hop_in(g):
-        return rcopy(G.at[g], X.at[g, z], hop_s.at[g], hop_r.at[g], (g, (s + 1) % NX, m))
+        return rcopy(HP.at[g], X.at[g, z], hop_s.at[g], hop_r.at[g], here)
 
     def hop_raw():
         return rcopy(HP, R, hop_s.at[4], hop_r.at[4], (d, (s + 1) % NX, m))
@@ -281,33 +303,34 @@
                 g = ypeer(k)
                 for j in (1, 3, 2):
                     ag_z_in(g, j).wait_recv()
-                return jnp.concatenate([X[g, zz, 0:ROWS] for zz in range(NZ)], axis=1)
+                return jnp.concatenate([X[g, zz] for zz in range(NZ)], axis=1)
 
             def both(k, start=False):
                 x = columns(k)
                 multiply(x, 1, ypeer(k), 1, start)
                 multiply(x, 0, ypeer(k), 0, start)
 
-            for n in range(3):
-                load(n, 0).wait()
-                swap(n).wait_recv()
+            def squares_of(k):
+                total = jnp.zeros((ROWS, 128), F32)
+                for zz in range(NZ):
+                    x = X[ypeer(k), zz].astype(F32)
+                    square = x * x
+                    total = total + square[:, 0:128] + square[:, 128:256]
+                return total
+
             arrived(0)
             arrived(3)
             arrived(1)
             arrived(2)
             both(0, True)
+            squares = squares_of(0)
             both(3)
+            squares = squares + squares_of(3)
             both(1)
+            squares = squares + squares_of(1)
             x = columns(2)
             multiply(x, 1, ypeer(2), 1)
-            total = jnp.zeros((16, 256), F32)
-            for zz in range(NZ):
-                for g in range(NY):
-                    total = total + X[g, zz, ROWS:ROWS + 16].astype(F32)
-            total = total[0:1, 0:128] + total[1:2, 0:128]
-            mine = (lax.broadcasted_iota(jnp.int32, (ROWS, 128), 1)
-                    == lax.broadcasted_iota(jnp.int32, (ROWS, 128), 0))
-            squares = jnp.where(mine, total, 0.0)
+            squares = squares + squares_of(2)
             QA.at[1][:, 768:896] = squares
             sums_out().start()
             multiply(x, 0, ypeer(2), 0)
@@ -362,22 +385,7 @@
             for k in (1, 3, 2):
                 zred(g, k).wait_recv()
                 total = total + ZR[g, k].astype(F32)
-            hidden = total.astype(BF)
-            HP.at[g][...] = hidden
-            wide = hidden.astype(F32)
-            G.at[g][0:ROWS, :] = (wide * NG[...]).astype(BF)
-            square = wide * wide
-            top = square.astype(BF)
-            rest = (square - top.astype(F32)).astype(BF)
-            ones = jnp.ones((16, 256), BF)
-            nt = (((1,), (1,)), ((), ()))
-            sums = (lax.dot_general(ones, top, nt, preferred_element_type=F32)
-                    + lax.dot_general(ones, rest, nt, preferred_element_type=F32))
-            top = sums.astype(BF).astype(F32)
-            row = lax.broadcasted_iota(jnp.int32, (16, ROWS), 0)
-            packed = jnp.where(row == 0, top, jnp.where(row == 1, sums - top, 0.0))
-            packed = jnp.concatenate([packed, jnp.zeros_like(packed)], axis=1).astype(BF)
-            G.at[g][ROWS:ROWS + 16, 0:128] = packed
+            HP.at[g][...] = total.astype(BF)
 
             @pl.when(s < NX - 1)
             def _():
@@ -393,10 +401,6 @@
         @pl.when(s > 0)
         def _():
             hop_raw().wait_recv()
-
-        @pl.when(s < NX - 1)
-        def _():
-            next_gain().wait_recv()
 
         pair(d)
         for k in (1, 3):
@@ -610,8 +614,6 @@
                 (eb_z(q, k) if k else eb_fwd(q, 0)).start()
 
     prepare()
-    for copy in small[1:]:
-        copy.wait()
     STO[...] = jnp.zeros_like(STO)
     lax.fori_loop(0, 5, step, 0)
 
@@ -630,12 +632,18 @@
     def stacked(highest, summed, picked):
         return jnp.concatenate([highest, summed, picked, jnp.zeros_like(picked)], axis=0)
 
-    def st_y(k):
-        return rcopy(SA.at[d], SA.at[d], st_s.at[0, k], st_r.at[0, d], (ypeer(k), s, m))
-
-    def st_y_in(k):
-        g = ypeer(k)
-        return rcopy(SA.at[g], SA.at[g], st_s.at[0, k], st_r.at[0, g], (g, s, m))
+    pairs = [(j, k) for j in range(NX) for k in range(NY) if j or k]
+
+    def st_yx(n):
+        j, k = pairs[n]
+        mine = s * NY + d
+        return rcopy(SA.at[mine], SA.at[mine], st_s.at[0, n], st_r.at[0, mine],
+                     (ypeer(k), (s + j) % NX, m))
+
+    def st_yx_in(n):
+        j, k = pairs[n]
+        other = ((s + j) % NX) * NY + ypeer(k)
+        return rcopy(SA.at[other], SA.at[other], st_s.at[0, n], st_r.at[0, other], here)
 
     def m_of(k):
         return (m + k) % NM
@@ -647,29 +655,17 @@
         mm = m_of(k)
         return rcopy(SB.at[mm], SB.at[mm], st_s.at[1, k], st_r.at[1, mm], (d, s, mm))
 
-    def st_x(k):
-        return rcopy(SC.at[s], SC.at[s], st_s.at[2, k], st_r.at[2, s], (d, (s + k) % NX, m))
-
-    def st_x_in(k):
-        ss = (s + k) % NX
-        return rcopy(SC.at[ss], SC.at[ss], st_s.at[2, k], st_r.at[2, ss], (d, ss, m))
-
-    SA.at[d][...] = STO[...]
-    for k in (2, 1, 3):
-        st_y(k).start()
-    for k in (1, 3, 2):
-        st_y_in(k).wait_recv()
-    SB.at[m][...] = stacked(*merge(SA, NY))
+    SA.at[s * NY + d][...] = STO[...]
+    for n in range(15):
+        st_yx(n).start()
+    for n in range(15):
+        st_yx_in(n).wait_recv()
+    SB.at[m][...] = stacked(*merge(SA, NX * NY))
     for k in (4, 3, 5, 2, 6, 1, 7):
         st_m(k).start()
     for k in (1, 7, 2, 6, 3, 5, 4):
         st_m_in(k).wait_recv()
-    SC.at[s][...] = stacked(*merge(SB, NM))
-    for k in (2, 1, 3):
-        st_x(k).start()
-    for k in (1, 3, 2):
-        st_x_in(k).wait_recv()
-    highest, summed, picked = merge(SC, NX)
+    highest, summed, picked = merge(SB, NM)
     logprob = picked - (highest + jnp.log(summed))
     terms = []
     for e in range(2):
@@ -716,7 +712,6 @@
         sums_out().wait_send()
         for n in range(3):
             swap(n).wait_send()
-        next_gain().wait_send()
 
     @pl.when(s < NX - 1)
     def _():
@@ -730,8 +725,8 @@
         part(g).wait_send()
     for k in range(1, 4):
         ctx(k).wait_send()
-        st_y(k).wait_send()
-        st_x(k).wait_send()
+    for n in range(15):
+        st_yx(n).wait_send()
     for k in range(1, 8):
         st_m(k).wait_send()
     for b in range(2):
@@ -788,9 +783,7 @@
             pltpu.VMEM((2, 4, vocab, 1024), BF),
             pltpu.VMEM((2, NM, 16, 2048), BF),
             pltpu.VMEM((NY, NM, ROWS, 256), BF),
-            pltpu.VMEM((NY, NZ, ROWS + 16, 256), BF),
-            pltpu.VMEM((NY, ROWS + 16, 256), BF),
-            pltpu.VMEM((1, 256), F32),
+            pltpu.VMEM((NY, NZ, ROWS, 256), BF),
             pltpu.VMEM((NY, ROWS, 256), BF),
             pltpu.VMEM((4 * ROWS, ROWS), F32),
             pltpu.VMEM((256, 256), BF),
@@ -808,12 +801,10 @@
             pltpu.VMEM((2, 2, 4, 4, 256, 256), BF),
             pltpu.VMEM((vocab, 256), F32),
             pltpu.VMEM((16, 128), F32),
-            pltpu.VMEM((NY, 16, 128), F32),
+            pltpu.VMEM((NX * NY, 16, 128), F32),
             pltpu.VMEM((NM, 16, 128), F32),
-            pltpu.VMEM((NX, 16, 128), F32),
             dma((20,)),
             dma((3,)), dma((3,)),
-            dma, dma,
             dma, dma,
             dma((2, 8)), dma((2, 8)),
             dma((5,)), dma((5,)),
@@ -823,7 +814,7 @@
             dma((4,)), dma((4,)),
             dma((4, 4)), dma((4, 4)),
             dma((2, 30)), dma((2, 22)),
-            dma((3, 8)), dma((3, 8)),
+            dma((2, 16)), dma((2, 16)),
         ],
         compiler_params=pltpu.CompilerParams(
             collective_id=0, has_side_effects=True, vmem_limit_bytes=60 * 1024 * 1024),

time: 153 us -> 149 us (0.974)
  Pallas kernels: 151 us -> 147 us
    pallas_call x1, Pallas kernels: 151 us -> 147 us  [per_device(): pl.pallas_call(kernel, out_shape=jax.ShapeDtypeStruct((2, 2, 32), F32), i...]
where the time goes in v10:
time: 149 us
  Pallas kernels  147 us (99%)
    pallas_call x1, Pallas kernels, per_device(): pl.pallas_call(kernel, out_shape=jax.ShapeDtypeStruct((2, 2, 32), F32), i...  147 us

profile of v10, /device:TPU:1, one launch (start us, length us, event | category | flops | bytes accessed | tf_op | source)
XLA Modules:
  0.0 148.8 jit_solution(9463062884455607055)
XLA Ops:
  0.6 146.9 %shard_map.140 = f32[2,2,32]{2,1,0:T(2,128)} custom-call(bf16[2,4,8192]{2,1,0:T(4,128)(2,1)} %emb_in.1, s32[8]{0:T(128)} %live.1, s32[8]{0:T(128)} %source_of.1, s32[8,32]{1,0:T(8,128)} %targets_in.1, f32[1,8192]{1,0:T(1,128)} %gain.1, f32[1,8192]{1,0:T(1,128)} %bitcast.13, f32[64,128]{1,0:T(8,128)} %constant.4.clone.cosine_in, ...), custom_call_target="tpu_custom_call" | custom-call | flops 8000000000 | bytes 24000000 | tf_op jit(solution)/shard_map/pallas_call | solution.py:769
  147.6 1.2 slice_bitcast_fusion

commit v11 on v10

--- a/solution.py
+++ b/solution.py
@@ -14,8 +14,6 @@
 NZ = 4
 NM = 8
 ROWS = 64
-LIVE = 192
-PIECE = LIVE + 16
 D = 8192
 QW = 512
 MESH = pl.DeviceIdType.MESH
@@ -30,7 +28,7 @@
 def kernel(
     emb_in, live, source_of, targets_in, gain, fgain_in, cosine_in, sine_in, wq, wk, wv, wo, head,
     out,
-    emb, targets, gains, fgain, cosine, sine, W, WO, HEAD, EB, XE, X, RX, MASK, SEL, SS, QA, QR, R, C, PS, PR, PO, ZS, ZR, HP, Y, LT, STO, SA, SB,
+    emb, targets, gains, fgain, cosine, sine, W, WO, HEAD, EB, XE, X, RX, MASK, SS, QA, QR, R, C, PS, PR, PO, ZS, ZR, HP, Y, LT, SQ, STO, SA, SB,
     w_sem, sw_s, sw_r, qr_s, qr_r, eb_s, eb_r, hop_s, hop_r, ag_s, ag_r, res_s, res_r, ctx_s, ctx_r, ps_s, ps_r,
     zz_s, zz_r, y_s, y_r, st_s, st_r,
 ):
@@ -122,22 +120,6 @@
         allowed = (slot_q == slot_k) & (pos_k <= pos_q) & (pos_k < live_k)
         MASK[...] = jnp.where(allowed, F32(0.0), F32(-1e30))
 
-        def first_row(slot):
-            start = jnp.zeros_like(slot)
-            for other in range(8):
-                start = start + jnp.where(slot > other, live[other], 0)
-            return start
-
-        def live_of(slot):
-            count = jnp.zeros_like(slot)
-            for other in range(8):
-                count = count + jnp.where(slot == other, live[other], 0)
-            return count
-
-        slot, position = row_slot(lax.broadcasted_iota(jnp.int32, (8, 256), 1))
-        packed_at = jnp.where(position < live_of(slot), first_row(slot) + position, 999)[0:1]
-        SEL[...] = (lax.broadcasted_iota(jnp.int32, (256, 256), 0) == packed_at).astype(F32).astype(BF)
-
         @pl.when(s > 0)
         def _():
             for n in range(3):
@@ -163,6 +145,27 @@
                 copy.wait()
         for copy in small[2:]:
             copy.wait()
+
+        @pl.when(s > 0)
+        def _():
+            scale_head()
+
+    def scale_head():
+        head_load.wait()
+
+        def off(n):
+            return jnp.where(n == 0, 0, jnp.where(n == 1, 3, jnp.where(n == 2, 1, 2)))
+
+        def scale(n, _):
+            cc, j, i = n // 16, (n // 4) % 4, n % 4
+            g = jnp.where(cc == 0, off(i), off(j))
+            zz = jnp.where(cc == 0, off(j), off(i))
+            col = ((d + g) % NY) * 2048 + ((z + zz) % NZ) * 512 + cc * 256
+            block = HEAD.at[cc, j, :, lane(i * 256, 256)]
+            block[...] = (block[...].astype(F32) * fgain[:, lane(col, 256)]).astype(BF)
+            return 0
+
+        lax.fori_loop(0, 32, scale, 0)
 
     def row_slot(lanes):
         return (lanes // 64) * 2 + (lanes // 4) % 2, ((lanes // 8) % 8) * 4 + lanes % 4
@@ -408,44 +411,38 @@
             project(ypeer(k))
         pair(ypeer(1))
         pair(ypeer(3))
+        def own_chunk(k):
+            @pl.when(s == NX - 1)
+            def _():
+                stage_own(1, k, True)
+                if k >= 1:
+                    stage_first(1, k - 1)
+                if k >= 2:
+                    stage_second(1, k - 2)
+
         total_of(d)
+        own_chunk(0)
         ctx_in(2).wait_recv()
         project(ypeer(2))
         total_of(ypeer(1))
         pair(ypeer(2))
+        own_chunk(1)
         total_of(ypeer(3))
+        own_chunk(2)
         total_of(ypeer(2))
+        own_chunk(3)
 
         @pl.when(s < NX - 1)
         def _():
             hop_raw().start()
 
-        @pl.when(s % 2 == 1)
-        def _():
-            emit(s // 2)
-
-    def emit(b):
-        mine = Y.at[b, c, 0, 0]
-        nt = (((1,), (1,)), ((), ()))
-        wide = HP[...].reshape(NY * ROWS, 256).astype(F32)
-        cols = lane(d * 2048 + m * 256, 256)
-        scaled = (wide * fgain[:, cols]).astype(BF)
-        live_rows = jnp.dot(SEL[0:LIVE], scaled, preferred_element_type=F32)
-        mine[0:LIVE, :] = live_rows.astype(BF)
-        square = wide * wide
-        top = square.astype(BF)
-        rest = (square - top.astype(F32)).astype(BF)
-        ones = jnp.ones((16, 256), BF)
-        sums = (lax.dot_general(ones, top, nt, preferred_element_type=F32)
-                + lax.dot_general(ones, rest, nt, preferred_element_type=F32))
-        top = sums.astype(BF).astype(F32)
-        row = lax.broadcasted_iota(jnp.int32, (16, NY * ROWS), 0)
-        packed = jnp.where(row == 0, top, jnp.where(row == 1, sums - top, 0.0)).astype(BF)
-        squares = lax.dot_general(packed, SEL[...], nt, preferred_element_type=F32)
-        mine[LIVE:PIECE, :] = squares.astype(BF)
-        for k in (2, 1, 3):
-            y_x(b, k).start()
-        spread_own(b)
+        @pl.when(s == 1)
+        def _():
+            def body(k, _):
+                stage_own(0, k, True)
+                return 0
+
+            lax.fori_loop(0, 4, body, 0)
 
     def first_dev(k):
         return (jnp.where(c == 0, ypeer(k), d), s, jnp.where(c == 0, m, zpeer(k)))
@@ -453,127 +450,179 @@
     def second_dev(k):
         return (jnp.where(c == 0, d, ypeer(k)), s, jnp.where(c == 0, zpeer(k), m))
 
-    def ycopy(src, dst, b, i, j, dev):
-        return rcopy(src, dst, y_s.at[b, i], y_r.at[b, j], dev)
-
-    def own(b, rows):
-        return Y.at[b, c, 0, 0, rows]
-
-    def y_x(b, k):
-        return ycopy(own(b, whole), own(b, whole), b, k, 0, (d, (s + k) % NX, m))
-
-    whole = pl.ds(0, PIECE)
-
-    def y_first(b, k):
-        slot = (1, 3, 2)[k - 1]
-        return ycopy(own(b, whole), Y.at[b, c, 0, slot, whole], b, 5 + k, slot, first_dev(k))
+    def ycopy(src, dst, b, k, i, j, dev):
+        return rcopy(src, dst, y_s.at[b, k, i], y_r.at[b, k, j], dev)
+
+    def y_x(b, k, n):
+        ref = Y.at[b, k, c, 0, 0]
+        return ycopy(ref, ref, b, k, n, 0, (d, (s + n) % NX, m))
+
+    def y_first(b, k, n):
+        slot = (1, 3, 2)[n - 1]
+        return ycopy(Y.at[b, k, c, 0, 0], Y.at[b, k, c, 0, slot], b, k, 3 + n, slot, first_dev(n))
 
     sets = (pl.ds(0, 1), pl.ds(1, 2), pl.ds(3, 1))
 
-    def y_second(b, part_no, k):
-        slot = 1 if k == 1 else 2
-        return ycopy(Y.at[b, c, 0, sets[part_no], whole], Y.at[b, c, slot, sets[part_no], whole],
-                     b, 11 + part_no * 2 + (slot - 1), 1 + 3 * slot + part_no, second_dev(k))
-
-    def y_second_relay(b, i):
-        slot, k = (1, 1) if i < 2 else (2, 3)
-        return ycopy(Y.at[b, c, slot, i, whole], Y.at[b, c, 3, i, whole],
-                     b, 17 + i, 10 + i, second_dev(k))
+    def y_second(b, k, part_no, n):
+        slot = 1 if n == 1 else 2
+        return ycopy(Y.at[b, k, c, 0, sets[part_no]], Y.at[b, k, c, slot, sets[part_no]], b, k,
+                     7 + part_no * 2 + (slot - 1), 1 + 3 * slot + part_no, second_dev(n))
+
+    def y_relay(b, k, half):
+        slot, n = ((1, 1), (2, 3))[half]
+        two = pl.ds(2 * half, 2)
+        return ycopy(Y.at[b, k, c, slot, two], Y.at[b, k, c, 3, two], b, k, 13 + half, 10 + half,
+                     second_dev(n))
 
     forwards = ((0, 0, 1), (0, 1, 2), (0, 3, 1), (1, 0, 4), (2, 0, 4), (3, 0, 2), (3, 2, 2))
 
-    def y_fwd(b, n, who):
+    def y_fwd(b, k, n, who):
         j, i, size = forwards[n]
-        ref = Y.at[b, who, j, pl.ds(i, size), whole]
-        return ycopy(ref, ref, b, 21 + n, 14 + n, here)
-
-    def spread_own(b):
-        for k in (2, 1, 3):
-            y_first(b, k).start()
-        for k in (1, 3):
-            y_second(b, 0, k).start()
-        y_fwd(b, 0, c).start()
-
-    def dots(b, cc, j, start):
-        pieces = jnp.concatenate([Y[b, cc, j, i, 0:256, :] for i in range(4)], axis=1)
-        term = lax.dot_general(HEAD[cc, j], pieces, (((1,), (1,)), ((), ())),
-                               preferred_element_type=F32)
-        LT[...] = term if start else LT[...] + term
+        ref = Y.at[b, k, who, j, pl.ds(i, size)]
+        return ycopy(ref, ref, b, k, 15 + n, 12 + n, here)
+
+    def chunk_order(step):
+        return jnp.where(step == 3, 2, jnp.where(step == 2, 3, step))
+
+    def stage_own(b, k, source):
+        if source:
+            Y.at[b, k, c, 0, 0][...] = HP[(d + chunk_order(k)) % NY]
+            for n in (2, 1, 3):
+                y_x(b, k, n).start()
+        else:
+            y_x(b, k, 1).wait_recv()
+        for n in (2, 1, 3):
+            y_first(b, k, n).start()
+        for n in (1, 3):
+            y_second(b, k, 0, n).start()
+        y_fwd(b, k, 0, c).start()
+
+    def stage_first(b, k):
+        y_first(b, k, 1).wait_recv()
+        y_first(b, k, 3).wait_recv()
+        for n in (1, 3):
+            y_second(b, k, 1, n).start()
+        y_fwd(b, k, 1, c).start()
+        y_first(b, k, 2).wait_recv()
+        for n in (1, 3):
+            y_second(b, k, 2, n).start()
+        y_fwd(b, k, 2, c).start()
+
+    def stage_second(b, k):
+        for part_no in (0, 1):
+            y_second(b, k, part_no, 1).wait_recv()
+        y_relay(b, k, 0).start()
+        for part_no in (1, 2):
+            y_second(b, k, part_no, 3).wait_recv()
+        y_relay(b, k, 1).start()
+        y_second(b, k, 2, 1).wait_recv()
+        y_fwd(b, k, 3, c).start()
+        y_second(b, k, 0, 3).wait_recv()
+        y_fwd(b, k, 4, c).start()
+
+    def stage_last(b, k):
+        for half in range(2):
+            y_relay(b, k, half).wait_recv()
+            y_fwd(b, k, 5 + half, c).start()
+        for n in range(7):
+            y_fwd(b, k, n, 1 - c).wait_recv()
+
+    def dots(b, cc, j):
+        blocks = []
+        for g in range(NY):
+            row = []
+            total = jnp.zeros((ROWS, 128), F32)
+            for i in range(4):
+                off_j = jnp.where(j == 0, 0, jnp.where(j == 1, 3, jnp.where(j == 2, 1, 2)))
+                sender = (d + jnp.where(cc == 0, (0, 3, 1, 2)[i], off_j)) % NY
+                k = chunk_order((g - sender + NY) % NY)
+                x = Y[b, k, cc, j, i]
+                row.append(x)
+                wide = x.astype(F32)
+                square = wide * wide
+                total = total + square[:, 0:128] + square[:, 128:256]
+            SQ.at[b, g][...] += total
+            blocks.append(jnp.concatenate(row, axis=1))
+        pieces = jnp.concatenate(blocks, axis=0)
+        LT.at[b][...] += lax.dot_general(HEAD[cc, j], pieces, (((1,), (1,)), ((), ())),
+                                         preferred_element_type=F32)
 
     def wanted_rows():
         slot, position = row_slot(lax.broadcasted_iota(jnp.int32, (32, 256), 1))
         place = (position == lax.broadcasted_iota(jnp.int32, (32, 256), 0)).astype(BF)
         tokens = targets[...]
-        nt = (((1,), (1,)), ((), ()))
         keep = slot[0:8] == lax.broadcasted_iota(jnp.int32, (8, 256), 0)
         parts = []
         for term in (tokens // 256, tokens % 256):
             every = jnp.dot(term.astype(F32).astype(BF), place, preferred_element_type=F32)
-            mine = jnp.sum(jnp.where(keep, every, 0.0), axis=0, keepdims=True)
-            spread = jnp.broadcast_to(mine, (16, 256)).astype(BF)
-            parts.append(lax.dot_general(spread, SEL[...], nt, preferred_element_type=F32)[0:1])
+            parts.append(jnp.sum(jnp.where(keep, every, 0.0), axis=0, keepdims=True))
         return parts[0] * 256.0 + parts[1]
 
     def gather(b):
         source = 2 * b + 1
-
-        @pl.when(s != source)
-        def _():
-            y_x(b, 1).wait_recv()
-            spread_own(b)
-
-        y_first(b, 1).wait_recv()
-        y_first(b, 3).wait_recv()
-        for k in (1, 3):
-            y_second(b, 1, k).start()
-        y_fwd(b, 1, c).start()
-        y_second(b, 0, 1).wait_recv()
-        y_second_relay(b, 0).start()
-        y_second(b, 0, 3).wait_recv()
-        y_first(b, 2).wait_recv()
-        for k in (1, 3):
-            y_second(b, 2, k).start()
-        y_fwd(b, 2, c).start()
-        y_second(b, 1, 1).wait_recv()
-        y_second_relay(b, 1).start()
-        y_second(b, 1, 3).wait_recv()
-        y_second_relay(b, 2).start()
-        y_second(b, 2, 3).wait_recv()
-        y_second_relay(b, 3).start()
-        y_fwd(b, 4, c).start()
-        y_second(b, 2, 1).wait_recv()
-        y_fwd(b, 3, c).start()
+        final = (b == 1) & (s == NX - 1)
+        late = (b == 1) & (s >= 2)
+
+        def body(t, _):
+            @pl.when((t < 4) & (s != source))
+            def _():
+                stage_own(b, t, False)
+
+            @pl.when((t >= 1) & (t < 5) & ((t == 4) | jnp.logical_not(final)))
+            def _():
+                stage_first(b, t - 1)
+
+            @pl.when((t >= 2) & (t < 6) & ((t >= 4) | jnp.logical_not(final)))
+            def _():
+                stage_second(b, t - 2)
+
+            @pl.when(t >= 3)
+            def _():
+                stage_last(b, t - 3)
+
+            @pl.when(late & (t == 0))
+            def _():
+                stage_last(0, 3)
+
+            @pl.when(late & (t >= 1) & (t < 5))
+            def _():
+                j = chunk_order(t - 1)
+                dots(0, c, j)
+                dots(0, 1 - c, j)
+            return 0
+
+        lax.fori_loop(0, 6, body, 0)
 
     def finish(b):
-        dots(b, c, 0, True)
-        for n in range(3):
-            y_fwd(b, n, 1 - c).wait_recv()
-        dots(b, 1 - c, 0, False)
-        dots(b, c, 2, False)
-        dots(b, c, 1, False)
-        y_second_relay(b, 0).wait_recv()
-        y_second_relay(b, 1).wait_recv()
-        y_fwd(b, 5, c).start()
-        y_fwd(b, 4, 1 - c).wait_recv()
-        dots(b, 1 - c, 2, False)
-        y_second_relay(b, 2).wait_recv()
-        y_second_relay(b, 3).wait_recv()
-        y_fwd(b, 6, c).start()
-        y_fwd(b, 3, 1 - c).wait_recv()
-        dots(b, 1 - c, 1, False)
-        dots(b, c, 3, False)
-        y_fwd(b, 5, 1 - c).wait_recv()
-        y_fwd(b, 6, 1 - c).wait_recv()
-        dots(b, 1 - c, 3, False)
-
-        extra = jnp.zeros((16, 256), F32)
-        for cc in range(2):
-            for j in range(4):
-                for i in range(4):
-                    extra = extra + Y[b, cc, j, i, LIVE:PIECE, :].astype(F32)
-        sums = jnp.sum(extra, axis=0, keepdims=True)
+        @pl.when((b == 1) | (s < 2))
+        def _():
+            dots(b, c, 0)
+            for n in range(3):
+                y_fwd(b, 3, n, 1 - c).wait_recv()
+            dots(b, 1 - c, 0)
+            dots(b, c, 1)
+            dots(b, c, 2)
+            for half in range(2):
+                y_relay(b, 3, half).wait_recv()
+                y_fwd(b, 3, 5 + half, c).start()
+            for n in (3, 4):
+                y_fwd(b, 3, n, 1 - c).wait_recv()
+            dots(b, 1 - c, 1)
+            dots(b, 1 - c, 2)
+            dots(b, c, 3)
+            for n in (5, 6):
+                y_fwd(b, 3, n, 1 - c).wait_recv()
+            dots(b, 1 - c, 3)
+
+        squares = SQ[b].reshape(NY * ROWS, 128)
+        top = squares.astype(BF)
+        rest = (squares - top.astype(F32)).astype(BF)
+        ones = jnp.ones((16, 128), BF)
+        nt = (((1,), (1,)), ((), ()))
+        sums = (lax.dot_general(ones, top, nt, preferred_element_type=F32)
+                + lax.dot_general(ones, rest, nt, preferred_element_type=F32))[0:1]
         r = lax.rsqrt(sums * (1.0 / D) + EPS)
-        logits = LT[...] * r
+        logits = LT[b] * r
         highest = jnp.max(logits, axis=0, keepdims=True)
         summed = jnp.sum(jnp.exp(logits - highest), axis=0, keepdims=True)
         vocab = HEAD.shape[2]
@@ -581,9 +630,7 @@
         index = (lax.broadcasted_iota(jnp.int32, logits.shape, 0) + first).astype(F32)
         wanted = wanted_rows()
         picked = jnp.sum(jnp.where(index == wanted, logits, 0.0), axis=0, keepdims=True)
-        alive = lax.broadcasted_iota(jnp.int32, (1, 256), 1) < LIVE
         for n, value in enumerate((highest, summed, picked)):
-            value = jnp.where(alive, value, 1.0)
             for half in range(2):
                 STO[pl.ds(n * 4 + b * 2 + half, 1), :] = value[:, half * 128:half * 128 + 128]
 
@@ -595,15 +642,15 @@
         def _():
             layer()
 
-        @pl.when(jnp.where(last, (t == 0) | (t == 2), (t == 1) | (t == 3)))
-        def _():
-            gather(jnp.where(t < 2, 0, 1))
-
-        @pl.when(jnp.where(last, t >= 3, (t == 2) | (t == 4)))
-        def _():
-            @pl.when(t == jnp.where(last, 3, 2))
+        @pl.when(jnp.where(last, (t == 0) | (t == 2), (t == 1) | (t == jnp.where(s < 2, 3, 2))))
+        def _():
+            gather(jnp.where((t == 0) | (t == 1), 0, 1))
+
+        @pl.when((t == 4) | (t == jnp.where(s < 2, 2, 3)))
+        def _():
+            @pl.when((t == 2) & (s == 0))
             def _():
-                head_load.wait()
+                scale_head()
             finish(jnp.where(t == 4, 1, 0))
         return 0
 
@@ -615,6 +662,8 @@
 
     prepare()
     STO[...] = jnp.zeros_like(STO)
+    SQ[...] = jnp.zeros_like(SQ)
+    LT[...] = jnp.zeros_like(LT)
     lax.fori_loop(0, 5, step, 0)
 
     def merge(ref, count):
@@ -679,15 +728,13 @@
     for j, term in enumerate(terms):
         stack = jnp.where(row == j, term, stack)
     stack = stack.astype(BF)
-    index = lax.broadcasted_iota(jnp.int32, (256, 32), 0)
+    slot, position = row_slot(lax.broadcasted_iota(jnp.int32, (256, 32), 0))
     place = lax.broadcasted_iota(jnp.int32, (256, 32), 1)
     results = []
     for i in range(2):
         chosen = source_of[2 * d + i]
-        start = 0
-        for other in range(8):
-            start = start + jnp.where(chosen > other, live[other], 0)
-        take = ((index == start + place) & (place < live[chosen])).astype(F32).astype(BF)
+        take = ((slot == chosen) & (position == place)
+                & (place < live[chosen])).astype(F32).astype(BF)
         got = jnp.dot(stack, take, preferred_element_type=F32)
         results.append([got[j:j + 1] + got[j + 1:j + 2] + got[j + 2:j + 3] for j in (0, 3)])
     for e in range(2):
@@ -729,21 +776,26 @@
         st_yx(n).wait_send()
     for k in range(1, 8):
         st_m(k).wait_send()
-    for b in range(2):
+    def sent(n, _):
+        b, k = n // 4, n % 4
+
         @pl.when(s == 2 * b + 1)
         def _():
-            for k in (1, 2, 3):
-                y_x(b, k).wait_send()
-
-        for k in (1, 2, 3):
-            y_first(b, k).wait_send()
-        for k in (1, 3):
-            for n in range(3):
-                y_second(b, n, k).wait_send()
-        for i in range(4):
-            y_second_relay(b, i).wait_send()
-        for n in range(7):
-            y_fwd(b, n, c).wait_send()
+            for j in (1, 2, 3):
+                y_x(b, k, j).wait_send()
+
+        for j in (1, 2, 3):
+            y_first(b, k, j).wait_send()
+        for j in (1, 3):
+            for part_no in range(3):
+                y_second(b, k, part_no, j).wait_send()
+        for half in range(2):
+            y_relay(b, k, half).wait_send()
+        for j in range(7):
+            y_fwd(b, k, j, c).wait_send()
+        return 0
+
+    lax.fori_loop(0, 8, sent, 0)
 
 
 def tables():
@@ -786,7 +838,6 @@
             pltpu.VMEM((NY, NZ, ROWS, 256), BF),
             pltpu.VMEM((NY, ROWS, 256), BF),
             pltpu.VMEM((4 * ROWS, ROWS), F32),
-            pltpu.VMEM((256, 256), BF),
             pltpu.VMEM((ROWS, 128), F32),
             pltpu.VMEM((2, ROWS, 896), F32),
             pltpu.VMEM((ROWS, 896), F32),
@@ -798,8 +849,9 @@
             pltpu.VMEM((NY, NZ, ROWS, 256), BF),
             pltpu.VMEM((NY, NZ, ROWS, 256), BF),
             pltpu.VMEM((NY, ROWS, 256), BF),
-            pltpu.VMEM((2, 2, 4, 4, 256, 256), BF),
-            pltpu.VMEM((vocab, 256), F32),
+            pltpu.VMEM((2, 4, 2, 4, 4, ROWS, 256), BF),
+            pltpu.VMEM((2, vocab, 256), F32),
+            pltpu.VMEM((2, NY, ROWS, 128), F32),
             pltpu.VMEM((16, 128), F32),
             pltpu.VMEM((NX * NY, 16, 128), F32),
             pltpu.VMEM((NM, 16, 128), F32),
@@ -813,7 +865,7 @@
             dma((4,)), dma((4,)),
             dma((4,)), dma((4,)),
             dma((4, 4)), dma((4, 4)),
-            dma((2, 30)), dma((2, 22)),
+            dma((2, 4, 22)), dma((2, 4, 19)),
             dma((2, 16)), dma((2, 16)),
         ],
         compiler_params=pltpu.CompilerParams(

time: 149 us -> 149 us (level)
  no operation moved by 1% of the time
where the time goes in v11:
time: 149 us
  Pallas kernels  147 us (99%)
    pallas_call x1, Pallas kernels, per_device(): pl.pallas_call(kernel, out_shape=jax.ShapeDtypeStruct((2, 2, 32), F32), i...  147 us

profile of v11, /device:TPU:1, one launch (start us, length us, event | category | flops | bytes accessed | tf_op | source)
XLA Modules:
  0.0 149.1 jit_solution(15514221962454134612)
XLA Ops:
  0.6 147.2 %shard_map.140 = f32[2,2,32]{2,1,0:T(2,128)} custom-call(bf16[2,4,8192]{2,1,0:T(4,128)(2,1)} %emb_in.1, s32[8]{0:T(128)} %live.1, s32[8]{0:T(128)} %source_of.1, s32[8,32]{1,0:T(8,128)} %targets_in.1, f32[1,8192]{1,0:T(1,128)} %gain.1, f32[1,8192]{1,0:T(1,128)} %bitcast.13, f32[64,128]{1,0:T(8,128)} %constant.4.clone.cosine_in, ...), custom_call_target="tpu_custom_call" | custom-call | flops 8000000000 | bytes 24000000 | tf_op jit(solution)/shard_map/pallas_call | solution.py:821
  147.9 1.2 slice_bitcast_fusion

commit v12 on v11

--- a/solution.py
+++ b/solution.py
@@ -28,7 +28,7 @@
 def kernel(
     emb_in, live, source_of, targets_in, gain, fgain_in, cosine_in, sine_in, wq, wk, wv, wo, head,
     out,
-    emb, targets, gains, fgain, cosine, sine, W, WO, HEAD, EB, XE, X, RX, MASK, SS, QA, QR, R, C, PS, PR, PO, ZS, ZR, HP, Y, LT, SQ, STO, SA, SB,
+    emb, targets, gains, fgain, cosine, sine, W, WO, HEAD, EB, XE, X, RX, MASK, SS, QA, QR, R, C, PS, PR, PO, ZS, ZR, HP, Y, LT, SQ, WANT, TAKE, STO, SA, SB,
     w_sem, sw_s, sw_r, qr_s, qr_r, eb_s, eb_r, hop_s, hop_r, ag_s, ag_r, res_s, res_r, ctx_s, ctx_r, ps_s, ps_r,
     zz_s, zz_r, y_s, y_r, st_s, st_r,
 ):
@@ -100,6 +100,20 @@
 
     head_load = pltpu.make_async_copy(HEAD, HEAD, w_sem.at[13])
 
+    def row_slot(lanes):
+        return (lanes // 64) * 2 + (lanes // 4) % 2, ((lanes // 8) % 8) * 4 + lanes % 4
+
+    def wanted_rows():
+        slot, position = row_slot(lax.broadcasted_iota(jnp.int32, (32, 256), 1))
+        place = (position == lax.broadcasted_iota(jnp.int32, (32, 256), 0)).astype(BF)
+        tokens = targets[...]
+        keep = slot[0:8] == lax.broadcasted_iota(jnp.int32, (8, 256), 0)
+        parts = []
+        for term in (tokens // 256, tokens % 256):
+            every = jnp.dot(term.astype(F32).astype(BF), place, preferred_element_type=F32)
+            parts.append(jnp.sum(jnp.where(keep, every, 0.0), axis=0, keepdims=True))
+        return parts[0] * 256.0 + parts[1]
+
     def prepare():
         wo_load.start()
         offsets = (0, 3, 1, 2)
@@ -146,6 +160,14 @@
         for copy in small[2:]:
             copy.wait()
 
+        WANT[...] = jnp.broadcast_to(wanted_rows(), WANT.shape)
+        slot, position = row_slot(lax.broadcasted_iota(jnp.int32, (256, 32), 0))
+        place = lax.broadcasted_iota(jnp.int32, (256, 32), 1)
+        for i in range(2):
+            chosen = source_of[2 * d + i]
+            TAKE.at[i][...] = ((slot == chosen) & (position == place)
+                               & (place < live[chosen])).astype(F32).astype(BF)
+
         @pl.when(s > 0)
         def _():
             scale_head()
@@ -166,9 +188,6 @@
             return 0
 
         lax.fori_loop(0, 32, scale, 0)
-
-    def row_slot(lanes):
-        return (lanes // 64) * 2 + (lanes // 4) % 2, ((lanes // 8) % 8) * 4 + lanes % 4
 
     small[0].wait()
 
@@ -547,16 +566,54 @@
         LT.at[b][...] += lax.dot_general(HEAD[cc, j], pieces, (((1,), (1,)), ((), ())),
                                          preferred_element_type=F32)
 
-    def wanted_rows():
-        slot, position = row_slot(lax.broadcasted_iota(jnp.int32, (32, 256), 1))
-        place = (position == lax.broadcasted_iota(jnp.int32, (32, 256), 0)).astype(BF)
-        tokens = targets[...]
-        keep = slot[0:8] == lax.broadcasted_iota(jnp.int32, (8, 256), 0)
-        parts = []
-        for term in (tokens // 256, tokens % 256):
-            every = jnp.dot(term.astype(F32).astype(BF), place, preferred_element_type=F32)
-            parts.append(jnp.sum(jnp.where(keep, every, 0.0), axis=0, keepdims=True))
-        return parts[0] * 256.0 + parts[1]
+    def layer_sent():
+        @pl.when(s == 0)
+        def _():
+            for q in range(2):
+                for k in range(1, 4):
+                    eb_z(q, k).wait_send()
+                for k in range(4):
+                    eb_fwd(q, k).wait_send()
+            for k in range(1, 4):
+                res(k).wait_send()
+
+        @pl.when(s > 0)
+        def _():
+            for g in range(NY):
+                for k in range(1, 4):
+                    ag_z(g, k).wait_send()
+            sums_out().wait_send()
+            for n in range(3):
+                swap(n).wait_send()
+
+        @pl.when(s < NX - 1)
+        def _():
+            for g in range(NY):
+                hop(g).wait_send()
+            hop_raw().wait_send()
+
+        for g in range(NY):
+            for k in range(1, 4):
+                zred(g, k).wait_send()
+            part(g).wait_send()
+        for k in range(1, 4):
+            ctx(k).wait_send()
+
+    def chunk_sent(b, k, source):
+        @pl.when(s == source)
+        def _():
+            for j in (1, 2, 3):
+                y_x(b, k, j).wait_send()
+
+        for j in (1, 2, 3):
+            y_first(b, k, j).wait_send()
+        for j in (1, 3):
+            for part_no in range(3):
+                y_second(b, k, part_no, j).wait_send()
+        for half in range(2):
+            y_relay(b, k, half).wait_send()
+        for j in range(7):
+            y_fwd(b, k, j, c).wait_send()
 
     def gather(b):
         source = 2 * b + 1
@@ -579,10 +636,12 @@
             @pl.when(t >= 3)
             def _():
                 stage_last(b, t - 3)
+                chunk_sent(b, t - 3, source)
 
             @pl.when(late & (t == 0))
             def _():
                 stage_last(0, 3)
+                chunk_sent(0, 3, 1)
 
             @pl.when(late & (t >= 1) & (t < 5))
             def _():
@@ -614,6 +673,10 @@
                 y_fwd(b, 3, n, 1 - c).wait_recv()
             dots(b, 1 - c, 3)
 
+        @pl.when((b == 0) & (s < 2))
+        def _():
+            chunk_sent(0, 3, 1)
+
         squares = SQ[b].reshape(NY * ROWS, 128)
         top = squares.astype(BF)
         rest = (squares - top.astype(F32)).astype(BF)
@@ -628,7 +691,7 @@
         vocab = HEAD.shape[2]
         first = ((d * NX + s) * NM + m) * vocab
         index = (lax.broadcasted_iota(jnp.int32, logits.shape, 0) + first).astype(F32)
-        wanted = wanted_rows()
+        wanted = WANT[0:1, :]
         picked = jnp.sum(jnp.where(index == wanted, logits, 0.0), axis=0, keepdims=True)
         for n, value in enumerate((highest, summed, picked)):
             for half in range(2):
@@ -707,11 +770,15 @@
     SA.at[s * NY + d][...] = STO[...]
     for n in range(15):
         st_yx(n).start()
+    layer_sent()
+    chunk_sent(1, 3, NX - 1)
     for n in range(15):
         st_yx_in(n).wait_recv()
     SB.at[m][...] = stacked(*merge(SA, NX * NY))
     for k in (4, 3, 5, 2, 6, 1, 7):
         st_m(k).start()
+    for n in range(15):
+        st_yx(n).wait_send()
     for k in (1, 7, 2, 6, 3, 5, 4):
         st_m_in(k).wait_recv()
     highest, summed, picked = merge(SB, NM)
@@ -728,74 +795,15 @@
     for j, term in enumerate(terms):
         stack = jnp.where(row == j, term, stack)
     stack = stack.astype(BF)
-    slot, position = row_slot(lax.broadcasted_iota(jnp.int32, (256, 32), 0))
-    place = lax.broadcasted_iota(jnp.int32, (256, 32), 1)
     results = []
     for i in range(2):
-        chosen = source_of[2 * d + i]
-        take = ((slot == chosen) & (position == place)
-                & (place < live[chosen])).astype(F32).astype(BF)
-        got = jnp.dot(stack, take, preferred_element_type=F32)
+        got = jnp.dot(stack, TAKE[i], preferred_element_type=F32)
         results.append([got[j:j + 1] + got[j + 1:j + 2] + got[j + 2:j + 3] for j in (0, 3)])
     for e in range(2):
         first = lax.broadcasted_iota(jnp.int32, (2, 32), 0) == 0
         out.at[e][...] = jnp.where(first, results[0][e], results[1][e])
-
-    @pl.when(s == 0)
-    def _():
-        for q in range(2):
-            for k in range(1, 4):
-                eb_z(q, k).wait_send()
-            for k in range(4):
-                eb_fwd(q, k).wait_send()
-        for k in range(1, 4):
-            res(k).wait_send()
-
-    @pl.when(s > 0)
-    def _():
-        for g in range(NY):
-            for k in range(1, 4):
-                ag_z(g, k).wait_send()
-        sums_out().wait_send()
-        for n in range(3):
-            swap(n).wait_send()
-
-    @pl.when(s < NX - 1)
-    def _():
-        for g in range(NY):
-            hop(g).wait_send()
-        hop_raw().wait_send()
-
-    for g in range(NY):
-        for k in range(1, 4):
-            zred(g, k).wait_send()
-        part(g).wait_send()
-    for k in range(1, 4):
-        ctx(k).wait_send()
-    for n in range(15):
-        st_yx(n).wait_send()
     for k in range(1, 8):
         st_m(k).wait_send()
-    def sent(n, _):
-        b, k = n // 4, n % 4
-
-        @pl.when(s == 2 * b + 1)
-        def _():
-            for j in (1, 2, 3):
-                y_x(b, k, j).wait_send()
-
-        for j in (1, 2, 3):
-            y_first(b, k, j).wait_send()
-        for j in (1, 3):
-            for part_no in range(3):
-                y_second(b, k, part_no, j).wait_send()
-        for half in range(2):
-            y_relay(b, k, half).wait_send()
-        for j in range(7):
-            y_fwd(b, k, j, c).wait_send()
-        return 0
-
-    lax.fori_loop(0, 8, sent, 0)
 
 
 def tables():
@@ -852,6 +860,8 @@
             pltpu.VMEM((2, 4, 2, 4, 4, ROWS, 256), BF),
             pltpu.VMEM((2, vocab, 256), F32),
             pltpu.VMEM((2, NY, ROWS, 128), F32),
+            pltpu.VMEM((8, 256), F32),
+            pltpu.VMEM((2, 256, 32), BF),
             pltpu.VMEM((16, 128), F32),
             pltpu.VMEM((NX * NY, 16, 128), F32),
             pltpu.VMEM((NM, 16, 128), F32),

time: 149 us -> 150 us (level)
  no operation moved by 1% of the time
where the time goes in v12:
time: 150 us
  Pallas kernels  148 us (99%)
    pallas_call x1, Pallas kernels, per_device(): pl.pallas_call(kernel, out_shape=jax.ShapeDtypeStruct((2, 2, 32), F32), i...  148 us

profile of v12, /device:TPU:1, one launch (start us, length us, event | category | flops | bytes accessed | tf_op | source)
XLA Modules:
  0.0 149.5 jit_solution(9163499061523652878)
XLA Ops:
  0.6 147.6 %shard_map.140 = f32[2,2,32]{2,1,0:T(2,128)} custom-call(bf16[2,4,8192]{2,1,0:T(4,128)(2,1)} %emb_in.1, s32[8]{0:T(128)} %live.1, s32[8]{0:T(128)} %source_of.1, s32[8,32]{1,0:T(8,128)} %targets_in.1, f32[1,8192]{1,0:T(1,128)} %gain.1, f32[1,8192]{1,0:T(1,128)} %bitcast.13, f32[64,128]{1,0:T(8,128)} %constant.4.clone.cosine_in, ...), custom_call_target="tpu_custom_call" | custom-call | flops 8000000000 | bytes 24000000 | tf_op jit(solution)/shard_map/pallas_call | solution.py:829
  148.3 1.2 slice_bitcast_fusion

commit v13 on v12

--- a/solution.py
+++ b/solution.py
@@ -493,6 +493,10 @@
         return ycopy(Y.at[b, k, c, slot, two], Y.at[b, k, c, 3, two], b, k, 13 + half, 10 + half,
                      second_dev(n))
 
+    def y_far(k):
+        ref = Y.at[0, k, c, 3]
+        return ycopy(ref, ref, 0, k, 22, 19, (d, NX - 1 - s, m))
+
     forwards = ((0, 0, 1), (0, 1, 2), (0, 3, 1), (1, 0, 4), (2, 0, 4), (3, 0, 2), (3, 2, 2))
 
     def y_fwd(b, k, n, who):
@@ -527,22 +531,48 @@
             y_second(b, k, 2, n).start()
         y_fwd(b, k, 2, c).start()
 
+    def relaying(b):
+        return (b == 1) | (s < 2)
+
     def stage_second(b, k):
         for part_no in (0, 1):
             y_second(b, k, part_no, 1).wait_recv()
-        y_relay(b, k, 0).start()
+
+        @pl.when(relaying(b))
+        def _():
+            y_relay(b, k, 0).start()
+
         for part_no in (1, 2):
             y_second(b, k, part_no, 3).wait_recv()
-        y_relay(b, k, 1).start()
+
+        @pl.when(relaying(b))
+        def _():
+            y_relay(b, k, 1).start()
+
         y_second(b, k, 2, 1).wait_recv()
         y_fwd(b, k, 3, c).start()
         y_second(b, k, 0, 3).wait_recv()
         y_fwd(b, k, 4, c).start()
 
+    def opposite(b, k):
+        @pl.when(relaying(b))
+        def _():
+            for half in range(2):
+                y_relay(b, k, half).wait_recv()
+                y_fwd(b, k, 5 + half, c).start()
+
+            @pl.when(b == 0)
+            def _():
+                y_far(k).start()
+
+        @pl.when(jnp.logical_not(relaying(b)))
+        def _():
+            y_far(k).wait_recv()
+            for half in range(2):
+                y_fwd(b, k, 5 + half, c).start()
+
     def stage_last(b, k):
-        for half in range(2):
-            y_relay(b, k, half).wait_recv()
-            y_fwd(b, k, 5 + half, c).start()
+        opposite(b, k)
         for n in range(7):
             y_fwd(b, k, n, 1 - c).wait_recv()
 
@@ -610,8 +640,16 @@
         for j in (1, 3):
             for part_no in range(3):
                 y_second(b, k, part_no, j).wait_send()
-        for half in range(2):
-            y_relay(b, k, half).wait_send()
+
+        @pl.when(relaying(b))
+        def _():
+            for half in range(2):
+                y_relay(b, k, half).wait_send()
+
+            @pl.when(b == 0)
+            def _():
+                y_far(k).wait_send()
+
         for j in range(7):
             y_fwd(b, k, j, c).wait_send()
 
@@ -633,15 +671,19 @@
             def _():
                 stage_second(b, t - 2)
 
-            @pl.when(t >= 3)
+            @pl.when((t >= 3) & relaying(b))
             def _():
                 stage_last(b, t - 3)
                 chunk_sent(b, t - 3, source)
 
             @pl.when(late & (t == 0))
             def _():
-                stage_last(0, 3)
-                chunk_sent(0, 3, 1)
+                def rest(k, _):
+                    stage_last(0, k)
+                    chunk_sent(0, k, 1)
+                    return 0
+
+                lax.fori_loop(0, 4, rest, 0)
 
             @pl.when(late & (t >= 1) & (t < 5))
             def _():
@@ -661,9 +703,7 @@
             dots(b, 1 - c, 0)
             dots(b, c, 1)
             dots(b, c, 2)
-            for half in range(2):
-                y_relay(b, 3, half).wait_recv()
-                y_fwd(b, 3, 5 + half, c).start()
+            opposite(b, 3)
             for n in (3, 4):
                 y_fwd(b, 3, n, 1 - c).wait_recv()
             dots(b, 1 - c, 1)
@@ -875,7 +915,7 @@
             dma((4,)), dma((4,)),
             dma((4,)), dma((4,)),
             dma((4, 4)), dma((4, 4)),
-            dma((2, 4, 22)), dma((2, 4, 19)),
+            dma((2, 4, 23)), dma((2, 4, 20)),
             dma((2, 16)), dma((2, 16)),
         ],
         compiler_params=pltpu.CompilerParams(

time: 150 us -> 151 us (level)
    pallas_call x1, Pallas kernels: 148 us -> 149 us  [per_device(): pl.pallas_call(kernel, out_shape=jax.ShapeDtypeStruct((2, 2, 32), F32), i...]
where the time goes in v13:
time: 151 us
  Pallas kernels  149 us (99%)
    pallas_call x1, Pallas kernels, per_device(): pl.pallas_call(kernel, out_shape=jax.ShapeDtypeStruct((2, 2, 32), F32), i...  149 us

profile of v13, /device:TPU:1, one launch (start us, length us, event | category | flops | bytes accessed | tf_op | source)
XLA Modules:
  0.0 151.3 jit_solution(9813650969030603242)
XLA Ops:
  0.6 149.5 %shard_map.140 = f32[2,2,32]{2,1,0:T(2,128)} custom-call(bf16[2,4,8192]{2,1,0:T(4,128)(2,1)} %emb_in.1, s32[8]{0:T(128)} %live.1, s32[8]{0:T(128)} %source_of.1, s32[8,32]{1,0:T(8,128)} %targets_in.1, f32[1,8192]{1,0:T(1,128)} %gain.1, f32[1,8192]{1,0:T(1,128)} %bitcast.13, f32[64,128]{1,0:T(8,128)} %constant.4.clone.cosine_in, ...), custom_call_target="tpu_custom_call" | custom-call | flops 8000000000 | bytes 24000000 | tf_op jit(solution)/shard_map/pallas_call | solution.py:869
  150.1 1.2 slice_bitcast_fusion

commit v14 on v12

--- a/solution.py
+++ b/solution.py
@@ -539,10 +539,12 @@
         y_second(b, k, 0, 3).wait_recv()
         y_fwd(b, k, 4, c).start()
 
-    def stage_last(b, k):
+    def opposite(b, k):
         for half in range(2):
             y_relay(b, k, half).wait_recv()
             y_fwd(b, k, 5 + half, c).start()
+
+    def sibling_in(b, k):
         for n in range(7):
             y_fwd(b, k, n, 1 - c).wait_recv()
 
@@ -615,68 +617,89 @@
         for j in range(7):
             y_fwd(b, k, j, c).wait_send()
 
+    def each(count, do):
+        def body(k, _):
+            do(k)
+            return 0
+
+        lax.fori_loop(0, count, body, 0)
+
+    def exit_dots(k):
+        j = chunk_order(k)
+        dots(0, c, j)
+        dots(0, 1 - c, j)
+
     def gather(b):
         source = 2 * b + 1
         final = (b == 1) & (s == NX - 1)
-        late = (b == 1) & (s >= 2)
+        others = jnp.logical_not(final)
 
         def body(t, _):
             @pl.when((t < 4) & (s != source))
             def _():
                 stage_own(b, t, False)
 
-            @pl.when((t >= 1) & (t < 5) & ((t == 4) | jnp.logical_not(final)))
+            @pl.when((t >= 1) & (t < 5) & ((t == 4) | others))
             def _():
                 stage_first(b, t - 1)
 
-            @pl.when((t >= 2) & (t < 6) & ((t >= 4) | jnp.logical_not(final)))
+            @pl.when((t >= 2) & (t < 6) & ((t >= 4) | others))
             def _():
                 stage_second(b, t - 2)
 
-            @pl.when(t >= 3)
+            @pl.when((t >= 3) & ((b == 0) | (t < 6)) & others)
             def _():
-                stage_last(b, t - 3)
-                chunk_sent(b, t - 3, source)
-
-            @pl.when(late & (t == 0))
+                opposite(b, t - 3)
+
+            @pl.when((b == 1) & (s == 2) & (t == 1))
             def _():
-                stage_last(0, 3)
-                chunk_sent(0, 3, 1)
-
-            @pl.when(late & (t >= 1) & (t < 5))
+                each(4, lambda k: sibling_in(0, k))
+
+            @pl.when((b == 1) & (s == 2) & (t >= 2) & (t < 6))
             def _():
-                j = chunk_order(t - 1)
-                dots(0, c, j)
-                dots(0, 1 - c, j)
+                exit_dots(t - 2)
             return 0
 
-        lax.fori_loop(0, 6, body, 0)
+        lax.fori_loop(0, 7, body, 0)
+
+        @pl.when(final)
+        def _():
+            each(3, lambda k: opposite(1, k))
+            each(4, lambda k: sibling_in(0, k))
+            each(4, exit_dots)
 
     def finish(b):
-        @pl.when((b == 1) | (s < 2))
-        def _():
-            dots(b, c, 0)
-            for n in range(3):
-                y_fwd(b, 3, n, 1 - c).wait_recv()
-            dots(b, 1 - c, 0)
-            dots(b, c, 1)
-            dots(b, c, 2)
-            for half in range(2):
-                y_relay(b, 3, half).wait_recv()
-                y_fwd(b, 3, 5 + half, c).start()
-            for n in (3, 4):
-                y_fwd(b, 3, n, 1 - c).wait_recv()
-            dots(b, 1 - c, 1)
-            dots(b, 1 - c, 2)
-            dots(b, c, 3)
-            for n in (5, 6):
-                y_fwd(b, 3, n, 1 - c).wait_recv()
-            dots(b, 1 - c, 3)
-
         @pl.when((b == 0) & (s < 2))
         def _():
-            chunk_sent(0, 3, 1)
-
+            each(4, lambda k: sibling_in(0, k))
+            each(4, exit_dots)
+
+        @pl.when(b == 1)
+        def _():
+            dots_order()
+
+        softmax(b)
+
+    def dots_order():
+        b = 1
+        dots(b, c, 0)
+        each(3, lambda k: sibling_in(1, k))
+        for n in range(3):
+            y_fwd(b, 3, n, 1 - c).wait_recv()
+        dots(b, 1 - c, 0)
+        opposite(b, 3)
+        dots(b, c, 1)
+        dots(b, c, 2)
+        for n in (3, 4):
+            y_fwd(b, 3, n, 1 - c).wait_recv()
+        dots(b, 1 - c, 1)
+        dots(b, 1 - c, 2)
+        dots(b, c, 3)
+        for n in (5, 6):
+            y_fwd(b, 3, n, 1 - c).wait_recv()
+        dots(b, 1 - c, 3)
+
+    def softmax(b):
         squares = SQ[b].reshape(NY * ROWS, 128)
         top = squares.astype(BF)
         rest = (squares - top.astype(F32)).astype(BF)
@@ -771,7 +794,8 @@
     for n in range(15):
         st_yx(n).start()
     layer_sent()
-    chunk_sent(1, 3, NX - 1)
+    each(4, lambda k: chunk_sent(0, k, 1))
+    each(4, lambda k: chunk_sent(1, k, NX - 1))
     for n in range(15):
         st_yx_in(n).wait_recv()
     SB.at[m][...] = stacked(*merge(SA, NX * NY))

time: 150 us -> 149 us (level)
  no operation moved by 1% of the time
where the time goes in v14:
time: 149 us
  Pallas kernels  147 us (99%)
    pallas_call x1, Pallas kernels, per_device(): pl.pallas_call(kernel, out_shape=jax.ShapeDtypeStruct((2, 2, 32), F32), i...  147 us

profile of v14, /device:TPU:1, one launch (start us, length us, event | category | flops | bytes accessed | tf_op | source)
XLA Modules:
  0.0 148.8 jit_solution(14521936833569181573)
XLA Ops:
  0.6 146.9 %shard_map.140 = f32[2,2,32]{2,1,0:T(2,128)} custom-call(bf16[2,4,8192]{2,1,0:T(4,128)(2,1)} %emb_in.1, s32[8]{0:T(128)} %live.1, s32[8]{0:T(128)} %source_of.1, s32[8,32]{1,0:T(8,128)} %targets_in.1, f32[1,8192]{1,0:T(1,128)} %gain.1, f32[1,8192]{1,0:T(1,128)} %bitcast.13, f32[64,128]{1,0:T(8,128)} %constant.4.clone.cosine_in, ...), custom_call_target="tpu_custom_call" | custom-call | flops 8000000000 | bytes 24000000 | tf_op jit(solution)/shard_map/pallas_call | solution.py:853
  147.6 1.2 slice_bitcast_fusion

commit v15 on v14

--- a/solution.py
+++ b/solution.py
@@ -430,26 +430,42 @@
             project(ypeer(k))
         pair(ypeer(1))
         pair(ypeer(3))
-        def own_chunk(k):
+        def in_last(do):
             @pl.when(s == NX - 1)
             def _():
-                stage_own(1, k, True)
-                if k >= 1:
-                    stage_first(1, k - 1)
-                if k >= 2:
-                    stage_second(1, k - 2)
+                do()
 
         total_of(d)
-        own_chunk(0)
+        in_last(lambda: own_x(1, 0))
         ctx_in(2).wait_recv()
         project(ypeer(2))
         total_of(ypeer(1))
+        in_last(lambda: own_x(1, 1))
         pair(ypeer(2))
-        own_chunk(1)
+
+        def first_two():
+            spread(1, 0)
+            spread(1, 1)
+
+        in_last(first_two)
         total_of(ypeer(3))
-        own_chunk(2)
+
+        def third():
+            own_x(1, 2)
+            spread(1, 2)
+
+        in_last(third)
         total_of(ypeer(2))
-        own_chunk(3)
+
+        def rest():
+            own_x(1, 3)
+            spread(1, 3)
+            for k in range(3):
+                stage_first(1, k)
+            for k in range(2):
+                stage_second(1, k)
+
+        in_last(rest)
 
         @pl.when(s < NX - 1)
         def _():
@@ -458,7 +474,8 @@
         @pl.when(s == 1)
         def _():
             def body(k, _):
-                stage_own(0, k, True)
+                own_x(0, k)
+                spread(0, k)
                 return 0
 
             lax.fori_loop(0, 4, body, 0)
@@ -503,13 +520,12 @@
     def chunk_order(step):
         return jnp.where(step == 3, 2, jnp.where(step == 2, 3, step))
 
-    def stage_own(b, k, source):
-        if source:
-            Y.at[b, k, c, 0, 0][...] = HP[(d + chunk_order(k)) % NY]
-            for n in (2, 1, 3):
-                y_x(b, k, n).start()
-        else:
-            y_x(b, k, 1).wait_recv()
+    def own_x(b, k):
+        Y.at[b, k, c, 0, 0][...] = HP[(d + chunk_order(k)) % NY]
+        for n in (2, 1, 3):
+            y_x(b, k, n).start()
+
+    def spread(b, k):
         for n in (2, 1, 3):
             y_first(b, k, n).start()
         for n in (1, 3):
@@ -637,7 +653,8 @@
         def body(t, _):
             @pl.when((t < 4) & (s != source))
             def _():
-                stage_own(b, t, False)
+                y_x(b, t, 1).wait_recv()
+                spread(b, t)
 
             @pl.when((t >= 1) & (t < 5) & ((t == 4) | others))
             def _():

time: 149 us -> 150 us (level)
  no operation moved by 1% of the time
where the time goes in v15:
time: 150 us
  Pallas kernels  148 us (99%)
    pallas_call x1, Pallas kernels, per_device(): pl.pallas_call(kernel, out_shape=jax.ShapeDtypeStruct((2, 2, 32), F32), i...  148 us

profile of v15, /device:TPU:1, one launch (start us, length us, event | category | flops | bytes accessed | tf_op | source)
XLA Modules:
  0.0 149.6 jit_solution(17239864576161901784)
XLA Ops:
  0.6 147.7 %shard_map.140 = f32[2,2,32]{2,1,0:T(2,128)} custom-call(bf16[2,4,8192]{2,1,0:T(4,128)(2,1)} %emb_in.1, s32[8]{0:T(128)} %live.1, s32[8]{0:T(128)} %source_of.1, s32[8,32]{1,0:T(8,128)} %targets_in.1, f32[1,8192]{1,0:T(1,128)} %gain.1, f32[1,8192]{1,0:T(1,128)} %bitcast.13, f32[64,128]{1,0:T(8,128)} %constant.4.clone.cosine_in, ...), custom_call_target="tpu_custom_call" | custom-call | flops 8000000000 | bytes 24000000 | tf_op jit(solution)/shard_map/pallas_call | solution.py:870
  148.3 1.2 slice_bitcast_fusion

commit v16 on v15

--- a/solution.py
+++ b/solution.py
@@ -385,6 +385,11 @@
         for k in (2, 1, 3):
             ctx(k).start()
 
+        @pl.when(s == NX - 1)
+        def _():
+            each(4, lambda k: stage_second(0, k))
+
+
         wo_load.wait()
 
         def project(g):
@@ -464,6 +469,7 @@
                 stage_first(1, k)
             for k in range(2):
                 stage_second(1, k)
+            each(4, lambda k: opposite(0, k))
 
         in_last(rest)
 
@@ -660,11 +666,13 @@
             def _():
                 stage_first(b, t - 1)
 
-            @pl.when((t >= 2) & (t < 6) & ((t >= 4) | others))
+            early = (b == 0) & (s == NX - 1)
+
+            @pl.when((t >= 2) & (t < 6) & ((t >= 4) | others) & jnp.logical_not(early))
             def _():
                 stage_second(b, t - 2)
 
-            @pl.when((t >= 3) & ((b == 0) | (t < 6)) & others)
+            @pl.when((t >= 3) & ((b == 0) | (t < 6)) & others & jnp.logical_not(early))
             def _():
                 opposite(b, t - 3)
 

time: 150 us -> 150 us (level)
  no operation moved by 1% of the time
where the time goes in v16:
time: 150 us; the launch traced here: 149 us
  Pallas kernels  147 us (98%)
    pallas_call x1, Pallas kernels, per_device(): pl.pallas_call(kernel, out_shape=jax.ShapeDtypeStruct((2, 2, 32), F32), i...  147 us

profile of v16, /device:TPU:1, one launch (start us, length us, event | category | flops | bytes accessed | tf_op | source)
XLA Modules:
  0.0 149.4 jit_solution(17547016907294846609)
XLA Ops:
  0.6 147.5 %shard_map.140 = f32[2,2,32]{2,1,0:T(2,128)} custom-call(bf16[2,4,8192]{2,1,0:T(4,128)(2,1)} %emb_in.1, s32[8]{0:T(128)} %live.1, s32[8]{0:T(128)} %source_of.1, s32[8,32]{1,0:T(8,128)} %targets_in.1, f32[1,8192]{1,0:T(1,128)} %gain.1, f32[1,8192]{1,0:T(1,128)} %bitcast.13, f32[64,128]{1,0:T(8,128)} %constant.4.clone.cosine_in, ...), custom_call_target="tpu_custom_call" | custom-call | flops 8000000000 | bytes 24000000 | tf_op jit(solution)/shard_map/pallas_call | solution.py:878
  148.1 1.2 slice_bitcast_fusion

commit v17 on v15

--- a/solution.py
+++ b/solution.py
@@ -16,6 +16,7 @@
 ROWS = 64
 D = 8192
 QW = 512
+VOCAB_DEV = 512
 MESH = pl.DeviceIdType.MESH
 BF = jnp.bfloat16
 F32 = jnp.float32
@@ -28,8 +29,8 @@
 def kernel(
     emb_in, live, source_of, targets_in, gain, fgain_in, cosine_in, sine_in, wq, wk, wv, wo, head,
     out,
-    emb, targets, gains, fgain, cosine, sine, W, WO, HEAD, EB, XE, X, RX, MASK, SS, QA, QR, R, C, PS, PR, PO, ZS, ZR, HP, Y, LT, SQ, WANT, TAKE, STO, SA, SB,
-    w_sem, sw_s, sw_r, qr_s, qr_r, eb_s, eb_r, hop_s, hop_r, ag_s, ag_r, res_s, res_r, ctx_s, ctx_r, ps_s, ps_r,
+    emb, targets, gains, fgain, cosine, sine, W, WO, HEAD, EB, XE, X, RX, MASK, SS, QA, QR, R, C, PS, PR, PO, ZS, ZR, HP, Y, LT, LR, SQ, WANT, TAKE, STO, SA, SB,
+    w_sem, sw_s, sw_r, lt_s, lt_r, qr_s, qr_r, eb_s, eb_r, hop_s, hop_r, ag_s, ag_r, res_s, res_r, ctx_s, ctx_r, ps_s, ps_r,
     zz_s, zz_r, y_s, y_r, st_s, st_r,
 ):
     d = lax.axis_index("dp")
@@ -98,7 +99,16 @@
         for n in range(3):
             load(n, 1).start()
 
-    head_load = pltpu.make_async_copy(HEAD, HEAD, w_sem.at[13])
+    head_load = pltpu.make_async_copy(HEAD.at[0], HEAD.at[0], w_sem.at[13])
+    head_swap = rcopy(HEAD.at[1], HEAD.at[1], sw_s.at[3], sw_r.at[3], here)
+
+    def off(n):
+        return jnp.where(n == 0, 0, jnp.where(n == 1, 3, jnp.where(n == 2, 1, 2)))
+
+    def slot_columns(core, j, i):
+        g = jnp.where(core == 0, off(i), off(j))
+        zz = jnp.where(core == 0, off(j), off(i))
+        return lane(((d + g) % NY) * 2048 + ((z + zz) % NZ) * 512 + core * 256, 256)
 
     def row_slot(lanes):
         return (lanes // 64) * 2 + (lanes // 4) % 2, ((lanes // 8) % 8) * 4 + lanes % 4
@@ -116,15 +126,13 @@
 
     def prepare():
         wo_load.start()
-        offsets = (0, 3, 1, 2)
-        for cc in range(2):
-            for j in range(4):
-                for i in range(4):
-                    g, zz = (offsets[i], offsets[j]) if cc == 0 else (offsets[j], offsets[i])
-                    col = ypeer(g) * 2048 + ((z + zz) % NZ) * 512 + cc * 256
-                    pltpu.make_async_copy(head.at[:, lane(col, 256)],
-                                          HEAD.at[cc, j, :, i * 256:i * 256 + 256],
-                                          w_sem.at[13]).start()
+        for j in range(4):
+            for i in range(4):
+                there = pl.ds(i * 256, 256)
+                pltpu.make_async_copy(head.at[:, slot_columns(c, j, i)], HEAD.at[0, j, :, there],
+                                      w_sem.at[13]).start()
+                rcopy(head.at[:, slot_columns(1 - c, j, i)], HEAD.at[1, j, :, there],
+                      sw_s.at[3], sw_r.at[3], here).start()
         shape = (4 * ROWS, ROWS)
         rq = lax.broadcasted_iota(jnp.int32, shape, 0) % ROWS
         rk = lax.broadcasted_iota(jnp.int32, shape, 1)
@@ -174,17 +182,12 @@
 
     def scale_head():
         head_load.wait()
-
-        def off(n):
-            return jnp.where(n == 0, 0, jnp.where(n == 1, 3, jnp.where(n == 2, 1, 2)))
+        head_swap.wait_recv()
 
         def scale(n, _):
             cc, j, i = n // 16, (n // 4) % 4, n % 4
-            g = jnp.where(cc == 0, off(i), off(j))
-            zz = jnp.where(cc == 0, off(j), off(i))
-            col = ((d + g) % NY) * 2048 + ((z + zz) % NZ) * 512 + cc * 256
             block = HEAD.at[cc, j, :, lane(i * 256, 256)]
-            block[...] = (block[...].astype(F32) * fgain[:, lane(col, 256)]).astype(BF)
+            block[...] = (block[...].astype(F32) * fgain[:, slot_columns(c, j, i)]).astype(BF)
             return 0
 
         lax.fori_loop(0, 32, scale, 0)
@@ -490,38 +493,31 @@
         return rcopy(src, dst, y_s.at[b, k, i], y_r.at[b, k, j], dev)
 
     def y_x(b, k, n):
-        ref = Y.at[b, k, c, 0, 0]
+        ref = Y.at[b, k, 0, 0]
         return ycopy(ref, ref, b, k, n, 0, (d, (s + n) % NX, m))
 
     def y_first(b, k, n):
         slot = (1, 3, 2)[n - 1]
-        return ycopy(Y.at[b, k, c, 0, 0], Y.at[b, k, c, 0, slot], b, k, 3 + n, slot, first_dev(n))
+        return ycopy(Y.at[b, k, 0, 0], Y.at[b, k, 0, slot], b, k, 3 + n, slot, first_dev(n))
 
     sets = (pl.ds(0, 1), pl.ds(1, 2), pl.ds(3, 1))
 
     def y_second(b, k, part_no, n):
         slot = 1 if n == 1 else 2
-        return ycopy(Y.at[b, k, c, 0, sets[part_no]], Y.at[b, k, c, slot, sets[part_no]], b, k,
+        return ycopy(Y.at[b, k, 0, sets[part_no]], Y.at[b, k, slot, sets[part_no]], b, k,
                      7 + part_no * 2 + (slot - 1), 1 + 3 * slot + part_no, second_dev(n))
 
     def y_relay(b, k, half):
         slot, n = ((1, 1), (2, 3))[half]
         two = pl.ds(2 * half, 2)
-        return ycopy(Y.at[b, k, c, slot, two], Y.at[b, k, c, 3, two], b, k, 13 + half, 10 + half,
+        return ycopy(Y.at[b, k, slot, two], Y.at[b, k, 3, two], b, k, 13 + half, 10 + half,
                      second_dev(n))
-
-    forwards = ((0, 0, 1), (0, 1, 2), (0, 3, 1), (1, 0, 4), (2, 0, 4), (3, 0, 2), (3, 2, 2))
-
-    def y_fwd(b, k, n, who):
-        j, i, size = forwards[n]
-        ref = Y.at[b, k, who, j, pl.ds(i, size)]
-        return ycopy(ref, ref, b, k, 15 + n, 12 + n, here)
 
     def chunk_order(step):
         return jnp.where(step == 3, 2, jnp.where(step == 2, 3, step))
 
     def own_x(b, k):
-        Y.at[b, k, c, 0, 0][...] = HP[(d + chunk_order(k)) % NY]
+        Y.at[b, k, 0, 0][...] = HP[(d + chunk_order(k)) % NY]
         for n in (2, 1, 3):
             y_x(b, k, n).start()
 
@@ -530,18 +526,15 @@
             y_first(b, k, n).start()
         for n in (1, 3):
             y_second(b, k, 0, n).start()
-        y_fwd(b, k, 0, c).start()
 
     def stage_first(b, k):
         y_first(b, k, 1).wait_recv()
         y_first(b, k, 3).wait_recv()
         for n in (1, 3):
             y_second(b, k, 1, n).start()
-        y_fwd(b, k, 1, c).start()
         y_first(b, k, 2).wait_recv()
         for n in (1, 3):
             y_second(b, k, 2, n).start()
-        y_fwd(b, k, 2, c).start()
 
     def stage_second(b, k):
         for part_no in (0, 1):
@@ -551,29 +544,21 @@
             y_second(b, k, part_no, 3).wait_recv()
         y_relay(b, k, 1).start()
         y_second(b, k, 2, 1).wait_recv()
-        y_fwd(b, k, 3, c).start()
         y_second(b, k, 0, 3).wait_recv()
-        y_fwd(b, k, 4, c).start()
 
     def opposite(b, k):
         for half in range(2):
             y_relay(b, k, half).wait_recv()
-            y_fwd(b, k, 5 + half, c).start()
-
-    def sibling_in(b, k):
-        for n in range(7):
-            y_fwd(b, k, n, 1 - c).wait_recv()
-
-    def dots(b, cc, j):
+
+    def dots(b, j, send=False):
         blocks = []
         for g in range(NY):
             row = []
             total = jnp.zeros((ROWS, 128), F32)
             for i in range(4):
-                off_j = jnp.where(j == 0, 0, jnp.where(j == 1, 3, jnp.where(j == 2, 1, 2)))
-                sender = (d + jnp.where(cc == 0, (0, 3, 1, 2)[i], off_j)) % NY
+                sender = (d + jnp.where(c == 0, (0, 3, 1, 2)[i], off(j))) % NY
                 k = chunk_order((g - sender + NY) % NY)
-                x = Y[b, k, cc, j, i]
+                x = Y[b, k, j, i]
                 row.append(x)
                 wide = x.astype(F32)
                 square = wide * wide
@@ -581,8 +566,25 @@
             SQ.at[b, g][...] += total
             blocks.append(jnp.concatenate(row, axis=1))
         pieces = jnp.concatenate(blocks, axis=0)
-        LT.at[b][...] += lax.dot_general(HEAD[cc, j], pieces, (((1,), (1,)), ((), ())),
-                                         preferred_element_type=F32)
+        for which in (1, 0):
+            LT.at[b, which][0:VOCAB_DEV, :] += lax.dot_general(
+                HEAD[which, j], pieces, (((1,), (1,)), ((), ())), preferred_element_type=F32)
+            if send and which == 1:
+                exchange(b)
+
+    def swap_logits(b):
+        return rcopy(LT.at[b, 1], LR.at[b], lt_s.at[b], lt_r.at[b], here)
+
+    def exchange(b):
+        squares = SQ[b].reshape(NY * ROWS, 128)
+        top = squares.astype(BF)
+        rest = (squares - top.astype(F32)).astype(BF)
+        ones = jnp.ones((16, 128), BF)
+        nt = (((1,), (1,)), ((), ()))
+        sums = (lax.dot_general(ones, top, nt, preferred_element_type=F32)
+                + lax.dot_general(ones, rest, nt, preferred_element_type=F32))
+        LT.at[b, 1][VOCAB_DEV:VOCAB_DEV + 8, :] = sums[0:8]
+        swap_logits(b).start()
 
     def layer_sent():
         @pl.when(s == 0)
@@ -630,8 +632,6 @@
                 y_second(b, k, part_no, j).wait_send()
         for half in range(2):
             y_relay(b, k, half).wait_send()
-        for j in range(7):
-            y_fwd(b, k, j, c).wait_send()
 
     def each(count, do):
         def body(k, _):
@@ -640,10 +640,8 @@
 
         lax.fori_loop(0, count, body, 0)
 
-    def exit_dots(k):
-        j = chunk_order(k)
-        dots(0, c, j)
-        dots(0, 1 - c, j)
+    def exit_dots(n):
+        dots(0, n)
 
     def gather(b):
         source = 2 * b + 1
@@ -668,13 +666,13 @@
             def _():
                 opposite(b, t - 3)
 
-            @pl.when((b == 1) & (s == 2) & (t == 1))
-            def _():
-                each(4, lambda k: sibling_in(0, k))
-
             @pl.when((b == 1) & (s == 2) & (t >= 2) & (t < 6))
             def _():
                 exit_dots(t - 2)
+
+            @pl.when((b == 1) & (s == 2) & (t == 6))
+            def _():
+                exchange(0)
             return 0
 
         lax.fori_loop(0, 7, body, 0)
@@ -682,54 +680,37 @@
         @pl.when(final)
         def _():
             each(3, lambda k: opposite(1, k))
-            each(4, lambda k: sibling_in(0, k))
             each(4, exit_dots)
+            exchange(0)
 
     def finish(b):
-        @pl.when((b == 0) & (s < 2))
-        def _():
-            each(4, lambda k: sibling_in(0, k))
+        @pl.when(b == 0)
+        def _():
             each(4, exit_dots)
+            exchange(0)
 
         @pl.when(b == 1)
         def _():
-            dots_order()
+            for j in range(3):
+                dots(1, j)
+            opposite(1, 3)
+            dots(1, 3, True)
+
+            @pl.when(s >= 2)
+            def _():
+                softmax(0)
 
         softmax(b)
 
-    def dots_order():
-        b = 1
-        dots(b, c, 0)
-        each(3, lambda k: sibling_in(1, k))
-        for n in range(3):
-            y_fwd(b, 3, n, 1 - c).wait_recv()
-        dots(b, 1 - c, 0)
-        opposite(b, 3)
-        dots(b, c, 1)
-        dots(b, c, 2)
-        for n in (3, 4):
-            y_fwd(b, 3, n, 1 - c).wait_recv()
-        dots(b, 1 - c, 1)
-        dots(b, 1 - c, 2)
-        dots(b, c, 3)
-        for n in (5, 6):
-            y_fwd(b, 3, n, 1 - c).wait_recv()
-        dots(b, 1 - c, 3)
-
     def softmax(b):
-        squares = SQ[b].reshape(NY * ROWS, 128)
-        top = squares.astype(BF)
-        rest = (squares - top.astype(F32)).astype(BF)
-        ones = jnp.ones((16, 128), BF)
-        nt = (((1,), (1,)), ((), ()))
-        sums = (lax.dot_general(ones, top, nt, preferred_element_type=F32)
-                + lax.dot_general(ones, rest, nt, preferred_element_type=F32))[0:1]
+        swap_logits(b).wait_recv()
+        last = pl.ds(VOCAB_DEV, 8)
+        sums = (LT[b, 1, last] + LR[b, last])[0:1]
         r = lax.rsqrt(sums * (1.0 / D) + EPS)
-        logits = LT[b] * r
+        logits = (LT[b, 0, 0:VOCAB_DEV] + LR[b, 0:VOCAB_DEV]) * r
         highest = jnp.max(logits, axis=0, keepdims=True)
         summed = jnp.sum(jnp.exp(logits - highest), axis=0, keepdims=True)
-        vocab = HEAD.shape[2]
-        first = ((d * NX + s) * NM + m) * vocab
+        first = ((d * NX + s) * NM + m) * VOCAB_DEV
         index = (lax.broadcasted_iota(jnp.int32, logits.shape, 0) + first).astype(F32)
         wanted = WANT[0:1, :]
         picked = jnp.sum(jnp.where(index == wanted, logits, 0.0), axis=0, keepdims=True)
@@ -749,7 +730,7 @@
         def _():
             gather(jnp.where((t == 0) | (t == 1), 0, 1))
 
-        @pl.when((t == 4) | (t == jnp.where(s < 2, 2, 3)))
+        @pl.when((t == 4) | ((t == 2) & (s < 2)))
         def _():
             @pl.when((t == 2) & (s == 0))
             def _():
@@ -811,6 +792,9 @@
     for n in range(15):
         st_yx(n).start()
     layer_sent()
+    head_swap.wait_send()
+    swap_logits(0).wait_send()
+    swap_logits(1).wait_send()
     each(4, lambda k: chunk_sent(0, k, 1))
     each(4, lambda k: chunk_sent(1, k, NX - 1))
     for n in range(15):
@@ -898,8 +882,9 @@
             pltpu.VMEM((NY, NZ, ROWS, 256), BF),
             pltpu.VMEM((NY, NZ, ROWS, 256), BF),
             pltpu.VMEM((NY, ROWS, 256), BF),
-            pltpu.VMEM((2, 4, 2, 4, 4, ROWS, 256), BF),
-            pltpu.VMEM((2, vocab, 256), F32),
+            pltpu.VMEM((2, 4, 4, 4, ROWS, 256), BF),
+            pltpu.VMEM((2, 2, vocab + 8, 256), F32),
+            pltpu.VMEM((2, vocab + 8, 256), F32),
             pltpu.VMEM((2, NY, ROWS, 128), F32),
             pltpu.VMEM((8, 256), F32),
             pltpu.VMEM((2, 256, 32), BF),
@@ -907,7 +892,8 @@
             pltpu.VMEM((NX * NY, 16, 128), F32),
             pltpu.VMEM((NM, 16, 128), F32),
             dma((20,)),
-            dma((3,)), dma((3,)),
+            dma((4,)), dma((4,)),
+            dma((2,)), dma((2,)),
             dma, dma,
             dma((2, 8)), dma((2, 8)),
             dma((5,)), dma((5,)),

time: 150 us -> 147 us (0.980)
  Pallas kernels: 148 us -> 145 us
    pallas_call x1, Pallas kernels: 148 us -> 145 us  [per_device(): pl.pallas_call(kernel, out_shape=jax.ShapeDtypeStruct((2, 2, 32), F32), i...]
where the time goes in v17:
time: 147 us
  Pallas kernels  145 us (99%)
    pallas_call x1, Pallas kernels, per_device(): pl.pallas_call(kernel, out_shape=jax.ShapeDtypeStruct((2, 2, 32), F32), i...  145 us

profile of v17, /device:TPU:1, one launch (start us, length us, event | category | flops | bytes accessed | tf_op | source)
XLA Modules:
  0.0 147.2 jit_solution(7662439944365435385)
XLA Ops:
  0.6 145.4 %shard_map.140 = f32[2,2,32]{2,1,0:T(2,128)} custom-call(bf16[2,4,8192]{2,1,0:T(4,128)(2,1)} %emb_in.1, s32[8]{0:T(128)} %live.1, s32[8]{0:T(128)} %source_of.1, s32[8,32]{1,0:T(8,128)} %targets_in.1, f32[1,8192]{1,0:T(1,128)} %gain.1, f32[1,8192]{1,0:T(1,128)} %bitcast.13, f32[64,128]{1,0:T(8,128)} %constant.4.clone.cosine_in, ...), custom_call_target="tpu_custom_call" | custom-call | flops 8000000000 | bytes 24000000 | tf_op jit(solution)/shard_map/pallas_call | solution.py:854
  146.0 1.2 slice_bitcast_fusion

commit v18 on v17

--- a/solution.py
+++ b/solution.py
@@ -91,13 +91,10 @@
         return rcopy(src.at[:, 1 - c], W.at[1, :, :, lanes], sw_s.at[n], sw_r.at[n], here)
 
     wo_load = pltpu.make_async_copy(wo, WO, w_sem.at[12])
-    for n in range(3):
-        load(n, 0).start()
-
-    @pl.when(s == 0)
+    @pl.when(s > 0)
     def _():
         for n in range(3):
-            load(n, 1).start()
+            load(n, 0).start()
 
     head_load = pltpu.make_async_copy(HEAD.at[0], HEAD.at[0], w_sem.at[13])
     head_swap = rcopy(HEAD.at[1], HEAD.at[1], sw_s.at[3], sw_r.at[3], here)
@@ -124,8 +121,7 @@
             parts.append(jnp.sum(jnp.where(keep, every, 0.0), axis=0, keepdims=True))
         return parts[0] * 256.0 + parts[1]
 
-    def prepare():
-        wo_load.start()
+    def head_start():
         for j in range(4):
             for i in range(4):
                 there = pl.ds(i * 256, 256)
@@ -133,6 +129,12 @@
                                       w_sem.at[13]).start()
                 rcopy(head.at[:, slot_columns(1 - c, j, i)], HEAD.at[1, j, :, there],
                       sw_s.at[3], sw_r.at[3], here).start()
+    def prepare():
+        @pl.when(s > 0)
+        def _():
+            wo_load.start()
+            head_start()
+
         shape = (4 * ROWS, ROWS)
         rq = lax.broadcasted_iota(jnp.int32, shape, 0) % ROWS
         rk = lax.broadcasted_iota(jnp.int32, shape, 1)
@@ -726,6 +728,10 @@
         def _():
             layer()
 
+            @pl.when(s == 0)
+            def _():
+                head_start()
+
         @pl.when(jnp.where(last, (t == 0) | (t == 2), (t == 1) | (t == jnp.where(s < 2, 3, 2))))
         def _():
             gather(jnp.where((t == 0) | (t == 1), 0, 1))
@@ -743,6 +749,10 @@
         for q in range(2):
             for k in (2, 1, 3, 0):
                 (eb_z(q, k) if k else eb_fwd(q, 0)).start()
+        for n in range(3):
+            load(n, 0).start()
+            load(n, 1).start()
+        wo_load.start()
 
     prepare()
     STO[...] = jnp.zeros_like(STO)

time: 147 us -> 147 us (level)
  no operation moved by 1% of the time
where the time goes in v18:
time: 147 us
  Pallas kernels  145 us (99%)
    pallas_call x1, Pallas kernels, per_device(): pl.pallas_call(kernel, out_shape=jax.ShapeDtypeStruct((2, 2, 32), F32), i...  145 us

profile of v18, /device:TPU:1, one launch (start us, length us, event | category | flops | bytes accessed | tf_op | source)
XLA Modules:
  0.0 147.1 jit_solution(35962776058197896)
XLA Ops:
  0.6 145.2 %shard_map.140 = f32[2,2,32]{2,1,0:T(2,128)} custom-call(bf16[2,4,8192]{2,1,0:T(4,128)(2,1)} %emb_in.1, s32[8]{0:T(128)} %live.1, s32[8]{0:T(128)} %source_of.1, s32[8,32]{1,0:T(8,128)} %targets_in.1, f32[1,8192]{1,0:T(1,128)} %gain.1, f32[1,8192]{1,0:T(1,128)} %bitcast.13, f32[64,128]{1,0:T(8,128)} %constant.4.clone.cosine_in, ...), custom_call_target="tpu_custom_call" | custom-call | flops 8000000000 | bytes 24000000 | tf_op jit(solution)/shard_map/pallas_call | solution.py:864
  145.8 1.2 slice_bitcast_fusion

commit v19 on v18

--- a/solution.py
+++ b/solution.py
@@ -67,6 +67,8 @@
         partners.append((ypeer(k), (s + 1) % NX, m))
         partners.append((ypeer(k), (s + 3) % NX, m))
         partners.append((ypeer(k), (s + 2) % NX, m))
+    for k in (1, 3):
+        partners.append((d, (s + k) % NX, zpeer(2)))
     partners.append(here)
     for dev in partners:
         pl.semaphore_signal(barrier, inc=1, device_id=dev, device_id_type=MESH)
@@ -196,7 +198,9 @@
 
     small[0].wait()
 
-    @pl.when(s == 0)
+    far_sender = s == jnp.where(c == 0, 1, 3)
+
+    @pl.when((s == 0) | far_sender)
     def _():
         rows = jnp.concatenate([emb[0], emb[1]], axis=0).astype(F32)
         for q in range(2):
@@ -212,7 +216,7 @@
             swap(n).start()
 
     def eb_z(q, k):
-        return rcopy(EB.at[q, m], EB.at[q, m], eb_s.at[q, k], eb_r.at[q, m], (d, s, zpeer(k)))
+        return rcopy(EB.at[q, m], EB.at[q, m], eb_s.at[q, k], eb_r.at[q, m], (d, 0, zpeer(k)))
 
     def eb_z_in(q, k):
         mk = zpeer(k)
@@ -589,10 +593,15 @@
         swap_logits(b).start()
 
     def layer_sent():
+        @pl.when(far_sender)
+        def _():
+            for q in range(2):
+                eb_z(q, 2).wait_send()
+
         @pl.when(s == 0)
         def _():
             for q in range(2):
-                for k in range(1, 4):
+                for k in (1, 3):
                     eb_z(q, k).wait_send()
                 for k in range(4):
                     eb_fwd(q, k).wait_send()
@@ -744,10 +753,15 @@
             finish(jnp.where(t == 4, 1, 0))
         return 0
 
+    @pl.when(far_sender)
+    def _():
+        for q in range(2):
+            eb_z(q, 2).start()
+
     @pl.when(s == 0)
     def _():
         for q in range(2):
-            for k in (2, 1, 3, 0):
+            for k in (1, 3, 0):
                 (eb_z(q, k) if k else eb_fwd(q, 0)).start()
         for n in range(3):
             load(n, 0).start()

time: 147 us -> 148 us (level)
  no operation moved by 1% of the time
where the time goes in v19:
time: 148 us
  Pallas kernels  146 us (99%)
    pallas_call x1, Pallas kernels, per_device(): pl.pallas_call(kernel, out_shape=jax.ShapeDtypeStruct((2, 2, 32), F32), i...  146 us

profile of v19, /device:TPU:1, one launch (start us, length us, event | category | flops | bytes accessed | tf_op | source)
XLA Modules:
  0.0 148.2 jit_solution(6581253702288036106)
XLA Ops:
  0.6 146.4 %shard_map.140 = f32[2,2,32]{2,1,0:T(2,128)} custom-call(bf16[2,4,8192]{2,1,0:T(4,128)(2,1)} %emb_in.1, s32[8]{0:T(128)} %live.1, s32[8]{0:T(128)} %source_of.1, s32[8,32]{1,0:T(8,128)} %targets_in.1, f32[1,8192]{1,0:T(1,128)} %gain.1, f32[1,8192]{1,0:T(1,128)} %bitcast.13, f32[64,128]{1,0:T(8,128)} %constant.4.clone.cosine_in, ...), custom_call_target="tpu_custom_call" | custom-call | flops 8000000000 | bytes 24000000 | tf_op jit(solution)/shard_map/pallas_call | solution.py:878
  147.0 1.2 slice_bitcast_fusion

commit v20 on v18

--- a/solution.py
+++ b/solution.py
@@ -664,30 +664,20 @@
             def _():
                 stage_second(b, t - 2)
 
-            @pl.when((t >= 3) & ((b == 0) | (t < 6)) & others)
-            def _():
-                opposite(b, t - 3)
-
-            @pl.when((b == 1) & (s == 2) & (t >= 2) & (t < 6))
-            def _():
-                exit_dots(t - 2)
-
-            @pl.when((b == 1) & (s == 2) & (t == 6))
-            def _():
-                exchange(0)
             return 0
 
-        lax.fori_loop(0, 7, body, 0)
-
-        @pl.when(final)
-        def _():
-            each(3, lambda k: opposite(1, k))
+        lax.fori_loop(0, 6, body, 0)
+
+        @pl.when((b == 1) & (s >= 2))
+        def _():
+            each(4, lambda k: opposite(0, k))
             each(4, exit_dots)
             exchange(0)
 
     def finish(b):
         @pl.when(b == 0)
         def _():
+            each(4, lambda k: opposite(0, k))
             each(4, exit_dots)
             exchange(0)
 
@@ -695,7 +685,7 @@
         def _():
             for j in range(3):
                 dots(1, j)
-            opposite(1, 3)
+            each(4, lambda k: opposite(1, k))
             dots(1, 3, True)
 
             @pl.when(s >= 2)

time: 147 us -> 148 us (level)
  no operation moved by 1% of the time
where the time goes in v20:
time: 148 us
  Pallas kernels  146 us (99%)
    pallas_call x1, Pallas kernels, per_device(): pl.pallas_call(kernel, out_shape=jax.ShapeDtypeStruct((2, 2, 32), F32), i...  146 us

profile of v20, /device:TPU:1, one launch (start us, length us, event | category | flops | bytes accessed | tf_op | source)
XLA Modules:
  0.0 147.8 jit_solution(10584033709470377620)
XLA Ops:
  0.6 145.9 %shard_map.140 = f32[2,2,32]{2,1,0:T(2,128)} custom-call(bf16[2,4,8192]{2,1,0:T(4,128)(2,1)} %emb_in.1, s32[8]{0:T(128)} %live.1, s32[8]{0:T(128)} %source_of.1, s32[8,32]{1,0:T(8,128)} %targets_in.1, f32[1,8192]{1,0:T(1,128)} %gain.1, f32[1,8192]{1,0:T(1,128)} %bitcast.13, f32[64,128]{1,0:T(8,128)} %constant.4.clone.cosine_in, ...), custom_call_target="tpu_custom_call" | custom-call | flops 8000000000 | bytes 24000000 | tf_op jit(solution)/shard_map/pallas_call | solution.py:854
  146.5 1.2 slice_bitcast_fusion

commit v21 on v18

--- a/solution.py
+++ b/solution.py
@@ -664,7 +664,9 @@
             def _():
                 stage_second(b, t - 2)
 
-            @pl.when((t >= 3) & ((b == 0) | (t < 6)) & others)
+            last = (b == 0) & (s == NX - 1)
+
+            @pl.when((t >= 3) & ((b == 0) | (t < 6)) & others & jnp.logical_not(last))
             def _():
                 opposite(b, t - 3)
 
@@ -682,6 +684,7 @@
         @pl.when(final)
         def _():
             each(3, lambda k: opposite(1, k))
+            each(4, lambda k: opposite(0, k))
             each(4, exit_dots)
             exchange(0)
 

time: 147 us -> 147 us (level)
  no operation moved by 1% of the time
where the time goes in v21:
time: 147 us
  Pallas kernels  145 us (99%)
    pallas_call x1, Pallas kernels, per_device(): pl.pallas_call(kernel, out_shape=jax.ShapeDtypeStruct((2, 2, 32), F32), i...  145 us

profile of v21, /device:TPU:1, one launch (start us, length us, event | category | flops | bytes accessed | tf_op | source)
XLA Modules:
  0.0 147.1 jit_solution(9304489161119529800)
XLA Ops:
  0.6 145.2 %shard_map.140 = f32[2,2,32]{2,1,0:T(2,128)} custom-call(bf16[2,4,8192]{2,1,0:T(4,128)(2,1)} %emb_in.1, s32[8]{0:T(128)} %live.1, s32[8]{0:T(128)} %source_of.1, s32[8,32]{1,0:T(8,128)} %targets_in.1, f32[1,8192]{1,0:T(1,128)} %gain.1, f32[1,8192]{1,0:T(1,128)} %bitcast.13, f32[64,128]{1,0:T(8,128)} %constant.4.clone.cosine_in, ...), custom_call_target="tpu_custom_call" | custom-call | flops 8000000000 | bytes 24000000 | tf_op jit(solution)/shard_map/pallas_call | solution.py:867
  145.8 1.2 slice_bitcast_fusion
